TPU v7x, 256 devices: a whole 4x4x8 slice. The times are simulated.
256 devices in a mesh: ctx: 16 (over z, core), head: 16 (over x, y).
Axes of the slice: x: 4, y: 4, z: 8, core: 2. Of those that a mesh axis runs over, the one named last changes fastest.
Arguments:
- queries: bfloat16 [16384, 2048], P(('ctx', 'head')), may hold values from -6 to 6
- keys: bfloat16 [16384, 2048], P(('ctx', 'head')), may hold values from -3 to 3
- values: bfloat16 [16384, 4096], P(('ctx', 'head')), may hold values from -6 to 6
- out_grad: bfloat16 [16384, 4096], P(('ctx', 'head')), may hold values from -6 to 6
- log_gates: bfloat16 [16384, 2048], P(('ctx', 'head')), may hold values from -1 to 0, as said below
- live_blocks: int32 [16], P('ctx'), may hold values from 1 to 16, 160 in all
- block_doc: int32 [256], P('ctx'), may hold values from 0 to 3, never falling along the last dimension, each value on 1 to 128 neighbouring positions
Outputs:
- query_grad: bfloat16 [16384, 2048], P(('ctx', 'head'))
- key_grad: bfloat16 [16384, 2048], P(('ctx', 'head'))
- value_grad: bfloat16 [16384, 4096], P(('ctx', 'head'))
- gate_grad: bfloat16 [16384, 2048], P(('ctx', 'head'))
Inputs may be any that keep to these rules, and one draw needn't show every extreme that they name: `live_blocks`: live blocks of each context owner's 16 blocks; an owner's live blocks come first in its part of the sequence and its padding blocks after; together they number 16 * 16 * 5 // 8, and some owner has all of its blocks live. `block_doc`: ids never fall along the sequence and start at 0; each of the 4 documents covers 1 to 128 blocks, one exactly 128. `log_gates`: never positive.
All inputs are finite; a program needn't handle non-finite values.
Results may differ from a plain program's by a relative error of at most 0.001.
Values may be sent and summed in bfloat16 or wider, within the bound.
No kernel may reach another device: no remote copies, remote signals or barrier semaphores. Data moves between devices by JAX's collectives and lax.ppermute only.
A program may use at most 64 MiB of HBM per device.

v0:
```python
import jax
import jax.numpy as jnp
from jax import lax
from jax.sharding import PartitionSpec as P

DK = 128
DV = 256
BLOCK = 64


FINEST_ARITHMETIC = lax.Precision.HIGHEST


def shifted(shard, axis, by):
    peers = lax.axis_size(axis)
    pairs = [(i, i + by) for i in range(peers) if 0 <= i + by < peers]
    return lax.ppermute(shard, axis, pairs)


def prefix(shard, axis, combine, identity, reverse):
    peers, index = (lax.axis_size(axis), lax.axis_index(axis))
    everything = jax.tree.map(lambda part: lax.all_gather(part, axis), shard)
    start = jax.tree.map(
        lambda part, zero: jnp.broadcast_to(jnp.asarray(zero, part.dtype), part.shape),
        shard,
        identity,
    )

    def step(k, before):
        at = peers - 1 - k if reverse else k
        reached = at > index if reverse else at < index
        new = combine(before, jax.tree.map(lambda part: part[at], everything))
        return jax.tree.map(lambda a, b: jnp.where(reached, a, b), new, before)

    return lax.fori_loop(0, peers, step, start)


def compose(former, latter):
    return (former[0] * latter[0], latter[0][..., None] * former[1] + latter[1])


def advance(carried, inputs):
    decay_now, update_now = inputs
    return ((decay_now * carried[0], decay_now[..., None] * carried[1] + update_now), carried)


def block_flags(live_blocks, block_doc):
    block_count = block_doc.shape[0]
    position = jnp.arange(block_count)
    live_flag = (position < live_blocks[0]).astype(jnp.float32)
    shifted_doc = block_doc + 1
    earlier_doc = shifted(shifted_doc[block_count - 1 :], "ctx", 1)
    previous = jnp.concatenate([earlier_doc, shifted_doc[:-1]])
    opening = (position == 0) & (lax.axis_index("ctx") == 0)
    keep_flag = jnp.where((previous == shifted_doc) & jnp.logical_not(opening), 1.0, 0.0).astype(
        jnp.float32
    )
    return (live_flag, keep_flag)


def local_terms(
    query_rows, key_rows, payload_array, grad_rows, forgetting_entries, live_flag, keep_flag
):
    block_count = query_rows.shape[0] // BLOCK
    head_count = query_rows.shape[1] // DK

    def shaped(matrix, span_width):
        return matrix.reshape(block_count, BLOCK, head_count, span_width).astype(jnp.float32)

    active_tensor_mask = live_flag[:, None, None, None]
    log_cumul = jnp.cumsum(shaped(forgetting_entries, DK) * active_tensor_mask, axis=1)
    final_log = log_cumul[:, -1]
    masked_key = shaped(key_rows, DK) * active_tensor_mask
    grad_out = shaped(grad_rows, DV) * active_tensor_mask
    value_block = shaped(payload_array, DV)
    query_scaled = DK ** (-0.5) * shaped(query_rows, DK) * jnp.exp(log_cumul)
    rising_key = masked_key * jnp.exp(-log_cumul)
    faded_lookup_vector = masked_key * jnp.exp(final_log[:, None] - log_cumul)
    decays = keep_flag[:, None, None] * jnp.exp(final_log)
    memory_increment = jnp.einsum(
        "nchk,nchv->nhkv", faded_lookup_vector, value_block, precision=FINEST_ARITHMETIC
    )
    reverse_update = keep_flag[:, None, None, None] * jnp.einsum(
        "nchk,nchv->nhkv", query_scaled, grad_out, precision=FINEST_ARITHMETIC
    )
    initial = (
        jnp.ones((head_count, DK), jnp.float32),
        jnp.zeros((head_count, DK, DV), jnp.float32),
    )
    forward_total, forward_parts = lax.scan(advance, initial, (decays, memory_increment))
    backward_total, backward_parts = lax.scan(
        advance, initial, (decays, reverse_update), reverse=True
    )
    prepared = (
        log_cumul,
        final_log,
        query_scaled,
        rising_key,
        faded_lookup_vector,
        grad_out,
        value_block,
        active_tensor_mask,
        keep_flag,
        forward_parts,
        backward_parts,
    )
    return (prepared, forward_total, backward_total)


def finish(prepared, incoming, from_right):
    (
        log_cumul,
        final_log,
        query_scaled,
        rising_key,
        faded_lookup_vector,
        grad_out,
        value_block,
        active_tensor_mask,
        keep_flag,
        forward_parts,
        backward_parts,
    ) = prepared
    incoming_state = keep_flag[:, None, None, None] * (
        forward_parts[0][..., None] * incoming[None] + forward_parts[1]
    )
    grad_state = backward_parts[0][..., None] * from_right[None] + backward_parts[1]
    causal = jnp.tril(jnp.ones((BLOCK, BLOCK), jnp.float32))
    scores = (
        jnp.einsum("nihk,njhk->nhij", query_scaled, rising_key, precision=FINEST_ARITHMETIC)
        * causal
    )
    score_grad = (
        jnp.einsum("nihv,njhv->nhij", grad_out, value_block, precision=FINEST_ARITHMETIC) * causal
    )
    query_part = jnp.einsum(
        "nihv,nhkv->nihk", grad_out, incoming_state, precision=FINEST_ARITHMETIC
    ) + jnp.einsum("nhij,njhk->nihk", score_grad, rising_key, precision=FINEST_ARITHMETIC)
    rising_part = jnp.einsum(
        "nhij,nihk->njhk", score_grad, query_scaled, precision=FINEST_ARITHMETIC
    )
    value_grad = jnp.einsum(
        "nhij,nihv->njhv", scores, grad_out, precision=FINEST_ARITHMETIC
    ) + jnp.einsum("njhk,nhkv->njhv", faded_lookup_vector, grad_state, precision=FINEST_ARITHMETIC)
    falling_part = jnp.einsum(
        "njhv,nhkv->njhk", value_block, grad_state, precision=FINEST_ARITHMETIC
    )
    final_grad = jnp.sum(falling_part * faded_lookup_vector, axis=1) + jnp.sum(
        grad_state * incoming_state, axis=-1
    ) * jnp.exp(final_log)
    cumul_grad = (
        query_part * query_scaled - rising_part * rising_key - falling_part * faded_lookup_vector
    )
    cumul_grad = cumul_grad.at[:, -1].add(final_grad)
    gate_grad = jnp.cumsum(cumul_grad[:, ::-1], axis=1)[:, ::-1] * active_tensor_mask
    query_grad = query_part * DK ** (-0.5) * jnp.exp(log_cumul)
    key_grad = (
        rising_part * jnp.exp(-log_cumul) + falling_part * jnp.exp(final_log[:, None] - log_cumul)
    ) * active_tensor_mask
    row_count = query_grad.shape[0] * BLOCK

    def flatten_rows(matrix):
        return matrix.reshape(row_count, -1).astype(jnp.bfloat16)

    return (
        flatten_rows(query_grad),
        flatten_rows(key_grad),
        flatten_rows(value_grad),
        flatten_rows(gate_grad),
    )


def per_device(queries, keys, values, out_grad, log_gates, live_blocks, block_doc):
    live_flag, keep_flag = block_flags(live_blocks, block_doc)
    arrived = (
        lax.all_to_all(queries, "head", split_axis=1, concat_axis=0, tiled=True),
        lax.all_to_all(keys, "head", split_axis=1, concat_axis=0, tiled=True),
        lax.all_to_all(values, "head", split_axis=1, concat_axis=0, tiled=True),
        lax.all_to_all(out_grad, "head", split_axis=1, concat_axis=0, tiled=True),
        lax.all_to_all(log_gates, "head", split_axis=1, concat_axis=0, tiled=True),
    )
    prepared, forward_total, backward_total = local_terms(
        arrived[0], arrived[1], arrived[2], arrived[3], arrived[4], live_flag, keep_flag
    )
    identity = (jnp.ones_like(forward_total[0]), jnp.zeros_like(forward_total[1]))
    incoming = prefix(forward_total, "ctx", compose, identity, False)[1]
    from_right = prefix(backward_total, "ctx", compose, identity, True)[1]
    results = finish(prepared, incoming, from_right)
    return (
        lax.all_to_all(results[0], "head", split_axis=0, concat_axis=1, tiled=True),
        lax.all_to_all(results[1], "head", split_axis=0, concat_axis=1, tiled=True),
        lax.all_to_all(results[2], "head", split_axis=0, concat_axis=1, tiled=True),
        lax.all_to_all(results[3], "head", split_axis=0, concat_axis=1, tiled=True),
    )


def solution(mesh):
    in_specs = (
        P(("ctx", "head"), None),
        P(("ctx", "head"), None),
        P(("ctx", "head"), None),
        P(("ctx", "head"), None),
        P(("ctx", "head"), None),
        P("ctx"),
        P("ctx"),
    )
    out_specs = (
        P(("ctx", "head"), None),
        P(("ctx", "head"), None),
        P(("ctx", "head"), None),
        P(("ctx", "head"), None),
    )
    return jax.shard_map(
        per_device, mesh=mesh, in_specs=in_specs, out_specs=out_specs, check_vma=False
    )
```

profile of v0, /device:TPU:32, one launch (start us, length us, event | category | flops | bytes accessed | tf_op | source)
XLA Modules:
  0.0 346.2 jit_solution(4964960924156985843)
XLA Ops:
  8.9 7.2 %all-to-all-start = ((bf16[64,16,128]{2,0,1:T(8,128)(2,1)}), bf16[64,16,128]{2,0,1:T(8,128)(2,1)S(1)}, u32[]{:S(2)}, u32[]{:S(2)}) async-start(bf16[64,16,128]{2,0,1:T(8,128)(2,1)} %copy_bitcast_fusion.7), calls=%async_computation | async-start | bytes 524288 | tf_op jit(solution)/shard_map/all_to_all | solution.py:180
  17.3 1.9 collective-permute-start
  19.9 1.7 copy_bitcast_fusion.6
  21.7 1.9 copy.126
  25.2 7.2 %all-to-all-start.1 = ((bf16[64,16,128]{2,0,1:T(8,128)(2,1)}), bf16[64,16,128]{2,0,1:T(8,128)(2,1)S(1)}, u32[]{:S(2)}, u32[]{:S(2)}) async-start(bf16[64,16,128]{2,0,1:T(8,128)(2,1)} %copy_bitcast_fusion.6), calls=%async_computation.1 | async-start | bytes 524288 | tf_op jit(solution)/shard_map/all_to_all | solution.py:177
  33.3 8.0 %all-to-all-done.1 = bf16[64,16,128]{2,0,1:T(8,128)(2,1)S(1)} async-done(((bf16[64,16,128]{2,0,1:T(8,128)(2,1)}), bf16[64,16,128]{2,0,1:T(8,128)(2,1)S(1)}, u32[]{:S(2)}, u32[]{:S(2)}) %all-to-all-start.1) | async-done | bytes 262176 | tf_op jit(solution)/shard_map/all_to_all | solution.py:177
  41.3 4.2 %all-to-all-start.5 = ((bf16[64,16,128]{2,0,1:T(8,128)(2,1)}), bf16[64,16,128]{2,0,1:T(8,128)(2,1)S(1)}, u32[]{:S(2)}, u32[]{:S(2)}) async-start(bf16[64,16,128]{2,0,1:T(8,128)(2,1)} %copy_bitcast_fusion.5), calls=%async_computation.5 | async-start | bytes 524288 | tf_op jit(solution)/shard_map/all_to_all | solution.py:176
  46.0 8.6 %all-to-all-done.5 = bf16[64,16,128]{2,0,1:T(8,128)(2,1)S(1)} async-done(((bf16[64,16,128]{2,0,1:T(8,128)(2,1)}), bf16[64,16,128]{2,0,1:T(8,128)(2,1)S(1)}, u32[]{:S(2)}, u32[]{:S(2)}) %all-to-all-start.5) | async-done | bytes 262176 | tf_op jit(solution)/shard_map/all_to_all | solution.py:176
  54.6 3.7 %all-to-all-start.2 = ((bf16[64,16,256]{2,0,1:T(8,128)(2,1)}), bf16[64,16,256]{2,0,1:T(8,128)(2,1)S(1)}, u32[]{:S(2)}, u32[]{:S(2)}) async-start(bf16[64,16,256]{2,0,1:T(8,128)(2,1)} %bitcast.240), calls=%async_computation.2 | async-start | bytes 1048576 | tf_op jit(solution)/shard_map/all_to_all | solution.py:178
  58.4 2.1 convolution_multiply_fusion.1
  60.5 8.9 %all-to-all-done.2 = bf16[64,16,256]{2,0,1:T(8,128)(2,1)S(1)} async-done(((bf16[64,16,256]{2,0,1:T(8,128)(2,1)}), bf16[64,16,256]{2,0,1:T(8,128)(2,1)S(1)}, u32[]{:S(2)}, u32[]{:S(2)}) %all-to-all-start.2) | async-done | bytes 524320 | tf_op jit(solution)/shard_map/all_to_all | solution.py:178
  69.3 3.6 %all-to-all-start.3 = ((bf16[64,16,256]{2,0,1:T(8,128)(2,1)}), bf16[64,16,256]{2,0,1:T(8,128)(2,1)S(1)}, u32[]{:S(2)}, u32[]{:S(2)}) async-start(bf16[64,16,256]{2,0,1:T(8,128)(2,1)} %bitcast.239), calls=%async_computation.3 | async-start | bytes 1048576 | tf_op jit(solution)/shard_map/all_to_all | solution.py:179
  73.0 2.5 convolution_bitcast_fusion
  75.5 1.6 broadcast.136.clone.1
  77.1 27.6 %while.69 = (s32[]{:T(128)}, f32[1,128]{1,0:T(1,128)S(1)}, f32[1,128,256]{2,1,0:T(8,128)S(1)}, f32[16,1,128]{2,1,0:T(1,128)S(1)}, f32[16,1,128,256]{3,2,1,0:T(8,...) while((s32[]{:T(128)}, f32[1,128]{1,0:T(1,128)S(1)}, ...), condition=%wide.region_2.3_spmd.clone, body=%wide.region_1.2_spmd.clone.sunk | while | flops 131459 | bytes 660090 | solution.py:90
  106.3 3.6 %multiply_bitcast_fusion = f32[16,1,128,256]{3,2,1,0:T(8,128)} fusion(f32[16]{0:T(128)S(1)} %and_select_fusion, bf16[64,16,256]{2,0,1:T(8,128)(2,1)S(1)} %all-to-all-done.3, f32[16]{0:T(128)S(1)} %compare_convert_fusion, bf16[64,16,128]{2,0,1:T(8,128)(2,1)S(1)} %all-to-all-done.5, f32[16,64,1,128]{3,0,1,2:T(8,128)S(1)} %fusion.51), kind=kOutput, calls=%fused_computation.28 | convolution fusion | flops 404094976 | bytes 3408000 | tf_op jit(solution)/shard_map/nchk,nchv->nhkv/dot_general | solution.py:83
  110.1 54.8 %while.71 = (s32[]{:T(128)}, f32[1,128]{1,0:T(1,128)}, f32[1,128,256]{2,1,0:T(8,128)S(1)}, f32[16,1,128]{2,1,0:T(1,128)S(1)}, f32[16,1,128,256]{3,2,1,0:T(8,128)...) while((s32[]{:T(128)}, f32[1,128]{1,0:T(1,128)}, ...), condition=%wide.region_6.7_spmd.clone, body=%wide.region_5.6_spmd.clone.sunk | while | flops 131460 | bytes 659602 | solution.py:91
  111.8 1.2 bitcast_multiply_fusion.12
  118.8 1.2 bitcast_multiply_fusion.12
  122.2 1.2 bitcast_multiply_fusion.12
  164.9 17.4 %all-gather.4 = f32[16,1,128]{2,1,0:T(1,128)} all-gather(f32[1,1,128]{2,1,0:T(1,128)} %bitcast.289), channel_id=2, replica_groups=mesh['ctx'=16,'head'=16] {'ctx'}, dimensions={0}, use_global_device_ids=true | all-gather | bytes 8704 | tf_op jit(solution)/shard_map/all_gather | solution.py:22
  182.4 17.1 %all-gather.5 = f32[16,1,128]{2,1,0:T(1,128)} all-gather(f32[1,1,128]{2,1,0:T(1,128)} %bitcast.288), channel_id=4, replica_groups=mesh['ctx'=16,'head'=16] {'ctx'}, dimensions={0}, use_global_device_ids=true | all-gather | bytes 8704 | tf_op jit(solution)/shard_map/all_gather | solution.py:22
  199.5 2.0 convolution_multiply_fusion
  201.5 2.2 fusion.63
  203.7 2.0 convolution_bitcast_fusion.1
  205.7 26.4 %while.70 = (s32[]{:T(128)}, f32[1,128,256]{2,1,0:T(8,128)S(1)}, s32[]{:T(128)}, f32[16,1,128]{2,1,0:T(1,128)}, f32[16,1,128,256]{3,2,1,0:T(8,128)}, /*index=5*/s32[]{:T(128)}, s32[]{:T(128)}) while((s32[]{:T(128)}, f32[1,128,256]{2,1,0:T(8,128)S(1)}, s32[]{:T(128)}, f32[16,1,128]{2,1,0:T(1,128)}, f32[16,1,128,256]{3,2,1,0:T(8,128)}, ...), condition=%wide.region_4.5_spmd.clone, body=%wide.region_3.4_spmd.clone.sunk | while | flops 131076 | bytes 394857 | solution.py:35
  232.1 6.0 %all-gather.11.cloned.1.call-done = f32[16,128,256]{2,1,0:T(8,128)} async-done(((f32[1,128,256]{2,1,0:T(8,128)}), f32[16,128,256]{2,1,0:T(8,128)}) %all-gather.11.cloned.1.call-update) | async-done | bytes 2097168 | tf_op jit(solution)/shard_map/all_gather | solution.py:22
  238.1 26.6 %while.72 = (s32[]{:T(128)}, f32[1,128,256]{2,1,0:T(8,128)S(1)}, s32[]{:T(128)}, f32[16,1,128]{2,1,0:T(1,128)}, f32[16,1,128,256]{3,2,1,0:T(8,128)}, /*index=5*/s32[]{:T(128)}, s32[]{:T(128)}, s32[]{:T(128)}, s32[]{:T(128)}) while((s32[]{:T(128)}, f32[1,128,256]{2,1,0:T(8,128)S(1)}, s32[]{:T(128)}, f32[16,1,128]{2,1,0:T(1,128)}, ...), condition=%wide.region_8.9_spmd.clone, body=%wide.region_7.8_spmd.clone.sunk | while | flops 131080 | bytes 394919 | solution.py:35
  264.8 2.4 multiply_reduce_fusion
  267.3 1.6 fusion.25
  269.1 4.0 %fusion.41 = (f32[16,64,1,128]{3,1,0,2:T(8,128)S(1)}, bf16[16,64,128]{2,1,0:T(8,128)(2,1)}, f32[16,128]{1,0:T(8,128)S(1)}, bf16[16,64,128]{2,1,0:T(8,128)(2,1)}) fusion(f32[16,64,1,128]{3,1,0,2:T(8,128)S(1)} %copy-done.17, f32[16,64,1,128]{3,1,0,2:T(8,128)S(1)} %fusion.25, bf16[64,16,128]{2,0,1:T(8,128)(2,1)S(1)} %copy-done.14, f32[16]{0:T(128)S(1)} %copy-done.24, ...), kind=kOutput, calls=%fused_computation.58 | convolution fusion | flops 408156160 | bytes 6447232 | tf_op jit(solution)/shard_map/nihv,nhkv->nihk/dot_general | solution.py:136
  273.8 1.5 slice_add_fusion
  275.3 1.5 scatter-add.4
  276.8 1.9 rev.6
  278.7 1.4 fusion.49
  281.0 1.9 rev.7
  282.8 1.9 fusion.59
  284.7 6.8 %all-to-all-start.8 = ((bf16[16,64,128]{2,1,0:T(8,128)(2,1)}), bf16[16,64,128]{2,1,0:T(8,128)(2,1)}, u32[]{:S(2)}, u32[]{:S(2)}) async-start(bf16[16,64,128]{2,1,0:T(8,128)(2,1)} %fusion.59), calls=%async_computation.8 | async-start | bytes 524288 | tf_op jit(solution)/shard_map/all_to_all | solution.py:193
  291.5 3.2 fusion.28
  294.8 5.7 %all-to-all-done.8 = bf16[16,64,128]{2,1,0:T(8,128)(2,1)} async-done(((bf16[16,64,128]{2,1,0:T(8,128)(2,1)}), bf16[16,64,128]{2,1,0:T(8,128)(2,1)}, u32[]{:S(2)}, u32[]{:S(2)}) %all-to-all-start.8) | async-done | bytes 262176 | tf_op jit(solution)/shard_map/all_to_all | solution.py:193
  300.5 3.6 %all-to-all-start.6 = ((bf16[16,64,128]{2,1,0:T(8,128)(2,1)}), bf16[16,64,128]{2,1,0:T(8,128)(2,1)S(1)}, u32[]{:S(2)}, u32[]{:S(2)}) async-start(bf16[16,64,128]{2,1,0:T(8,128)(2,1)} %get-tuple-element.621), calls=%async_computation.6 | async-start | bytes 524288 | tf_op jit(solution)/shard_map/all_to_all | solution.py:191
  304.1 3.8 %fusion.22 = bf16[16,64,256]{2,1,0:T(8,128)(2,1)} fusion(f32[16,256,64]{1,2,0:T(8,128)} %fusion.28, f32[16,1,128,256]{3,2,1,0:T(8,128)S(1)} %get-tuple-element.435, f32[128,256]{1,0:T(8,128)S(1)} %bitcast.273, f32[16,128]{1,0:T(8,128)S(1)} %bitcast.284, bf16[64,16,128]{2,0,1:T(8,128)(2,1)} %copy-done.8, f32[16,128]{1,0:T(8,128)S(1)} %bitcast.287, ...), kind=kOutput, calls=%fused_computation.36 | convolution fusion | flops 404750336 | bytes 4603968 | tf_op jit(solution)/shard_map/njhk,nhkv->njhv/dot_general | solution.py:144
  307.9 4.7 %all-to-all-done.6 = bf16[16,64,128]{2,1,0:T(8,128)(2,1)S(1)} async-done(((bf16[16,64,128]{2,1,0:T(8,128)(2,1)}), bf16[16,64,128]{2,1,0:T(8,128)(2,1)S(1)}, u32[]{:S(2)}, u32[]{:S(2)}) %all-to-all-start.6) | async-done | bytes 262176 | tf_op jit(solution)/shard_map/all_to_all | solution.py:191
  312.6 3.7 %all-to-all-start.4 = ((bf16[16,64,128]{2,1,0:T(8,128)(2,1)}), bf16[16,64,128]{2,1,0:T(8,128)(2,1)S(1)}, u32[]{:S(2)}, u32[]{:S(2)}) async-start(bf16[16,64,128]{2,1,0:T(8,128)(2,1)} %get-tuple-element.623), calls=%async_computation.4 | async-start | bytes 524288 | tf_op jit(solution)/shard_map/all_to_all | solution.py:190
  316.2 1.7 copy_bitcast_fusion.2
  317.9 6.8 %all-to-all-done.4 = bf16[16,64,128]{2,1,0:T(8,128)(2,1)S(1)} async-done(((bf16[16,64,128]{2,1,0:T(8,128)(2,1)}), bf16[16,64,128]{2,1,0:T(8,128)(2,1)S(1)}, u32[]{:S(2)}, u32[]{:S(2)}) %all-to-all-start.4) | async-done | bytes 262176 | tf_op jit(solution)/shard_map/all_to_all | solution.py:190
  324.7 3.7 %all-to-all-start.7 = ((bf16[16,64,256]{2,1,0:T(8,128)(2,1)}), bf16[16,64,256]{2,1,0:T(8,128)(2,1)S(1)}, u32[]{:S(2)}, u32[]{:S(2)}) async-start(bf16[16,64,256]{2,1,0:T(8,128)(2,1)} %fusion.22), calls=%async_computation.7 | async-start | bytes 1048576 | tf_op jit(solution)/shard_map/all_to_all | solution.py:192
  329.9 8.6 %all-to-all-done.7 = bf16[16,64,256]{2,1,0:T(8,128)(2,1)S(1)} async-done(((bf16[16,64,256]{2,1,0:T(8,128)(2,1)}), bf16[16,64,256]{2,1,0:T(8,128)(2,1)S(1)}, u32[]{:S(2)}, u32[]{:S(2)}) %all-to-all-start.7) | async-done | bytes 524320 | tf_op jit(solution)/shard_map/all_to_all | solution.py:192
  (321 shorter events, 142.4 us)
Async XLA Ops:
  7.2 1.0 copy-start
  7.2 16.4 %copy-start.18 = (bf16[64,4096]{1,0:T(8,128)(2,1)S(1)}, bf16[64,4096]{1,0:T(8,128)(2,1)}, u32[]{:S(2)}) copy-start(bf16[64,4096]{1,0:T(8,128)(2,1)} %param.20) | copy-start | bytes 1572868
  8.1 16.3 %copy-start.21 = (bf16[64,2048]{1,0:T(8,128)(2,1)S(1)}, bf16[64,2048]{1,0:T(8,128)(2,1)}, u32[]{:S(2)}) copy-start(bf16[64,2048]{1,0:T(8,128)(2,1)} %param.17) | copy-start | bytes 786436
  8.9 23.6 %copy-start.32 = (s32[16]{0:T(128)S(1)}, s32[16]{0:T(128)}, u32[]{:S(2)}) copy-start(s32[16]{0:T(128)} %param.23) | copy-start | bytes 196
  8.9 16.3 %all-to-all-start = ((bf16[64,16,128]{2,0,1:T(8,128)(2,1)}), bf16[64,16,128]{2,0,1:T(8,128)(2,1)S(1)}, u32[]{:S(2)}, u32[]{:S(2)}) async-start(bf16[64,16,128]{2,0,1:T(8,128)(2,1)} %copy_bitcast_fusion.7), calls=%async_computation | async-start | bytes 524288 | tf_op jit(solution)/shard_map/all_to_all | solution.py:180
  17.3 15.1 %collective-permute-start = (s32[1]{0:T(128)}, s32[1]{0:T(128)}, u32[]{:S(2)}, u32[]{:S(2)}) collective-permute-start(s32[1]{0:T(128)} %slice.36), channel_id=1, source_target_pairs={{0,16},{16,32},{32,48},{48,64},{64,80},{80,96},{96,112},{112,128},... | collective-permute-start | bytes 20 | tf_op jit(solution)/shard_map/ppermute | solution.py:17
  19.3 39.1 %copy-start.20 = (f32[64,64]{1,0:T(8,128)}, f32[64,64]{1,0:T(8,128)S(1)}, u32[]{:S(2)}) copy-start(f32[64,64]{1,0:T(8,128)S(1)} %fusion.61) | copy-start | bytes 49156
  21.7 83.8 %copy-start.23 = (f32[16]{0:T(128)}, f32[16]{0:T(128)S(1)}, u32[]{:S(2)}) copy-start(f32[16]{0:T(128)S(1)} %compare_convert_fusion) | copy-start | bytes 196
  25.2 16.1 %all-to-all-start.1 = ((bf16[64,16,128]{2,0,1:T(8,128)(2,1)}), bf16[64,16,128]{2,0,1:T(8,128)(2,1)S(1)}, u32[]{:S(2)}, u32[]{:S(2)}) async-start(bf16[64,16,128]{2,0,1:T(8,128)(2,1)} %copy_bitcast_fusion.6), calls=%async_computation.1 | async-start | bytes 524288 | tf_op jit(solution)/shard_map/all_to_all | solution.py:177
  33.2 72.3 %copy-start.29 = (f32[16]{0:T(128)}, f32[16]{0:T(128)S(1)}, u32[]{:S(2)}) copy-start(f32[16]{0:T(128)S(1)} %and_select_fusion) | copy-start | bytes 196
  41.3 160.2 %copy-start.8 = (bf16[64,16,128]{2,0,1:T(8,128)(2,1)}, bf16[64,16,128]{2,0,1:T(8,128)(2,1)S(1)}, u32[]{:S(2)}) copy-start(bf16[64,16,128]{2,0,1:T(8,128)(2,1)S(1)} %all-to-all-done.1) | copy-start | bytes 786436
  41.3 13.3 %all-to-all-start.5 = ((bf16[64,16,128]{2,0,1:T(8,128)(2,1)}), bf16[64,16,128]{2,0,1:T(8,128)(2,1)S(1)}, u32[]{:S(2)}, u32[]{:S(2)}) async-start(bf16[64,16,128]{2,0,1:T(8,128)(2,1)} %copy_bitcast_fusion.5), calls=%async_computation.5 | async-start | bytes 524288 | tf_op jit(solution)/shard_map/all_to_all | solution.py:176
  46.0 23.4 %copy-start.15 = (f32[16,64,1,128]{3,1,0,2:T(8,128)}, f32[16,64,1,128]{3,1,0,2:T(8,128)S(1)}, u32[]{:S(2)}) copy-start(f32[16,64,1,128]{3,1,0,2:T(8,128)S(1)} %copy.51) | copy-start | bytes 1572868
  54.6 50.9 %copy-start.12 = (bf16[64,16,128]{2,0,1:T(8,128)(2,1)}, bf16[64,16,128]{2,0,1:T(8,128)(2,1)S(1)}, u32[]{:S(2)}) copy-start(bf16[64,16,128]{2,0,1:T(8,128)(2,1)S(1)} %all-to-all-done.5) | copy-start | bytes 786436
  54.6 14.7 %all-to-all-start.2 = ((bf16[64,16,256]{2,0,1:T(8,128)(2,1)}), bf16[64,16,256]{2,0,1:T(8,128)(2,1)S(1)}, u32[]{:S(2)}, u32[]{:S(2)}) async-start(bf16[64,16,256]{2,0,1:T(8,128)(2,1)} %bitcast.240), calls=%async_computation.2 | async-start | bytes 1048576 | tf_op jit(solution)/shard_map/all_to_all | solution.py:178
  69.3 6.2 %copy-start.6 = (bf16[64,16,256]{2,0,1:T(8,128)(2,1)}, bf16[64,16,256]{2,0,1:T(8,128)(2,1)S(1)}, u32[]{:S(2)}) copy-start(bf16[64,16,256]{2,0,1:T(8,128)(2,1)S(1)} %all-to-all-done.2) | copy-start | bytes 1572868
  69.3 36.1 %all-to-all-start.3 = ((bf16[64,16,256]{2,0,1:T(8,128)(2,1)}), bf16[64,16,256]{2,0,1:T(8,128)(2,1)S(1)}, u32[]{:S(2)}, u32[]{:S(2)}) async-start(bf16[64,16,256]{2,0,1:T(8,128)(2,1)} %bitcast.239), calls=%async_computation.3 | async-start | bytes 1048576 | tf_op jit(solution)/shard_map/all_to_all | solution.py:179
  72.9 132.7 %all-gather.9.cloned.1.call-start = ((), (), s32[]{:S(2)}) async-start(), calls=%async_computation.9 | async-start | bytes 2228224 | tf_op jit(solution)/shard_map/all_gather | solution.py:22
  104.7 0.7 copy-start.2
  104.7 0.8 copy-start.25
  104.7 0.8 copy-start.28
  104.7 5.2 %copy-start.22 = (f32[1,128]{1,0:T(1,128)}, f32[1,128]{1,0:T(1,128)S(1)}, u32[]{:S(2)}) copy-start(f32[1,128]{1,0:T(1,128)S(1)} %get-tuple-element.427) | copy-start | bytes 1540
  105.4 132.7 %all-gather.11.cloned.1.call-start = ((), (), s32[]{:S(2)}) async-start(), calls=%async_computation.10 | async-start | bytes 2228224 | tf_op jit(solution)/shard_map/all_gather | solution.py:22
  105.5 0.8 copy-start.4
  164.9 34.5 %copy-start.1 = (f32[1,128,256]{2,1,0:T(8,128)}, f32[1,128,256]{2,1,0:T(8,128)S(1)}, u32[]{:S(2)}) copy-start(f32[1,128,256]{2,1,0:T(8,128)S(1)} %get-tuple-element.433) | copy-start | bytes 393220
  199.5 4.2 %copy-start.13 = (bf16[64,16,128]{2,0,1:T(8,128)(2,1)S(1)}, bf16[64,16,128]{2,0,1:T(8,128)(2,1)}, u32[]{:S(2)}) copy-start(bf16[64,16,128]{2,0,1:T(8,128)(2,1)} %copy-done.12) | copy-start | bytes 786436
  205.7 59.1 %copy-start.26 = (f32[16,1,128]{2,1,0:T(1,128)S(1)}, f32[16,1,128]{2,1,0:T(1,128)}, u32[]{:S(2)}) copy-start(f32[16,1,128]{2,1,0:T(1,128)} %copy-done.25) | copy-start | bytes 24580
  205.7 59.1 %copy-start.30 = (f32[16]{0:T(128)S(1)}, f32[16]{0:T(128)}, u32[]{:S(2)}) copy-start(f32[16]{0:T(128)} %copy-done.29) | copy-start | bytes 196
  232.1 32.7 %copy-start.10 = (f32[1,128,256]{2,1,0:T(8,128)}, f32[1,128,256]{2,1,0:T(8,128)S(1)}, u32[]{:S(2)}) copy-start(f32[1,128,256]{2,1,0:T(8,128)S(1)} %get-tuple-element.429) | copy-start | bytes 393220
  264.7 2.4 copy-start.7
  264.8 4.1 %copy-start.17 = (f32[16,64,1,128]{3,1,0,2:T(8,128)S(1)}, f32[16,64,1,128]{3,1,0,2:T(8,128)}, u32[]{:S(2)}) copy-start(f32[16,64,1,128]{3,1,0,2:T(8,128)} %convolution_bitcast_fusion.1) | copy-start | bytes 1572868
  264.8 4.1 %copy-start.19 = (f32[16,128,64]{1,2,0:T(8,128)S(1)}, f32[16,128,64]{1,2,0:T(8,128)}, u32[]{:S(2)}) copy-start(f32[16,128,64]{1,2,0:T(8,128)} %fusion.63) | copy-start | bytes 1572868
  264.8 4.1 %copy-start.27 = (f32[16,1,128]{2,1,0:T(1,128)S(1)}, f32[16,1,128]{2,1,0:T(1,128)}, u32[]{:S(2)}) copy-start(f32[16,1,128]{2,1,0:T(1,128)} %copy-done.25) | copy-start | bytes 24580
  267.2 1.7 copy-start.3
  267.2 1.7 copy-start.5
  267.2 1.7 copy-start.9
  267.2 1.7 copy-start.11
  267.2 1.8 copy-start.14
  267.3 1.8 copy-start.24
  267.3 1.8 copy-start.31
  273.0 0.8 copy-start.16
  284.7 15.8 %all-to-all-start.8 = ((bf16[16,64,128]{2,1,0:T(8,128)(2,1)}), bf16[16,64,128]{2,1,0:T(8,128)(2,1)}, u32[]{:S(2)}, u32[]{:S(2)}) async-start(bf16[16,64,128]{2,1,0:T(8,128)(2,1)} %fusion.59), calls=%async_computation.8 | async-start | bytes 524288 | tf_op jit(solution)/shard_map/all_to_all | solution.py:193
  300.5 12.1 %all-to-all-start.6 = ((bf16[16,64,128]{2,1,0:T(8,128)(2,1)}), bf16[16,64,128]{2,1,0:T(8,128)(2,1)S(1)}, u32[]{:S(2)}, u32[]{:S(2)}) async-start(bf16[16,64,128]{2,1,0:T(8,128)(2,1)} %get-tuple-element.621), calls=%async_computation.6 | async-start | bytes 524288 | tf_op jit(solution)/shard_map/all_to_all | solution.py:191
  312.6 12.1 %all-to-all-start.4 = ((bf16[16,64,128]{2,1,0:T(8,128)(2,1)}), bf16[16,64,128]{2,1,0:T(8,128)(2,1)S(1)}, u32[]{:S(2)}, u32[]{:S(2)}) async-start(bf16[16,64,128]{2,1,0:T(8,128)(2,1)} %get-tuple-element.623), calls=%async_computation.4 | async-start | bytes 524288 | tf_op jit(solution)/shard_map/all_to_all | solution.py:190
  324.7 13.8 %all-to-all-start.7 = ((bf16[16,64,256]{2,1,0:T(8,128)(2,1)}), bf16[16,64,256]{2,1,0:T(8,128)(2,1)S(1)}, u32[]{:S(2)}, u32[]{:S(2)}) async-start(bf16[16,64,256]{2,1,0:T(8,128)(2,1)} %fusion.22), calls=%async_computation.7 | async-start | bytes 1048576 | tf_op jit(solution)/shard_map/all_to_all | solution.py:192
Sparse Core Ops, SparseCore 0:
  105.5 40.9 all-gather.8
  199.6 38.4 all-gather.10
where the time goes:
time: 350 us; the launch traced here: 346 us
  other arithmetic  112 us (32%)
  waiting for transfers between devices  57.4 us (16%)
  local copies, waits for them, and re-layouts  53.1 us (15%)
  starting transfers between devices  45.6 us (13%)
  blocking collectives  34.5 us (10%)
  matrix products  27 us (8%)
  between operations  15.2 us (4%)
    all_gather x2, blocking collectives, prefix(): everything = jax.tree.map(lambda part: lax.all_gather(part, axis), shard)  34.5 us
    select_n x32, other arithmetic, step(): return jax.tree.map(lambda a, b: jnp.where(reached, a, b), new, before)  31.8 us
    add x32, other arithmetic, advance(): decay_now[..., None] * carried[1] + update_now  31.8 us
    mul x32, local copies, waits for them, and re-layouts, compose(): return (former[0] * latter[0], latter[0][..., None] * former[1] + latter[1])  20.4 us
    dynamic_update_slice x64, other arithmetic, local_terms(): lax.scan(advance, initial, (decays, memory_increment))  20.4 us
    mul x32, other arithmetic, advance(): decay_now * carried[0]  18.9 us
    mul x32, local copies, waits for them, and re-layouts, advance(): decay_now[..., None] * carried[1] + update_now  10.6 us
    all_to_all x1, waiting for transfers between devices, per_device(): lax.all_to_all(values, 'head', split_axis=1, concat_axis=0, tiled=True)  8.88 us
  transfers between devices with their start and end apart: 12, of which 8 were waited for; matrix products, arithmetic and copies ran while one was open for 41% of the time, Pallas kernels for 0%

commit v1 on v0

v1 whole, which is shorter than its diff:
```python
import functools

import jax
import jax.numpy as jnp
from jax import lax
from jax.experimental import pallas as pl
from jax.experimental.pallas import tpu as pltpu
from jax.sharding import PartitionSpec as P

DK = 128
DV = 256
BLOCK = 64
HEADS = 16
NB = 16
IN_W = 3 * DK + 2 * DV
OUT_W = 3 * DK + DV
QC, KC, GC, VC, UC = 0, DK, 2 * DK, 3 * DK, 3 * DK + DV
MSG = DV + 8
SCALE = DK ** (-0.5)
BF = jnp.bfloat16
F32 = jnp.float32
VMEM = pltpu.VMEM
SMEM = pltpu.SMEM


def vspec():
    return pl.BlockSpec(memory_space=VMEM)


def sspec():
    return pl.BlockSpec(memory_space=SMEM)


def split(x):
    hi = x.astype(BF)
    lo = (x - hi.astype(F32)).astype(BF)
    return hi, lo


def dot(a, b, ca, cb):
    return lax.dot_general(a, b, (((ca,), (cb,)), ((), ())), preferred_element_type=F32)


def halves(r):
    return r[:, :DK] + r[:, DK:]


def triangle(lower, strict):
    i = lax.broadcasted_iota(jnp.int32, (BLOCK, BLOCK), 0)
    j = lax.broadcasted_iota(jnp.int32, (BLOCK, BLOCK), 1)
    if lower:
        return (j < i) if strict else (j <= i)
    return j >= i


def flags(live_ref, doc_ref, prev_ref):
    live = live_ref[0]
    lives, keeps = [], []
    for b in range(NB):
        lives.append(jnp.where(b < live, 1.0, 0.0).astype(F32))
        before = prev_ref[0] if b == 0 else doc_ref[b - 1] + 1
        keeps.append(jnp.where(before == doc_ref[b] + 1, 1.0, 0.0).astype(F32))
    return lives, keeps


def pack_kernel(q, k, g, v, u, out):
    for h in range(HEADS):
        kc = slice(h * DK, (h + 1) * DK)
        vc = slice(h * DV, (h + 1) * DV)
        out[h, :, QC : QC + DK] = q[:, kc]
        out[h, :, KC : KC + DK] = k[:, kc]
        out[h, :, GC : GC + DK] = g[:, kc]
        out[h, :, VC : VC + DV] = v[:, vc]
        out[h, :, UC : UC + DV] = u[:, vc]


def pack(q, k, g, v, u):
    return pl.pallas_call(
        pack_kernel,
        out_shape=jax.ShapeDtypeStruct((HEADS, BLOCK, IN_W), BF),
        in_specs=[vspec()] * 5,
        out_specs=vspec(),
        name="pack",
    )(q, k, g, v, u)


def unpack_kernel(x, dq, dk, dv, dg):
    for h in range(HEADS):
        kc = slice(h * DK, (h + 1) * DK)
        vc = slice(h * DV, (h + 1) * DV)
        dq[:, kc] = x[h, :, 0:DK]
        dk[:, kc] = x[h, :, DK : 2 * DK]
        dg[:, kc] = x[h, :, 2 * DK : 3 * DK]
        dv[:, vc] = x[h, :, 3 * DK :]


def unpack(x):
    narrow = jax.ShapeDtypeStruct((BLOCK, HEADS * DK), BF)
    wide = jax.ShapeDtypeStruct((BLOCK, HEADS * DV), BF)
    return pl.pallas_call(
        unpack_kernel,
        out_shape=(narrow, narrow, wide, narrow),
        in_specs=[vspec()],
        out_specs=(vspec(),) * 4,
        name="unpack",
    )(x)


def totals_kernel(live_ref, doc_ref, prev_ref, x, fwd, bwd, kw, qw, cs):
    lives, keeps = flags(live_ref, doc_ref, prev_ref)
    tri = jnp.where(triangle(True, False), 1.0, 0.0).astype(BF)
    for b in range(NB):
        cs[b] = dot(tri, x[b, :, GC : GC + DK], 1, 0) * lives[b]
    suffix = jnp.ones((1, DK), F32)
    for b in reversed(range(NB)):
        c = cs[b]
        last = c[BLOCK - 1 : BLOCK, :]
        kf = x[b, :, KC : KC + DK].astype(F32) * (jnp.exp(last - c) * (suffix * lives[b]))
        kw[b, :, :DK], kw[b, :, DK:] = split(kf)
        suffix = suffix * (keeps[b] * jnp.exp(last))
    prefix = jnp.ones((1, DK), F32)
    for b in range(NB):
        c = cs[b]
        last = c[BLOCK - 1 : BLOCK, :]
        qt = x[b, :, QC : QC + DK].astype(F32) * (
            jnp.exp(c) * (prefix * (keeps[b] * lives[b] * SCALE))
        )
        qw[b, :, :DK], qw[b, :, DK:] = split(qt)
        prefix = prefix * (keeps[b] * jnp.exp(last))
    rows = NB * BLOCK
    v = x[:, :, VC : VC + DV].reshape(rows, DV)
    u = x[:, :, UC : UC + DV].reshape(rows, DV)
    fwd[:DV] = halves(dot(v, kw[...].reshape(rows, 2 * DK), 0, 0))
    bwd[:DV] = halves(dot(u, qw[...].reshape(rows, 2 * DK), 0, 0))
    fwd[DV:] = jnp.broadcast_to(prefix, (MSG - DV, DK))
    bwd[DV:] = jnp.broadcast_to(prefix, (MSG - DV, DK))


def totals(live, doc, prev, x):
    msg = jax.ShapeDtypeStruct((MSG, DK), F32)
    return pl.pallas_call(
        totals_kernel,
        out_shape=(msg, msg),
        in_specs=[sspec()] * 3 + [vspec()],
        out_specs=(vspec(),) * 2,
        scratch_shapes=[
            VMEM((NB, BLOCK, 2 * DK), BF),
            VMEM((NB, BLOCK, 2 * DK), BF),
            VMEM((NB, BLOCK, DK), F32),
        ],
        compiler_params=pltpu.CompilerParams(vmem_limit_bytes=40 * 1024 * 1024),
        name="totals",
    )(live, doc, prev, x)


def joined(near, far):
    return jnp.concatenate(
        [near[DV : DV + 1] * far[:DV] + near[:DV], near[DV:] * far[DV:]], axis=0
    )


def shift(x, by):
    n = lax.axis_size("ctx")
    return lax.ppermute(x, "ctx", [(i, i + by) for i in range(n) if 0 <= i + by < n])


def window(fwd, bwd):
    f1, f2 = shift(fwd, 1), shift(fwd, 2)
    b1, b2 = shift(bwd, -1), shift(bwd, -2)
    f, b = joined(f1, f2), joined(b1, b2)
    f2, b2 = shift(f, 2), shift(b, -2)
    f, b = joined(f, f2), joined(b, b2)
    return f, shift(f, 4), b, shift(b, -4)


def grads_kernel(live_ref, doc_ref, prev_ref, x, fn, ff, bn, bf, out, states):
    lives, keeps = flags(live_ref, doc_ref, prev_ref)
    tri = jnp.where(triangle(True, False), 1.0, 0.0).astype(BF)
    causal = triangle(True, False)
    anti = triangle(False, False)
    upper = jnp.where(anti, 1.0, 0.0).astype(BF)
    strict = jnp.where(triangle(True, True), 1.0, 0.0).astype(BF)

    def cumul(b):
        return dot(tri, x[b, :, GC : GC + DK], 1, 0) * lives[b]

    state = fn[DV : DV + 1] * ff[:DV] + fn[:DV]
    for b in range(NB):
        entering = keeps[b] * state
        states[b] = entering
        if b < NB - 1:
            c = cumul(b)
            last = c[BLOCK - 1 : BLOCK, :]
            kf = x[b, :, KC : KC + DK].astype(F32) * (jnp.exp(last - c) * lives[b])
            kfs = jnp.concatenate(split(kf), axis=1)
            state = jnp.exp(last) * entering + halves(dot(x[b, :, VC : VC + DV], kfs, 0, 0))

    grad = bn[DV : DV + 1] * bf[:DV] + bn[:DV]
    for b in reversed(range(NB)):
        c = cumul(b)
        last = c[BLOCK - 1 : BLOCK, :]
        up, down, fade = jnp.exp(c), jnp.exp(-c), jnp.exp(last - c)
        k = x[b, :, KC : KC + DK].astype(F32) * lives[b]
        qt = x[b, :, QC : QC + DK].astype(F32) * (up * SCALE)
        kt = k * down
        kf = k * fade
        v = x[b, :, VC : VC + DV]
        u = x[b, :, UC : UC + DV] * lives[b].astype(BF)
        qh, ql = split(qt)
        kh, kl = split(kt)
        fh, fl = split(kf)
        st = dot(kh, qh, 1, 1) + dot(kh, ql, 1, 1) + dot(kl, qh, 1, 1)
        st = jnp.where(anti, st, 0.0)
        ds = jnp.where(causal, dot(u, v, 1, 1), 0.0)
        dst = jnp.where(anti, dot(v, u, 1, 1), 0.0)
        sh, sl = split(st)
        dh, dl = split(ds)
        th, tl = split(dst)
        entering = states[b]
        eh, el = split(entering)
        gh, gl = split(grad)
        kk = jnp.concatenate([kh, kl], axis=1)
        qq = jnp.concatenate([qh, ql], axis=1)
        query_part = (
            halves(dot(u, jnp.concatenate([eh, el], axis=1), 1, 0))
            + halves(dot(dh, kk, 1, 0))
            + dot(dl, kh, 1, 0)
        )
        rising = halves(dot(th, qq, 1, 0)) + dot(tl, qh, 1, 0)
        falling = halves(dot(v, jnp.concatenate([gh, gl], axis=1), 1, 0))
        value_grad = (
            dot(sh, u, 1, 0)
            + dot(sl, u, 1, 0)
            + dot(fh, gh, 1, 1)
            + dot(fh, gl, 1, 1)
            + dot(fl, gh, 1, 1)
        )
        carry = jnp.sum(grad * entering, axis=0, keepdims=True) * jnp.exp(last)
        ah, al = split(query_part * qt - rising * kt)
        bh, bl = split(falling * kf)
        gate = (
            dot(upper, ah, 1, 0) + dot(upper, al, 1, 0) + dot(strict, bh, 1, 0) + dot(strict, bl, 1, 0)
        )
        out[b, :, 0:DK] = (query_part * (up * SCALE)).astype(BF)
        out[b, :, DK : 2 * DK] = ((rising * down + falling * fade) * lives[b]).astype(BF)
        out[b, :, 2 * DK : 3 * DK] = ((gate + carry) * lives[b]).astype(BF)
        out[b, :, 3 * DK :] = value_grad.astype(BF)
        if b > 0:
            grad = keeps[b] * (jnp.exp(last) * grad + halves(dot(u, qq, 0, 0)))


def grads(live, doc, prev, x, fn, ff, bn, bf):
    return pl.pallas_call(
        grads_kernel,
        out_shape=jax.ShapeDtypeStruct((NB, BLOCK, OUT_W), BF),
        in_specs=[sspec()] * 3 + [vspec()] * 5,
        out_specs=vspec(),
        scratch_shapes=[VMEM((NB, DV, DK), F32)],
        compiler_params=pltpu.CompilerParams(vmem_limit_bytes=40 * 1024 * 1024),
        name="grads",
    )(live, doc, prev, x, fn, ff, bn, bf)


def per_device(queries, keys, values, out_grad, log_gates, live_blocks, block_doc):
    prev = shift(block_doc[NB - 1 :] + 1, 1)
    packed = pack(queries, keys, log_gates, values, out_grad)
    x = lax.all_to_all(packed, "head", split_axis=0, concat_axis=0, tiled=True)
    fwd, bwd = totals(live_blocks, block_doc, prev, x)
    fn, ff, bn, bf = window(fwd, bwd)
    y = grads(live_blocks, block_doc, prev, x, fn, ff, bn, bf)
    return unpack(lax.all_to_all(y, "head", split_axis=0, concat_axis=0, tiled=True))


def solution(mesh):
    rows = P(("ctx", "head"), None)
    return jax.shard_map(
        per_device,
        mesh=mesh,
        in_specs=(rows,) * 5 + (P("ctx"), P("ctx")),
        out_specs=(rows,) * 4,
        check_vma=False,
    )
```

time: 350 us -> 116 us (0.33)
  other arithmetic: 112 us -> 0.15 us
  local copies, waits for them, and re-layouts: 53.1 us -> 0.6 us
  matrix products: 27 us -> 0 us
  waiting for transfers between devices: 57.4 us -> 36.1 us
  Pallas kernels: 0 us -> 18.3 us
  between operations: 15.2 us -> 2.18 us
  blocking collectives: 34.5 us -> 22.9 us
  starting transfers between devices: 45.6 us -> 34.3 us
    all_to_all x9 -> x1, starting transfers between devices: 43.6 us -> 7.17 us  [per_device(): x = lax.all_to_all(packed, 'head', split_axis=0, concat_axis=0, tiled=True)]
    all_gather x2 -> x0, blocking collectives: 34.5 us -> none  [prefix(): everything = jax.tree.map(lambda part: lax.all_gather(part, axis), shard)]
    add x34 -> x4, other arithmetic: 33.9 us -> 0.08 us  [joined(): near[DV:DV + 1] * far[:DV] + near[:DV]]
    select_n x34 -> x0, other arithmetic: 32.5 us -> none  [the longest x32 31.8 us: step(): return jax.tree.map(lambda a, b: jnp.where(reached, a, b), new, before)]
    mul x64 -> x4, local copies, waits for them, and re-layouts: 31 us -> 0.01 us  [joined(): near[DV:DV + 1] * far[:DV] + near[:DV]]
    all_to_all x9 -> x1, waiting for transfers between devices: 51.3 us -> 20.8 us  [per_device(): x = lax.all_to_all(packed, 'head', split_axis=0, concat_axis=0, tiled=True)]
    dot_general x10 -> x0, matrix products: 27 us -> none  [the longest x1 3.97 us: finish(): jnp.einsum('nihv,nhkv->nihk', grad_out, incoming_state, precision=FINEST_...]
    ppermute x1 -> x9, starting transfers between devices: 1.91 us -> 27.1 us  [shift(): lax.ppermute(x, 'ctx', [(i, i + by) for i in range(n) if 0 <= i + by < n])]
  transfers between devices with their start and end apart: 12 -> 10, of which waited for: 8 -> 5; matrix products, arithmetic and copies ran while one was open for 41% -> 1% of each run, Pallas kernels for 0% -> 0%
where the time goes in v1:
time: 116 us; the launch traced here: 115 us
  waiting for transfers between devices  36.1 us (31%)
  starting transfers between devices  34.3 us (30%)
  blocking collectives  22.9 us (20%)
  Pallas kernels  18.3 us (16%)
  between operations  2.18 us (2%)
    ppermute x9, starting transfers between devices, shift(): lax.ppermute(x, 'ctx', [(i, i + by) for i in range(n) if 0 <= i + by < n])  27.1 us
    all_to_all x1, blocking collectives, per_device(): lax.all_to_all(y, 'head', split_axis=0, concat_axis=0, tiled=True)  22.9 us
    all_to_all x1, waiting for transfers between devices, per_device(): x = lax.all_to_all(packed, 'head', split_axis=0, concat_axis=0, tiled=True)  20.8 us
    ppermute x9, waiting for transfers between devices, shift(): lax.ppermute(x, 'ctx', [(i, i + by) for i in range(n) if 0 <= i + by < n])  15.2 us
    pallas_call x1, Pallas kernels, grads(): pl.pallas_call(grads_kernel, out_shape=jax.ShapeDtypeStruct((NB, BLOCK, O...  11 us
    all_to_all x1, starting transfers between devices, per_device(): x = lax.all_to_all(packed, 'head', split_axis=0, concat_axis=0, tiled=True)  7.17 us
    pallas_call x1, Pallas kernels, pack(): pl.pallas_call(pack_kernel, out_shape=jax.ShapeDtypeStruct((HEADS, BLOCK,...  2.9 us
    pallas_call x1, Pallas kernels, unpack(): pl.pallas_call(unpack_kernel, out_shape=(narrow, narrow, wide, narrow), i...  2.52 us
  transfers between devices with their start and end apart: 10, of which 5 were waited for; matrix products, arithmetic and copies ran while one was open for 1% of the time, Pallas kernels for 0%

profile of v1, /device:TPU:32, one launch (start us, length us, event | category | flops | bytes accessed | tf_op | source)
XLA Modules:
  0.0 114.6 jit_solution(16082814240128705357)
XLA Ops:
  0.6 2.9 %pack.1 = bf16[16,64,896]{2,1,0:T(8,128)(2,1)} custom-call(bf16[64,2048]{1,0:T(8,128)(2,1)} %q.1, bf16[64,2048]{1,0:T(8,128)(2,1)} %k.1, bf16[64,2048]{1,0:T(8,128)(2,1)} %g.1, bf16[64,4096]{1,0:T(8,128)(2,1)} %v.1, bf16[64,4096]{1,0:T(8,128)(2,1)} %u.1), custom_call_target="tpu_custom_call" | custom-call | tf_op jit(solution)/shard_map/pack/pallas_call | solution.py:78
  3.5 0.0 copy-start
  3.5 7.2 %all-to-all-start = ((bf16[16,64,896]{2,1,0:T(8,128)(2,1)}), bf16[16,64,896]{2,1,0:T(8,128)(2,1)S(1)}, u32[]{:S(2)}, u32[]{:S(2)}) async-start(bf16[16,64,896]{2,1,0:T(8,128)(2,1)} %pack.1), calls=%async_computation | async-start | bytes 3670016 | tf_op jit(solution)/shard_map/all_to_all | solution.py:267
  10.7 0.0 copy-done
  10.7 0.6 slice.51
  11.9 2.9 %collective-permute-start = (s32[1]{0:T(128)}, s32[1]{0:T(128)}, u32[]{:S(2)}, u32[]{:S(2)}) collective-permute-start(s32[1]{0:T(128)} %add.15), channel_id=1, source_target_pairs={{0,16},{16,32},{32,48},{48,64},{64,80},{80,96},{96,112},{112,128},... | collective-permute-start | bytes 20 | tf_op jit(solution)/shard_map/ppermute | solution.py:164
  15.5 1.5 %collective-permute-done.prev_ref = s32[1]{0:T(128)} collective-permute-done((s32[1]{0:T(128)}, s32[1]{0:T(128)}, u32[]{:S(2)}, u32[]{:S(2)}) %collective-permute-start) | collective-permute-done | bytes 36 | tf_op jit(solution)/shard_map/ppermute | solution.py:164
  16.9 20.8 %all-to-all-done.x = bf16[16,64,896]{2,1,0:T(8,128)(2,1)S(1)} async-done(((bf16[16,64,896]{2,1,0:T(8,128)(2,1)}), bf16[16,64,896]{2,1,0:T(8,128)(2,1)S(1)}, u32[]{:S(2)}, u32[]{:S(2)}) %all-to-all-start) | async-done | bytes 1835040 | tf_op jit(solution)/shard_map/all_to_all | solution.py:267
  37.7 2.0 %totals.1 = (f32[264,128]{1,0:T(8,128)S(1)}, f32[264,128]{1,0:T(8,128)S(1)}) custom-call(s32[1]{0:T(128)S(6)} %copy.11.live_ref, s32[16]{0:T(128)S(1)} %copy-done, s32[1]{0:T(128)} %collective-permute-done.prev_ref, bf16[16,64,896]{2,1,0:T(8,128)(2,1)S(1)} %all-to-all-done.x), custom_call_target="tpu_custom_call" | custom-call | tf_op jit(solution)/shard_map/totals/pallas_call | solution.py:141
  39.7 1.9 %collective-permute-start.1 = (f32[264,128]{1,0:T(8,128)S(1)}, f32[264,128]{1,0:T(8,128)S(1)}, u32[]{:S(2)}, u32[]{:S(2)}) collective-permute-start(f32[264,128]{1,0:T(8,128)S(1)} %get-tuple-element.6), channel_id=1, source_target_pairs={{0,16},{16,32},{32,48},{48,64},{64,80},{80,96},{96,112},{112,128},... | collective-permute-start | bytes 405512 | tf_op jit(solution)/shard_map/ppermute | solution.py:164
  41.7 3.8 %collective-permute-start.2 = (f32[264,128]{1,0:T(8,128)S(1)}, f32[264,128]{1,0:T(8,128)S(1)}, u32[]{:S(2)}, u32[]{:S(2)}) collective-permute-start(f32[264,128]{1,0:T(8,128)S(1)} %get-tuple-element.6), channel_id=1, source_target_pairs={{0,32},{16,48},{32,64},{48,80},{64,96},{80,112},{96,128},{112,144}... | collective-permute-start | bytes 405512 | tf_op jit(solution)/shard_map/ppermute | solution.py:164
  45.5 2.0 %collective-permute-start.6 = (f32[264,128]{1,0:T(8,128)S(1)}, f32[264,128]{1,0:T(8,128)S(1)}, u32[]{:S(2)}, u32[]{:S(2)}) collective-permute-start(f32[264,128]{1,0:T(8,128)S(1)} %get-tuple-element.7), channel_id=1, source_target_pairs={{32,0},{48,16},{64,32},{80,48},{96,64},{112,80},{128,96},{144,112}... | collective-permute-start | bytes 405512 | tf_op jit(solution)/shard_map/ppermute | solution.py:164
  47.5 2.6 %collective-permute-start.5 = (f32[264,128]{1,0:T(8,128)S(1)}, f32[264,128]{1,0:T(8,128)S(1)}, u32[]{:S(2)}, u32[]{:S(2)}) collective-permute-start(f32[264,128]{1,0:T(8,128)S(1)} %get-tuple-element.7), channel_id=1, source_target_pairs={{16,0},{32,16},{48,32},{64,48},{80,64},{96,80},{112,96},{128,112},... | collective-permute-start | bytes 405512 | tf_op jit(solution)/shard_map/ppermute | solution.py:164
  50.2 0.0 collective-permute-done.1
  50.2 0.0 collective-permute-done.2
  50.2 4.4 %collective-permute-start.3 = (f32[264,128]{1,0:T(8,128)S(1)}, f32[264,128]{1,0:T(8,128)S(1)}, u32[]{:S(2)}, u32[]{:S(2)}) collective-permute-start(f32[264,128]{1,0:T(8,128)S(1)} %pad_maximum_fusion), channel_id=1, source_target_pairs={{0,32},{16,48},{32,64},{48,80},{64,96},{80,112},{96,128},{112,144}... | collective-permute-start | bytes 405512 | tf_op jit(solution)/shard_map/ppermute | solution.py:164
  54.7 0.0 collective-permute-done.5
  54.7 0.0 collective-permute-done.6
  54.8 1.9 %collective-permute-start.7 = (f32[264,128]{1,0:T(8,128)S(1)}, f32[264,128]{1,0:T(8,128)S(1)}, u32[]{:S(2)}, u32[]{:S(2)}) collective-permute-start(f32[264,128]{1,0:T(8,128)S(1)} %pad_maximum_fusion.2), channel_id=1, source_target_pairs={{32,0},{48,16},{64,32},{80,48},{96,64},{112,80},{128,96},{144,112}... | collective-permute-start | bytes 405512 | tf_op jit(solution)/shard_map/ppermute | solution.py:164
  56.7 1.8 %collective-permute-done.3 = f32[264,128]{1,0:T(8,128)S(1)} collective-permute-done((f32[264,128]{1,0:T(8,128)S(1)}, f32[264,128]{1,0:T(8,128)S(1)}, u32[]{:S(2)}, u32[]{:S(2)}) %collective-permute-start.3) | collective-permute-done | bytes 135200 | tf_op jit(solution)/shard_map/ppermute | solution.py:164
  58.6 6.2 %collective-permute-start.4 = (f32[264,128]{1,0:T(8,128)S(1)}, f32[264,128]{1,0:T(8,128)S(1)}, u32[]{:S(2)}, u32[]{:S(2)}) collective-permute-start(f32[264,128]{1,0:T(8,128)S(1)} %pad_maximum_fusion.1.fn), channel_id=1, source_target_pairs={{0,64},{16,80},{32,96},{48,112},{64,128},{80,144},{96,160},{112,17... | collective-permute-start | bytes 405512 | tf_op jit(solution)/shard_map/ppermute | solution.py:164
  64.8 0.0 collective-permute-done.7
  64.9 1.3 %collective-permute-start.8 = (f32[264,128]{1,0:T(8,128)S(1)}, f32[264,128]{1,0:T(8,128)S(1)}, u32[]{:S(2)}, u32[]{:S(2)}) collective-permute-start(f32[264,128]{1,0:T(8,128)S(1)} %pad_maximum_fusion.3.bn), channel_id=1, source_target_pairs={{64,0},{80,16},{96,32},{112,48},{128,64},{144,80},{160,96},{176,11... | collective-permute-start | bytes 405512 | tf_op jit(solution)/shard_map/ppermute | solution.py:164
  66.2 3.6 %collective-permute-done.4.ff = f32[264,128]{1,0:T(8,128)S(1)} collective-permute-done((f32[264,128]{1,0:T(8,128)S(1)}, f32[264,128]{1,0:T(8,128)S(1)}, u32[]{:S(2)}, u32[]{:S(2)}) %collective-permute-start.4) | collective-permute-done | bytes 135200 | tf_op jit(solution)/shard_map/ppermute | solution.py:164
  69.8 8.4 %collective-permute-done.8.bf = f32[264,128]{1,0:T(8,128)S(1)} collective-permute-done((f32[264,128]{1,0:T(8,128)S(1)}, f32[264,128]{1,0:T(8,128)S(1)}, u32[]{:S(2)}, u32[]{:S(2)}) %collective-permute-start.8) | collective-permute-done | bytes 135200 | tf_op jit(solution)/shard_map/ppermute | solution.py:164
  78.2 11.0 %grads.1 = bf16[16,64,640]{2,1,0:T(8,128)(2,1)S(1)} custom-call(s32[1]{0:T(128)S(6)} %copy.11.live_ref, s32[16]{0:T(128)S(1)} %copy-done, s32[1]{0:T(128)} %collective-permute-done.prev_ref, bf16[16,64,896]{2,1,0:T(8,128)(2,1)S(1)} %all-to-all-done.x, f32[264,128]{1,0:T(8,128)S(1)} %pad_maximum_fusion.1.fn, f32[264,128]{1,0:T(8,128)S(1)} %collective-permute-done.4.ff, ...), custom_call_target="tpu_custom_call" | custom-call | tf_op jit(solution)/shard_map/grads/pallas_call | solution.py:253
  89.1 22.9 %all_to_all.10.x = bf16[16,64,640]{2,1,0:T(8,128)(2,1)} all-to-all(bf16[16,64,640]{2,1,0:T(8,128)(2,1)S(1)} %grads.1), channel_id=1, replica_groups=mesh['ctx'=16,'head'=16] {'head'}, dimensions={0} | all-to-all | bytes 2621440 | tf_op jit(solution)/shard_map/all_to_all | solution.py:271
  112.0 2.5 %unpack.1 = (bf16[64,2048]{1,0:T(8,128)(2,1)}, bf16[64,2048]{1,0:T(8,128)(2,1)}, bf16[64,4096]{1,0:T(8,128)(2,1)}, bf16[64,2048]{1,0:T(8,128)(2,1)}) custom-call(bf16[16,64,640]{2,1,0:T(8,128)(2,1)} %all_to_all.10.x), custom_call_target="tpu_custom_call" | custom-call | tf_op jit(solution)/shard_map/unpack/pallas_call | solution.py:100
  (16 shorter events, 0.2 us)
Async XLA Ops:
  3.5 7.2 %copy-start = (s32[16]{0:T(128)S(1)}, s32[16]{0:T(128)}, u32[]{:S(2)}) copy-start(s32[16]{0:T(128)} %doc_ref.3) | copy-start | bytes 196
  3.5 34.2 %all-to-all-start = ((bf16[16,64,896]{2,1,0:T(8,128)(2,1)}), bf16[16,64,896]{2,1,0:T(8,128)(2,1)S(1)}, u32[]{:S(2)}, u32[]{:S(2)}) async-start(bf16[16,64,896]{2,1,0:T(8,128)(2,1)} %pack.1), calls=%async_computation | async-start | bytes 3670016 | tf_op jit(solution)/shard_map/all_to_all | solution.py:267
  11.9 5.0 %collective-permute-start = (s32[1]{0:T(128)}, s32[1]{0:T(128)}, u32[]{:S(2)}, u32[]{:S(2)}) collective-permute-start(s32[1]{0:T(128)} %add.15), channel_id=1, source_target_pairs={{0,16},{16,32},{32,48},{48,64},{64,80},{80,96},{96,112},{112,128},... | collective-permute-start | bytes 20 | tf_op jit(solution)/shard_map/ppermute | solution.py:164
  39.7 10.4 %collective-permute-start.1 = (f32[264,128]{1,0:T(8,128)S(1)}, f32[264,128]{1,0:T(8,128)S(1)}, u32[]{:S(2)}, u32[]{:S(2)}) collective-permute-start(f32[264,128]{1,0:T(8,128)S(1)} %get-tuple-element.6), channel_id=1, source_target_pairs={{0,16},{16,32},{32,48},{48,64},{64,80},{80,96},{96,112},{112,128},... | collective-permute-start | bytes 405512 | tf_op jit(solution)/shard_map/ppermute | solution.py:164
  41.7 8.5 %collective-permute-start.2 = (f32[264,128]{1,0:T(8,128)S(1)}, f32[264,128]{1,0:T(8,128)S(1)}, u32[]{:S(2)}, u32[]{:S(2)}) collective-permute-start(f32[264,128]{1,0:T(8,128)S(1)} %get-tuple-element.6), channel_id=1, source_target_pairs={{0,32},{16,48},{32,64},{48,80},{64,96},{80,112},{96,128},{112,144}... | collective-permute-start | bytes 405512 | tf_op jit(solution)/shard_map/ppermute | solution.py:164
  45.5 9.3 %collective-permute-start.6 = (f32[264,128]{1,0:T(8,128)S(1)}, f32[264,128]{1,0:T(8,128)S(1)}, u32[]{:S(2)}, u32[]{:S(2)}) collective-permute-start(f32[264,128]{1,0:T(8,128)S(1)} %get-tuple-element.7), channel_id=1, source_target_pairs={{32,0},{48,16},{64,32},{80,48},{96,64},{112,80},{128,96},{144,112}... | collective-permute-start | bytes 405512 | tf_op jit(solution)/shard_map/ppermute | solution.py:164
  47.5 7.2 %collective-permute-start.5 = (f32[264,128]{1,0:T(8,128)S(1)}, f32[264,128]{1,0:T(8,128)S(1)}, u32[]{:S(2)}, u32[]{:S(2)}) collective-permute-start(f32[264,128]{1,0:T(8,128)S(1)} %get-tuple-element.7), channel_id=1, source_target_pairs={{16,0},{32,16},{48,32},{64,48},{80,64},{96,80},{112,96},{128,112},... | collective-permute-start | bytes 405512 | tf_op jit(solution)/shard_map/ppermute | solution.py:164
  50.2 8.3 %collective-permute-start.3 = (f32[264,128]{1,0:T(8,128)S(1)}, f32[264,128]{1,0:T(8,128)S(1)}, u32[]{:S(2)}, u32[]{:S(2)}) collective-permute-start(f32[264,128]{1,0:T(8,128)S(1)} %pad_maximum_fusion), channel_id=1, source_target_pairs={{0,32},{16,48},{32,64},{48,80},{64,96},{80,112},{96,128},{112,144}... | collective-permute-start | bytes 405512 | tf_op jit(solution)/shard_map/ppermute | solution.py:164
  54.8 10.0 %collective-permute-start.7 = (f32[264,128]{1,0:T(8,128)S(1)}, f32[264,128]{1,0:T(8,128)S(1)}, u32[]{:S(2)}, u32[]{:S(2)}) collective-permute-start(f32[264,128]{1,0:T(8,128)S(1)} %pad_maximum_fusion.2), channel_id=1, source_target_pairs={{32,0},{48,16},{64,32},{80,48},{96,64},{112,80},{128,96},{144,112}... | collective-permute-start | bytes 405512 | tf_op jit(solution)/shard_map/ppermute | solution.py:164
  58.6 11.2 %collective-permute-start.4 = (f32[264,128]{1,0:T(8,128)S(1)}, f32[264,128]{1,0:T(8,128)S(1)}, u32[]{:S(2)}, u32[]{:S(2)}) collective-permute-start(f32[264,128]{1,0:T(8,128)S(1)} %pad_maximum_fusion.1.fn), channel_id=1, source_target_pairs={{0,64},{16,80},{32,96},{48,112},{64,128},{80,144},{96,160},{112,17... | collective-permute-start | bytes 405512 | tf_op jit(solution)/shard_map/ppermute | solution.py:164
  64.9 13.3 %collective-permute-start.8 = (f32[264,128]{1,0:T(8,128)S(1)}, f32[264,128]{1,0:T(8,128)S(1)}, u32[]{:S(2)}, u32[]{:S(2)}) collective-permute-start(f32[264,128]{1,0:T(8,128)S(1)} %pad_maximum_fusion.3.bn), channel_id=1, source_target_pairs={{64,0},{80,16},{96,32},{112,48},{128,64},{144,80},{160,96},{176,11... | collective-permute-start | bytes 405512 | tf_op jit(solution)/shard_map/ppermute | solution.py:164

commit v2 on v1

--- a/solution.py
+++ b/solution.py
@@ -53,13 +53,16 @@
     return j >= i
 
 
-def flags(live_ref, doc_ref, prev_ref):
+def flags(live_ref, doc_ref, prev_ref, pos_ref):
     live = live_ref[0]
+    first = pos_ref[0] == 0
     lives, keeps = [], []
     for b in range(NB):
         lives.append(jnp.where(b < live, 1.0, 0.0).astype(F32))
-        before = prev_ref[0] if b == 0 else doc_ref[b - 1] + 1
-        keeps.append(jnp.where(before == doc_ref[b] + 1, 1.0, 0.0).astype(F32))
+        same = (prev_ref[NB - 1] if b == 0 else doc_ref[b - 1]) == doc_ref[b]
+        if b == 0:
+            same = same & jnp.logical_not(first)
+        keeps.append(jnp.where(same, 1.0, 0.0).astype(F32))
     return lives, keeps
 
 
@@ -106,8 +109,8 @@
     )(x)
 
 
-def totals_kernel(live_ref, doc_ref, prev_ref, x, fwd, bwd, kw, qw, cs):
-    lives, keeps = flags(live_ref, doc_ref, prev_ref)
+def totals_kernel(live_ref, doc_ref, prev_ref, pos_ref, x, kept, sent, kw, qw, cs):
+    lives, keeps = flags(live_ref, doc_ref, prev_ref, pos_ref)
     tri = jnp.where(triangle(True, False), 1.0, 0.0).astype(BF)
     for b in range(NB):
         cs[b] = dot(tri, x[b, :, GC : GC + DK], 1, 0) * lives[b]
@@ -130,18 +133,21 @@
     rows = NB * BLOCK
     v = x[:, :, VC : VC + DV].reshape(rows, DV)
     u = x[:, :, UC : UC + DV].reshape(rows, DV)
-    fwd[:DV] = halves(dot(v, kw[...].reshape(rows, 2 * DK), 0, 0))
-    bwd[:DV] = halves(dot(u, qw[...].reshape(rows, 2 * DK), 0, 0))
-    fwd[DV:] = jnp.broadcast_to(prefix, (MSG - DV, DK))
-    bwd[DV:] = jnp.broadcast_to(prefix, (MSG - DV, DK))
-
-
-def totals(live, doc, prev, x):
+    fwd = halves(dot(v, kw[...].reshape(rows, 2 * DK), 0, 0))
+    bwd = halves(dot(u, qw[...].reshape(rows, 2 * DK), 0, 0))
+    even = lax.rem(pos_ref[0], 2) == 0
+    kept[:DV] = jnp.where(even, fwd, bwd)
+    sent[:DV] = jnp.where(even, bwd, fwd)
+    kept[DV:] = jnp.broadcast_to(prefix, (MSG - DV, DK))
+    sent[DV:] = jnp.broadcast_to(prefix, (MSG - DV, DK))
+
+
+def totals(live, doc, prev, pos, x):
     msg = jax.ShapeDtypeStruct((MSG, DK), F32)
     return pl.pallas_call(
         totals_kernel,
         out_shape=(msg, msg),
-        in_specs=[sspec()] * 3 + [vspec()],
+        in_specs=[sspec()] * 4 + [vspec()],
         out_specs=(vspec(),) * 2,
         scratch_shapes=[
             VMEM((NB, BLOCK, 2 * DK), BF),
@@ -150,7 +156,7 @@
         ],
         compiler_params=pltpu.CompilerParams(vmem_limit_bytes=40 * 1024 * 1024),
         name="totals",
-    )(live, doc, prev, x)
+    )(live, doc, prev, pos, x)
 
 
 def joined(near, far):
@@ -159,22 +165,30 @@
     )
 
 
-def shift(x, by):
+def swapped(x):
     n = lax.axis_size("ctx")
-    return lax.ppermute(x, "ctx", [(i, i + by) for i in range(n) if 0 <= i + by < n])
-
-
-def window(fwd, bwd):
-    f1, f2 = shift(fwd, 1), shift(fwd, 2)
-    b1, b2 = shift(bwd, -1), shift(bwd, -2)
-    f, b = joined(f1, f2), joined(b1, b2)
-    f2, b2 = shift(f, 2), shift(b, -2)
-    f, b = joined(f, f2), joined(b, b2)
-    return f, shift(f, 4), b, shift(b, -4)
-
-
-def grads_kernel(live_ref, doc_ref, prev_ref, x, fn, ff, bn, bf, out, states):
-    lives, keeps = flags(live_ref, doc_ref, prev_ref)
+    return lax.ppermute(x, "ctx", [(i, i ^ 1) for i in range(n)])
+
+
+def upstream(x, index, by):
+    n = lax.axis_size("ctx")
+    moved = lax.ppermute(
+        x, "ctx", [(i, (i + (2 * by if i % 2 == 0 else -2 * by)) % n) for i in range(n)]
+    )
+    source = jnp.where(index % 2 == 0, index - 2 * by, index + 2 * by)
+    return jnp.where((source >= 0) & (source < n), moved, 0.0)
+
+
+def window(kept, sent, index):
+    other = swapped(sent)
+    chip = joined(other, kept)
+    e = joined(upstream(chip, index, 1), upstream(chip, index, 2))
+    e = joined(e, upstream(e, index, 2))
+    return e, swapped(joined(kept, e))
+
+
+def grads_kernel(live_ref, doc_ref, prev_ref, pos_ref, x, own, other, out, states):
+    lives, keeps = flags(live_ref, doc_ref, prev_ref, pos_ref)
     tri = jnp.where(triangle(True, False), 1.0, 0.0).astype(BF)
     causal = triangle(True, False)
     anti = triangle(False, False)
@@ -184,7 +198,8 @@
     def cumul(b):
         return dot(tri, x[b, :, GC : GC + DK], 1, 0) * lives[b]
 
-    state = fn[DV : DV + 1] * ff[:DV] + fn[:DV]
+    even = lax.rem(pos_ref[0], 2) == 0
+    state = jnp.where(even, own[:DV], other[:DV])
     for b in range(NB):
         entering = keeps[b] * state
         states[b] = entering
@@ -195,7 +210,7 @@
             kfs = jnp.concatenate(split(kf), axis=1)
             state = jnp.exp(last) * entering + halves(dot(x[b, :, VC : VC + DV], kfs, 0, 0))
 
-    grad = bn[DV : DV + 1] * bf[:DV] + bn[:DV]
+    grad = jnp.where(even, other[:DV], own[:DV])
     for b in reversed(range(NB)):
         c = cumul(b)
         last = c[BLOCK - 1 : BLOCK, :]
@@ -249,25 +264,28 @@
             grad = keeps[b] * (jnp.exp(last) * grad + halves(dot(u, qq, 0, 0)))
 
 
-def grads(live, doc, prev, x, fn, ff, bn, bf):
+def grads(live, doc, prev, pos, x, own, other):
     return pl.pallas_call(
         grads_kernel,
         out_shape=jax.ShapeDtypeStruct((NB, BLOCK, OUT_W), BF),
-        in_specs=[sspec()] * 3 + [vspec()] * 5,
+        in_specs=[sspec()] * 4 + [vspec()] * 3,
         out_specs=vspec(),
         scratch_shapes=[VMEM((NB, DV, DK), F32)],
         compiler_params=pltpu.CompilerParams(vmem_limit_bytes=40 * 1024 * 1024),
         name="grads",
-    )(live, doc, prev, x, fn, ff, bn, bf)
+    )(live, doc, prev, pos, x, own, other)
 
 
 def per_device(queries, keys, values, out_grad, log_gates, live_blocks, block_doc):
-    prev = shift(block_doc[NB - 1 :] + 1, 1)
+    n = lax.axis_size("ctx")
+    index = lax.axis_index("ctx")
+    pos = index.reshape(1)
+    prev = lax.ppermute(block_doc, "ctx", [(i, (i + 1) % n) for i in range(n)])
     packed = pack(queries, keys, log_gates, values, out_grad)
     x = lax.all_to_all(packed, "head", split_axis=0, concat_axis=0, tiled=True)
-    fwd, bwd = totals(live_blocks, block_doc, prev, x)
-    fn, ff, bn, bf = window(fwd, bwd)
-    y = grads(live_blocks, block_doc, prev, x, fn, ff, bn, bf)
+    kept, sent = totals(live_blocks, block_doc, prev, pos, x)
+    own, other = window(kept, sent, index)
+    y = grads(live_blocks, block_doc, prev, pos, x, own, other)
     return unpack(lax.all_to_all(y, "head", split_axis=0, concat_axis=0, tiled=True))
 
 

time: 116 us -> 98.9 us (0.85)
  the two profiles are of different devices: /device:TPU:32 before, /device:TPU:1 now
where the time goes in v2:
time: 98.9 us; the launch traced here: 98.6 us
  waiting for transfers between devices  29.9 us (30%)
  starting transfers between devices  27.5 us (28%)
  blocking collectives  22.3 us (23%)
  Pallas kernels  17.3 us (17%)
  between operations  1.39 us (1%)
    all_to_all x1, blocking collectives, per_device(): lax.all_to_all(y, 'head', split_axis=0, concat_axis=0, tiled=True)  22.3 us
    all_to_all x1, waiting for transfers between devices, per_device(): x = lax.all_to_all(packed, 'head', split_axis=0, concat_axis=0, tiled=True)  20.6 us
    pallas_call x1, Pallas kernels, grads(): pl.pallas_call(grads_kernel, out_shape=jax.ShapeDtypeStruct((NB, BLOCK, O...  10.4 us
    ppermute x3, starting transfers between devices, upstream(): lax.ppermute(x, 'ctx', [(i, (i + (2 * by if i % 2 == 0 else -2 * by)) % n...  9.77 us
    all_to_all x1, starting transfers between devices, per_device(): x = lax.all_to_all(packed, 'head', split_axis=0, concat_axis=0, tiled=True)  7.72 us
    ppermute x2, starting transfers between devices, swapped(): return lax.ppermute(x, 'ctx', [(i, i ^ 1) for i in range(n)])  7.54 us
    ppermute x3, waiting for transfers between devices, upstream(): lax.ppermute(x, 'ctx', [(i, (i + (2 * by if i % 2 == 0 else -2 * by)) % n...  7.27 us
    pallas_call x1, Pallas kernels, pack(): pl.pallas_call(pack_kernel, out_shape=jax.ShapeDtypeStruct((HEADS, BLOCK,...  2.9 us
  transfers between devices with their start and end apart: 7, of which 7 were waited for; matrix products, arithmetic and copies ran while one was open for 0% of the time, Pallas kernels for 0%

profile of v2, /device:TPU:1, one launch (start us, length us, event | category | flops | bytes accessed | tf_op | source)
XLA Modules:
  0.0 98.6 jit_solution(5685949036722915738)
XLA Ops:
  0.6 2.9 %pack.1 = bf16[16,64,896]{2,1,0:T(8,128)(2,1)} custom-call(bf16[64,2048]{1,0:T(8,128)(2,1)} %q.1, bf16[64,2048]{1,0:T(8,128)(2,1)} %k.1, bf16[64,2048]{1,0:T(8,128)(2,1)} %g.1, bf16[64,4096]{1,0:T(8,128)(2,1)} %v.1, bf16[64,4096]{1,0:T(8,128)(2,1)} %u.1), custom_call_target="tpu_custom_call" | custom-call | tf_op jit(solution)/shard_map/pack/pallas_call | solution.py:81
  3.5 0.0 copy-start
  3.5 7.7 %all-to-all-start = ((bf16[16,64,896]{2,1,0:T(8,128)(2,1)}), bf16[16,64,896]{2,1,0:T(8,128)(2,1)S(1)}, u32[]{:S(2)}, u32[]{:S(2)}) async-start(bf16[16,64,896]{2,1,0:T(8,128)(2,1)} %pack.1), calls=%async_computation | async-start | bytes 3670016 | tf_op jit(solution)/shard_map/all_to_all | solution.py:285
  11.3 0.0 copy-done
  11.3 2.5 %collective-permute-start = (s32[16]{0:T(128)S(1)}, s32[16]{0:T(128)S(1)}, u32[]{:S(2)}, u32[]{:S(2)}) collective-permute-start(s32[16]{0:T(128)S(1)} %copy-done), channel_id=1, source_target_pairs={{0,16},{16,32},{32,48},{48,64},{64,80},{80,96},{96,112},{112,128},... | collective-permute-start | bytes 200 | tf_op jit(solution)/shard_map/ppermute | solution.py:283
  14.4 0.1 collective-permute-done.prev_ref
  14.5 20.6 %all-to-all-done.x = bf16[16,64,896]{2,1,0:T(8,128)(2,1)S(1)} async-done(((bf16[16,64,896]{2,1,0:T(8,128)(2,1)}), bf16[16,64,896]{2,1,0:T(8,128)(2,1)S(1)}, u32[]{:S(2)}, u32[]{:S(2)}) %all-to-all-start) | async-done | bytes 1835040 | tf_op jit(solution)/shard_map/all_to_all | solution.py:285
  35.1 1.4 %totals.1 = (f32[264,128]{1,0:T(8,128)S(1)}, f32[264,128]{1,0:T(8,128)S(1)}) custom-call(s32[1]{0:T(128)S(6)} %copy.11.live_ref, s32[16]{0:T(128)S(1)} %copy-done, s32[16]{0:T(128)S(1)} %collective-permute-done.prev_ref, s32[1]{0:T(128)} %bitcast.pos_ref, bf16[16,64,896]{2,1,0:T(8,128)(2,1)S(1)} %all-to-all-done.x), custom_call_target="tpu_custom_call" | custom-call | tf_op jit(solution)/shard_map/totals/pallas_call | solution.py:147
  36.5 4.2 %collective-permute-start.1 = (f32[264,128]{1,0:T(8,128)S(1)}, f32[264,128]{1,0:T(8,128)S(1)}, u32[]{:S(2)}, u32[]{:S(2)}) collective-permute-start(f32[264,128]{1,0:T(8,128)S(1)} %get-tuple-element.6), channel_id=1, source_target_pairs={{0,16},{16,0},{32,48},{48,32},{64,80},{80,64},{96,112},{112,96},{1... | collective-permute-start | bytes 405512 | tf_op jit(solution)/shard_map/ppermute | solution.py:170
  40.8 1.0 %collective-permute-done.1 = f32[264,128]{1,0:T(8,128)S(1)} collective-permute-done((f32[264,128]{1,0:T(8,128)S(1)}, f32[264,128]{1,0:T(8,128)S(1)}, u32[]{:S(2)}, u32[]{:S(2)}) %collective-permute-start.1) | collective-permute-done | bytes 135200 | tf_op jit(solution)/shard_map/ppermute | solution.py:170
  41.8 5.7 %collective-permute-start.2 = (f32[264,128]{1,0:T(8,128)S(1)}, f32[264,128]{1,0:T(8,128)S(1)}, u32[]{:S(2)}, u32[]{:S(2)}) collective-permute-start(f32[264,128]{1,0:T(8,128)S(1)} %pad_maximum_fusion), channel_id=1, source_target_pairs={{0,32},{16,240},{32,64},{48,16},{64,96},{80,48},{96,128},{112,80},... | collective-permute-start | bytes 405512 | tf_op jit(solution)/shard_map/ppermute | solution.py:175
  47.5 1.2 %collective-permute-start.3 = (f32[264,128]{1,0:T(8,128)S(1)}, f32[264,128]{1,0:T(8,128)S(1)}, u32[]{:S(2)}, u32[]{:S(2)}) collective-permute-start(f32[264,128]{1,0:T(8,128)S(1)} %pad_maximum_fusion), channel_id=1, source_target_pairs={{0,64},{16,208},{32,96},{48,240},{64,128},{80,16},{96,160},{112,48... | collective-permute-start | bytes 405512 | tf_op jit(solution)/shard_map/ppermute | solution.py:175
  48.6 0.8 collective-permute-done.2
  49.5 3.1 %collective-permute-done.3 = f32[264,128]{1,0:T(8,128)S(1)} collective-permute-done((f32[264,128]{1,0:T(8,128)S(1)}, f32[264,128]{1,0:T(8,128)S(1)}, u32[]{:S(2)}, u32[]{:S(2)}) %collective-permute-start.3) | collective-permute-done | bytes 135200 | tf_op jit(solution)/shard_map/ppermute | solution.py:175
  52.6 2.9 %collective-permute-start.4 = (f32[264,128]{1,0:T(8,128)S(1)}, f32[264,128]{1,0:T(8,128)S(1)}, u32[]{:S(2)}, u32[]{:S(2)}) collective-permute-start(f32[264,128]{1,0:T(8,128)S(1)} %pad_maximum_fusion.1), channel_id=1, source_target_pairs={{0,64},{16,208},{32,96},{48,240},{64,128},{80,16},{96,160},{112,48... | collective-permute-start | bytes 405512 | tf_op jit(solution)/shard_map/ppermute | solution.py:175
  55.6 3.4 %collective-permute-done.4 = f32[264,128]{1,0:T(8,128)S(1)} collective-permute-done((f32[264,128]{1,0:T(8,128)S(1)}, f32[264,128]{1,0:T(8,128)S(1)}, u32[]{:S(2)}, u32[]{:S(2)}) %collective-permute-start.4) | collective-permute-done | bytes 135200 | tf_op jit(solution)/shard_map/ppermute | solution.py:175
  59.1 3.3 %collective-permute-start.5 = (f32[264,128]{1,0:T(8,128)S(1)}, f32[264,128]{1,0:T(8,128)S(1)}, u32[]{:S(2)}, u32[]{:S(2)}) collective-permute-start(f32[264,128]{1,0:T(8,128)S(1)} %pad_maximum_fusion.3), channel_id=1, source_target_pairs={{0,16},{16,0},{32,48},{48,32},{64,80},{80,64},{96,112},{112,96},{1... | collective-permute-start | bytes 405512 | tf_op jit(solution)/shard_map/ppermute | solution.py:170
  62.4 1.0 collective-permute-done.5.other
  63.3 10.4 %grads.1 = bf16[16,64,640]{2,1,0:T(8,128)(2,1)S(1)} custom-call(s32[1]{0:T(128)S(6)} %copy.11.live_ref, s32[16]{0:T(128)S(1)} %copy-done, s32[16]{0:T(128)S(1)} %collective-permute-done.prev_ref, s32[1]{0:T(128)} %bitcast.pos_ref, bf16[16,64,896]{2,1,0:T(8,128)(2,1)S(1)} %all-to-all-done.x, f32[264,128]{1,0:T(8,128)S(1)} %pad_maximum_fusion.2.own, ...), custom_call_target="tpu_custom_call" | custom-call | tf_op jit(solution)/shard_map/grads/pallas_call | solution.py:268
  73.8 22.3 %all_to_all.10.x = bf16[16,64,640]{2,1,0:T(8,128)(2,1)} all-to-all(bf16[16,64,640]{2,1,0:T(8,128)(2,1)S(1)} %grads.1), channel_id=1, replica_groups=mesh['ctx'=16,'head'=16] {'head'}, dimensions={0} | all-to-all | bytes 2621440 | tf_op jit(solution)/shard_map/all_to_all | solution.py:289
  96.1 2.5 %unpack.1 = (bf16[64,2048]{1,0:T(8,128)(2,1)}, bf16[64,2048]{1,0:T(8,128)(2,1)}, bf16[64,4096]{1,0:T(8,128)(2,1)}, bf16[64,2048]{1,0:T(8,128)(2,1)}) custom-call(bf16[16,64,640]{2,1,0:T(8,128)(2,1)} %all_to_all.10.x), custom_call_target="tpu_custom_call" | custom-call | tf_op jit(solution)/shard_map/unpack/pallas_call | solution.py:103
  (17 shorter events, 0.2 us)
Async XLA Ops:
  3.5 7.7 %copy-start = (s32[16]{0:T(128)S(1)}, s32[16]{0:T(128)}, u32[]{:S(2)}) copy-start(s32[16]{0:T(128)} %doc_ref.3) | copy-start | bytes 196
  3.5 31.6 %all-to-all-start = ((bf16[16,64,896]{2,1,0:T(8,128)(2,1)}), bf16[16,64,896]{2,1,0:T(8,128)(2,1)S(1)}, u32[]{:S(2)}, u32[]{:S(2)}) async-start(bf16[16,64,896]{2,1,0:T(8,128)(2,1)} %pack.1), calls=%async_computation | async-start | bytes 3670016 | tf_op jit(solution)/shard_map/all_to_all | solution.py:285
  11.3 3.2 %collective-permute-start = (s32[16]{0:T(128)S(1)}, s32[16]{0:T(128)S(1)}, u32[]{:S(2)}, u32[]{:S(2)}) collective-permute-start(s32[16]{0:T(128)S(1)} %copy-done), channel_id=1, source_target_pairs={{0,16},{16,32},{32,48},{48,64},{64,80},{80,96},{96,112},{112,128},... | collective-permute-start | bytes 200 | tf_op jit(solution)/shard_map/ppermute | solution.py:283
  36.5 5.2 %collective-permute-start.1 = (f32[264,128]{1,0:T(8,128)S(1)}, f32[264,128]{1,0:T(8,128)S(1)}, u32[]{:S(2)}, u32[]{:S(2)}) collective-permute-start(f32[264,128]{1,0:T(8,128)S(1)} %get-tuple-element.6), channel_id=1, source_target_pairs={{0,16},{16,0},{32,48},{48,32},{64,80},{80,64},{96,112},{112,96},{1... | collective-permute-start | bytes 405512 | tf_op jit(solution)/shard_map/ppermute | solution.py:170
  41.8 7.6 %collective-permute-start.2 = (f32[264,128]{1,0:T(8,128)S(1)}, f32[264,128]{1,0:T(8,128)S(1)}, u32[]{:S(2)}, u32[]{:S(2)}) collective-permute-start(f32[264,128]{1,0:T(8,128)S(1)} %pad_maximum_fusion), channel_id=1, source_target_pairs={{0,32},{16,240},{32,64},{48,16},{64,96},{80,48},{96,128},{112,80},... | collective-permute-start | bytes 405512 | tf_op jit(solution)/shard_map/ppermute | solution.py:175
  47.5 5.1 %collective-permute-start.3 = (f32[264,128]{1,0:T(8,128)S(1)}, f32[264,128]{1,0:T(8,128)S(1)}, u32[]{:S(2)}, u32[]{:S(2)}) collective-permute-start(f32[264,128]{1,0:T(8,128)S(1)} %pad_maximum_fusion), channel_id=1, source_target_pairs={{0,64},{16,208},{32,96},{48,240},{64,128},{80,16},{96,160},{112,48... | collective-permute-start | bytes 405512 | tf_op jit(solution)/shard_map/ppermute | solution.py:175
  52.6 6.3 %collective-permute-start.4 = (f32[264,128]{1,0:T(8,128)S(1)}, f32[264,128]{1,0:T(8,128)S(1)}, u32[]{:S(2)}, u32[]{:S(2)}) collective-permute-start(f32[264,128]{1,0:T(8,128)S(1)} %pad_maximum_fusion.1), channel_id=1, source_target_pairs={{0,64},{16,208},{32,96},{48,240},{64,128},{80,16},{96,160},{112,48... | collective-permute-start | bytes 405512 | tf_op jit(solution)/shard_map/ppermute | solution.py:175
  59.1 4.3 %collective-permute-start.5 = (f32[264,128]{1,0:T(8,128)S(1)}, f32[264,128]{1,0:T(8,128)S(1)}, u32[]{:S(2)}, u32[]{:S(2)}) collective-permute-start(f32[264,128]{1,0:T(8,128)S(1)} %pad_maximum_fusion.3), channel_id=1, source_target_pairs={{0,16},{16,0},{32,48},{48,32},{64,80},{80,64},{96,112},{112,96},{1... | collective-permute-start | bytes 405512 | tf_op jit(solution)/shard_map/ppermute | solution.py:170

commit v3 on v2

--- a/solution.py
+++ b/solution.py
@@ -66,8 +66,12 @@
     return lives, keeps
 
 
+PACK_STEPS = 2
+PER = HEADS // PACK_STEPS
+
+
 def pack_kernel(q, k, g, v, u, out):
-    for h in range(HEADS):
+    for h in range(PER):
         kc = slice(h * DK, (h + 1) * DK)
         vc = slice(h * DV, (h + 1) * DV)
         out[h, :, QC : QC + DK] = q[:, kc]
@@ -78,11 +82,14 @@
 
 
 def pack(q, k, g, v, u):
+    narrow = pl.BlockSpec((BLOCK, PER * DK), lambda i: (0, i))
+    wide = pl.BlockSpec((BLOCK, PER * DV), lambda i: (0, i))
     return pl.pallas_call(
         pack_kernel,
+        grid=(PACK_STEPS,),
         out_shape=jax.ShapeDtypeStruct((HEADS, BLOCK, IN_W), BF),
-        in_specs=[vspec()] * 5,
-        out_specs=vspec(),
+        in_specs=[narrow] * 3 + [wide] * 2,
+        out_specs=pl.BlockSpec((PER, BLOCK, IN_W), lambda i: (i, 0, 0)),
         name="pack",
     )(q, k, g, v, u)
 
@@ -105,6 +112,7 @@
         out_shape=(narrow, narrow, wide, narrow),
         in_specs=[vspec()],
         out_specs=(vspec(),) * 4,
+        compiler_params=pltpu.CompilerParams(vmem_limit_bytes=16 * 1024 * 1024),
         name="unpack",
     )(x)
 
@@ -187,81 +195,107 @@
     return e, swapped(joined(kept, e))
 
 
-def grads_kernel(live_ref, doc_ref, prev_ref, pos_ref, x, own, other, out, states):
+PAIR = 2 * BLOCK
+NP = NB // 2
+
+
+def rows_of(x, p, col, width):
+    return x[2 * p : 2 * p + 2, :, col : col + width].reshape(PAIR, width)
+
+
+def two(x):
+    return jnp.concatenate(split(x), axis=1)
+
+
+def grads_kernel(
+    live_ref, doc_ref, prev_ref, pos_ref, x, own, other, out, states, qw, kw, fw, qsw, ksw
+):
     lives, keeps = flags(live_ref, doc_ref, prev_ref, pos_ref)
-    tri = jnp.where(triangle(True, False), 1.0, 0.0).astype(BF)
-    causal = triangle(True, False)
-    anti = triangle(False, False)
-    upper = jnp.where(anti, 1.0, 0.0).astype(BF)
-    strict = jnp.where(triangle(True, True), 1.0, 0.0).astype(BF)
-
-    def cumul(b):
-        return dot(tri, x[b, :, GC : GC + DK], 1, 0) * lives[b]
+    i = lax.broadcasted_iota(jnp.int32, (PAIR, PAIR), 0)
+    j = lax.broadcasted_iota(jnp.int32, (PAIR, PAIR), 1)
+    first = i < BLOCK
+    same = first == (j < BLOCK)
+    one = lambda m: jnp.where(m, 1.0, 0.0).astype(F32)
+    tri = one((j <= i) & same).astype(BF)
+    low_same, low_cross = one((j <= i) & same), one((j < i) & jnp.logical_not(same))
+    up_same, up_cross = one((j >= i) & same), one((j > i) & jnp.logical_not(same))
+    upper, strict = one(j >= i).astype(BF), one(j < i).astype(BF)
+    sums = jnp.concatenate([upper, upper, strict, strict], axis=1)
+    first_v = lax.broadcasted_iota(jnp.int32, (PAIR, DV), 0) < BLOCK
 
     even = lax.rem(pos_ref[0], 2) == 0
     state = jnp.where(even, own[:DV], other[:DV])
-    for b in range(NB):
-        entering = keeps[b] * state
-        states[b] = entering
-        if b < NB - 1:
-            c = cumul(b)
-            last = c[BLOCK - 1 : BLOCK, :]
-            kf = x[b, :, KC : KC + DK].astype(F32) * (jnp.exp(last - c) * lives[b])
-            kfs = jnp.concatenate(split(kf), axis=1)
-            state = jnp.exp(last) * entering + halves(dot(x[b, :, VC : VC + DV], kfs, 0, 0))
+    ends = []
+    for p in range(NP):
+        a, b = 2 * p, 2 * p + 1
+        live = jnp.where(first, lives[a], lives[b])
+        c = dot(tri, rows_of(x, p, GC, DK), 1, 0) * live
+        ca, cb = c[BLOCK - 1 : BLOCK], c[PAIR - 1 : PAIR]
+        d = jnp.where(first, c - ca, c)
+        qs, ks = jnp.exp(d), jnp.exp(-d)
+        ea, eb = keeps[a] * jnp.exp(ca), jnp.exp(cb)
+        ends.append((ea, eb))
+        q = rows_of(x, p, QC, DK).astype(F32) * (qs * SCALE)
+        k = rows_of(x, p, KC, DK).astype(F32) * (ks * live)
+        kf = k * jnp.where(first, keeps[b] * eb, eb)
+        qsw[p], ksw[p] = qs, ks
+        qw[p], kw[p] = two(q), two(k)
+        kfs = two(kf)
+        fw[p] = kfs
+        states[p] = two(state)
+        if p < NP - 1:
+            state = (ea * (keeps[b] * eb)) * state + halves(dot(rows_of(x, p, VC, DV), kfs, 0, 0))
 
     grad = jnp.where(even, other[:DV], own[:DV])
-    for b in reversed(range(NB)):
-        c = cumul(b)
-        last = c[BLOCK - 1 : BLOCK, :]
-        up, down, fade = jnp.exp(c), jnp.exp(-c), jnp.exp(last - c)
-        k = x[b, :, KC : KC + DK].astype(F32) * lives[b]
-        qt = x[b, :, QC : QC + DK].astype(F32) * (up * SCALE)
-        kt = k * down
-        kf = k * fade
-        v = x[b, :, VC : VC + DV]
-        u = x[b, :, UC : UC + DV] * lives[b].astype(BF)
-        qh, ql = split(qt)
-        kh, kl = split(kt)
-        fh, fl = split(kf)
-        st = dot(kh, qh, 1, 1) + dot(kh, ql, 1, 1) + dot(kl, qh, 1, 1)
-        st = jnp.where(anti, st, 0.0)
-        ds = jnp.where(causal, dot(u, v, 1, 1), 0.0)
-        dst = jnp.where(anti, dot(v, u, 1, 1), 0.0)
-        sh, sl = split(st)
+    for p in reversed(range(NP)):
+        a, b = 2 * p, 2 * p + 1
+        ea, eb = ends[p]
+        live = jnp.where(first, lives[a], lives[b])
+        qin = jnp.where(first, ea, ea * keeps[b])
+        kout = jnp.where(first, keeps[b] * eb, eb)
+        qq, kk, ff = qw[p], kw[p], fw[p]
+        qh, ql, kh = qq[:, :DK], qq[:, DK:], kk[:, :DK]
+        qs, ks = qsw[p], ksw[p]
+        v = rows_of(x, p, VC, DV)
+        u = rows_of(x, p, UC, DV) * jnp.where(first_v, lives[a], lives[b]).astype(BF)
+        st = dot(kk, jnp.concatenate([qh, qh], axis=1), 1, 1) + dot(kh, ql, 1, 1)
+        up = up_same + keeps[b] * up_cross
+        st = jnp.where(up > 0.0, st, 0.0)
+        dst = dot(v, u, 1, 1) * up
+        ds = dot(u, v, 1, 1) * (low_same + keeps[b] * low_cross)
         dh, dl = split(ds)
         th, tl = split(dst)
-        entering = states[b]
-        eh, el = split(entering)
-        gh, gl = split(grad)
-        kk = jnp.concatenate([kh, kl], axis=1)
-        qq = jnp.concatenate([qh, ql], axis=1)
-        query_part = (
-            halves(dot(u, jnp.concatenate([eh, el], axis=1), 1, 0))
-            + halves(dot(dh, kk, 1, 0))
+        ss = states[p]
+        gg = two(grad)
+        gh, gl = gg[:, :DK], gg[:, DK:]
+        query = qs * (
+            halves(dot(dh, kk, 1, 0))
             + dot(dl, kh, 1, 0)
+            + qin * halves(dot(u, ss, 1, 0))
         )
-        rising = halves(dot(th, qq, 1, 0)) + dot(tl, qh, 1, 0)
-        falling = halves(dot(v, jnp.concatenate([gh, gl], axis=1), 1, 0))
-        value_grad = (
-            dot(sh, u, 1, 0)
-            + dot(sl, u, 1, 0)
-            + dot(fh, gh, 1, 1)
-            + dot(fh, gl, 1, 1)
-            + dot(fl, gh, 1, 1)
+        rising = ks * (halves(dot(th, qq, 1, 0)) + dot(tl, qh, 1, 0))
+        falling = (ks * kout) * halves(dot(v, gg, 1, 0))
+        value = (
+            dot(two(st), jnp.concatenate([u, u], axis=0), 1, 0)
+            + dot(ff, jnp.concatenate([gh, gh], axis=1), 1, 1)
+            + dot(ff[:, :DK], gl, 1, 1)
         )
-        carry = jnp.sum(grad * entering, axis=0, keepdims=True) * jnp.exp(last)
-        ah, al = split(query_part * qt - rising * kt)
-        bh, bl = split(falling * kf)
-        gate = (
-            dot(upper, ah, 1, 0) + dot(upper, al, 1, 0) + dot(strict, bh, 1, 0) + dot(strict, bl, 1, 0)
-        )
-        out[b, :, 0:DK] = (query_part * (up * SCALE)).astype(BF)
-        out[b, :, DK : 2 * DK] = ((rising * down + falling * fade) * lives[b]).astype(BF)
-        out[b, :, 2 * DK : 3 * DK] = ((gate + carry) * lives[b]).astype(BF)
-        out[b, :, 3 * DK :] = value_grad.astype(BF)
-        if b > 0:
-            grad = keeps[b] * (jnp.exp(last) * grad + halves(dot(u, qq, 0, 0)))
+        query = query * SCALE
+        q = rows_of(x, p, QC, DK).astype(F32)
+        k = rows_of(x, p, KC, DK).astype(F32) * live
+        decay = ea * (keeps[b] * eb)
+        s32 = ss[:, :DK].astype(F32) + ss[:, DK:].astype(F32)
+        carry = jnp.sum(grad * s32, axis=0, keepdims=True) * decay
+        terms = jnp.concatenate([*split(query * q - rising * k), *split(falling * k)], axis=0)
+        gate = dot(sums, terms, 1, 0) + carry
+        shape = lambda r: r.astype(BF).reshape(2, BLOCK, r.shape[1])
+        out[a : a + 2, :, 0:DK] = shape(query)
+        out[a : a + 2, :, DK : 2 * DK] = shape((rising + falling) * live)
+        out[a : a + 2, :, 2 * DK : 3 * DK] = shape(gate * live)
+        out[a : a + 2, :, 3 * DK :] = shape(value)
+        if p > 0:
+            qf = rows_of(x, p, QC, DK).astype(F32) * (qs * SCALE) * qin
+            grad = decay * grad + halves(dot(u, two(qf), 0, 0))
 
 
 def grads(live, doc, prev, pos, x, own, other):
@@ -270,7 +304,14 @@
         out_shape=jax.ShapeDtypeStruct((NB, BLOCK, OUT_W), BF),
         in_specs=[sspec()] * 4 + [vspec()] * 3,
         out_specs=vspec(),
-        scratch_shapes=[VMEM((NB, DV, DK), F32)],
+        scratch_shapes=[
+            VMEM((NP, DV, 2 * DK), BF),
+            VMEM((NP, PAIR, 2 * DK), BF),
+            VMEM((NP, PAIR, 2 * DK), BF),
+            VMEM((NP, PAIR, 2 * DK), BF),
+            VMEM((NP, PAIR, DK), F32),
+            VMEM((NP, PAIR, DK), F32),
+        ],
         compiler_params=pltpu.CompilerParams(vmem_limit_bytes=40 * 1024 * 1024),
         name="grads",
     )(live, doc, prev, pos, x, own, other)

time: 98.9 us -> 92.8 us (0.938)
  Pallas kernels: 17.3 us -> 11.4 us
    pallas_call x1, Pallas kernels: 10.4 us -> 6.06 us  [grads(): pl.pallas_call(grads_kernel, out_shape=jax.ShapeDtypeStruct((NB, BLOCK, O...]
    pallas_call x1, Pallas kernels: 2.52 us -> 1.28 us  [unpack(): pl.pallas_call(unpack_kernel, out_shape=(narrow, narrow, wide, narrow), i...]
where the time goes in v3:
time: 92.8 us; the launch traced here: 92.6 us
  waiting for transfers between devices  29.9 us (32%)
  starting transfers between devices  27.5 us (30%)
  blocking collectives  22.2 us (24%)
  Pallas kernels  11.4 us (12%)
  between operations  1.39 us (1%)
    all_to_all x1, blocking collectives, per_device(): lax.all_to_all(y, 'head', split_axis=0, concat_axis=0, tiled=True)  22.2 us
    all_to_all x1, waiting for transfers between devices, per_device(): x = lax.all_to_all(packed, 'head', split_axis=0, concat_axis=0, tiled=True)  20.6 us
    ppermute x3, starting transfers between devices, upstream(): lax.ppermute(x, 'ctx', [(i, (i + (2 * by if i % 2 == 0 else -2 * by)) % n...  9.77 us
    all_to_all x1, starting transfers between devices, per_device(): x = lax.all_to_all(packed, 'head', split_axis=0, concat_axis=0, tiled=True)  7.72 us
    ppermute x2, starting transfers between devices, swapped(): return lax.ppermute(x, 'ctx', [(i, i ^ 1) for i in range(n)])  7.54 us
    ppermute x3, waiting for transfers between devices, upstream(): lax.ppermute(x, 'ctx', [(i, (i + (2 * by if i % 2 == 0 else -2 * by)) % n...  7.27 us
    pallas_call x1, Pallas kernels, grads(): pl.pallas_call(grads_kernel, out_shape=jax.ShapeDtypeStruct((NB, BLOCK, O...  6.06 us
    pallas_call x1, Pallas kernels, pack(): pl.pallas_call(pack_kernel, grid=(PACK_STEPS,), out_shape=jax.ShapeDtypeS...  2.59 us
  transfers between devices with their start and end apart: 7, of which 7 were waited for; matrix products, arithmetic and copies ran while one was open for 0% of the time, Pallas kernels for 0%

profile of v3, /device:TPU:1, one launch (start us, length us, event | category | flops | bytes accessed | tf_op | source)
XLA Modules:
  0.0 92.6 jit_solution(10259142353541183612)
XLA Ops:
  0.6 2.6 %pack.1 = bf16[16,64,896]{2,1,0:T(8,128)(2,1)} custom-call(bf16[64,2048]{1,0:T(8,128)(2,1)} %q.1, bf16[64,2048]{1,0:T(8,128)(2,1)} %k.1, bf16[64,2048]{1,0:T(8,128)(2,1)} %g.1, bf16[64,4096]{1,0:T(8,128)(2,1)} %v.1, bf16[64,4096]{1,0:T(8,128)(2,1)} %u.1), custom_call_target="tpu_custom_call" | custom-call | tf_op jit(solution)/shard_map/pack/pallas_call | solution.py:87
  3.2 0.0 copy-start
  3.2 7.7 %all-to-all-start = ((bf16[16,64,896]{2,1,0:T(8,128)(2,1)}), bf16[16,64,896]{2,1,0:T(8,128)(2,1)S(1)}, u32[]{:S(2)}, u32[]{:S(2)}) async-start(bf16[16,64,896]{2,1,0:T(8,128)(2,1)} %pack.1), calls=%async_computation | async-start | bytes 3670016 | tf_op jit(solution)/shard_map/all_to_all | solution.py:326
  10.9 0.0 copy-done
  11.0 2.5 %collective-permute-start = (s32[16]{0:T(128)S(1)}, s32[16]{0:T(128)S(1)}, u32[]{:S(2)}, u32[]{:S(2)}) collective-permute-start(s32[16]{0:T(128)S(1)} %copy-done), channel_id=1, source_target_pairs={{0,16},{16,32},{32,48},{48,64},{64,80},{80,96},{96,112},{112,128},... | collective-permute-start | bytes 200 | tf_op jit(solution)/shard_map/ppermute | solution.py:324
  14.1 0.1 collective-permute-done.prev_ref
  14.2 20.6 %all-to-all-done.x = bf16[16,64,896]{2,1,0:T(8,128)(2,1)S(1)} async-done(((bf16[16,64,896]{2,1,0:T(8,128)(2,1)}), bf16[16,64,896]{2,1,0:T(8,128)(2,1)S(1)}, u32[]{:S(2)}, u32[]{:S(2)}) %all-to-all-start) | async-done | bytes 1835040 | tf_op jit(solution)/shard_map/all_to_all | solution.py:326
  34.8 1.4 %totals.1 = (f32[264,128]{1,0:T(8,128)S(1)}, f32[264,128]{1,0:T(8,128)S(1)}) custom-call(s32[1]{0:T(128)S(6)} %copy.11.live_ref, s32[16]{0:T(128)S(1)} %copy-done, s32[16]{0:T(128)S(1)} %collective-permute-done.prev_ref, s32[1]{0:T(128)} %bitcast.pos_ref, bf16[16,64,896]{2,1,0:T(8,128)(2,1)S(1)} %all-to-all-done.x), custom_call_target="tpu_custom_call" | custom-call | tf_op jit(solution)/shard_map/totals/pallas_call | solution.py:155
  36.2 4.2 %collective-permute-start.1 = (f32[264,128]{1,0:T(8,128)S(1)}, f32[264,128]{1,0:T(8,128)S(1)}, u32[]{:S(2)}, u32[]{:S(2)}) collective-permute-start(f32[264,128]{1,0:T(8,128)S(1)} %get-tuple-element.6), channel_id=1, source_target_pairs={{0,16},{16,0},{32,48},{48,32},{64,80},{80,64},{96,112},{112,96},{1... | collective-permute-start | bytes 405512 | tf_op jit(solution)/shard_map/ppermute | solution.py:178
  40.5 1.0 %collective-permute-done.1 = f32[264,128]{1,0:T(8,128)S(1)} collective-permute-done((f32[264,128]{1,0:T(8,128)S(1)}, f32[264,128]{1,0:T(8,128)S(1)}, u32[]{:S(2)}, u32[]{:S(2)}) %collective-permute-start.1) | collective-permute-done | bytes 135200 | tf_op jit(solution)/shard_map/ppermute | solution.py:178
  41.5 5.7 %collective-permute-start.2 = (f32[264,128]{1,0:T(8,128)S(1)}, f32[264,128]{1,0:T(8,128)S(1)}, u32[]{:S(2)}, u32[]{:S(2)}) collective-permute-start(f32[264,128]{1,0:T(8,128)S(1)} %pad_maximum_fusion), channel_id=1, source_target_pairs={{0,32},{16,240},{32,64},{48,16},{64,96},{80,48},{96,128},{112,80},... | collective-permute-start | bytes 405512 | tf_op jit(solution)/shard_map/ppermute | solution.py:183
  47.2 1.2 %collective-permute-start.3 = (f32[264,128]{1,0:T(8,128)S(1)}, f32[264,128]{1,0:T(8,128)S(1)}, u32[]{:S(2)}, u32[]{:S(2)}) collective-permute-start(f32[264,128]{1,0:T(8,128)S(1)} %pad_maximum_fusion), channel_id=1, source_target_pairs={{0,64},{16,208},{32,96},{48,240},{64,128},{80,16},{96,160},{112,48... | collective-permute-start | bytes 405512 | tf_op jit(solution)/shard_map/ppermute | solution.py:183
  48.3 0.8 collective-permute-done.2
  49.2 3.1 %collective-permute-done.3 = f32[264,128]{1,0:T(8,128)S(1)} collective-permute-done((f32[264,128]{1,0:T(8,128)S(1)}, f32[264,128]{1,0:T(8,128)S(1)}, u32[]{:S(2)}, u32[]{:S(2)}) %collective-permute-start.3) | collective-permute-done | bytes 135200 | tf_op jit(solution)/shard_map/ppermute | solution.py:183
  52.3 2.9 %collective-permute-start.4 = (f32[264,128]{1,0:T(8,128)S(1)}, f32[264,128]{1,0:T(8,128)S(1)}, u32[]{:S(2)}, u32[]{:S(2)}) collective-permute-start(f32[264,128]{1,0:T(8,128)S(1)} %pad_maximum_fusion.1), channel_id=1, source_target_pairs={{0,64},{16,208},{32,96},{48,240},{64,128},{80,16},{96,160},{112,48... | collective-permute-start | bytes 405512 | tf_op jit(solution)/shard_map/ppermute | solution.py:183
  55.3 3.4 %collective-permute-done.4 = f32[264,128]{1,0:T(8,128)S(1)} collective-permute-done((f32[264,128]{1,0:T(8,128)S(1)}, f32[264,128]{1,0:T(8,128)S(1)}, u32[]{:S(2)}, u32[]{:S(2)}) %collective-permute-start.4) | collective-permute-done | bytes 135200 | tf_op jit(solution)/shard_map/ppermute | solution.py:183
  58.7 3.3 %collective-permute-start.5 = (f32[264,128]{1,0:T(8,128)S(1)}, f32[264,128]{1,0:T(8,128)S(1)}, u32[]{:S(2)}, u32[]{:S(2)}) collective-permute-start(f32[264,128]{1,0:T(8,128)S(1)} %pad_maximum_fusion.3), channel_id=1, source_target_pairs={{0,16},{16,0},{32,48},{48,32},{64,80},{80,64},{96,112},{112,96},{1... | collective-permute-start | bytes 405512 | tf_op jit(solution)/shard_map/ppermute | solution.py:178
  62.0 1.0 %collective-permute-done.5.other = f32[264,128]{1,0:T(8,128)S(1)} collective-permute-done((f32[264,128]{1,0:T(8,128)S(1)}, f32[264,128]{1,0:T(8,128)S(1)}, u32[]{:S(2)}, u32[]{:S(2)}) %collective-permute-start.5) | collective-permute-done | bytes 135200 | tf_op jit(solution)/shard_map/ppermute | solution.py:178
  63.0 6.1 %grads.1 = bf16[16,64,640]{2,1,0:T(8,128)(2,1)S(1)} custom-call(s32[1]{0:T(128)S(6)} %copy.11.live_ref, s32[16]{0:T(128)S(1)} %copy-done, s32[16]{0:T(128)S(1)} %collective-permute-done.prev_ref, s32[1]{0:T(128)} %bitcast.pos_ref, bf16[16,64,896]{2,1,0:T(8,128)(2,1)S(1)} %all-to-all-done.x, f32[264,128]{1,0:T(8,128)S(1)} %pad_maximum_fusion.2.own, ...), custom_call_target="tpu_custom_call" | custom-call | tf_op jit(solution)/shard_map/grads/pallas_call | solution.py:302
  69.1 22.2 %all_to_all.10.x = bf16[16,64,640]{2,1,0:T(8,128)(2,1)S(1)} all-to-all(bf16[16,64,640]{2,1,0:T(8,128)(2,1)S(1)} %grads.1), channel_id=1, replica_groups=mesh['ctx'=16,'head'=16] {'head'}, dimensions={0} | all-to-all | bytes 2621440 | tf_op jit(solution)/shard_map/all_to_all | solution.py:330
  91.3 1.3 %unpack.1 = (bf16[64,2048]{1,0:T(8,128)(2,1)}, bf16[64,2048]{1,0:T(8,128)(2,1)}, bf16[64,4096]{1,0:T(8,128)(2,1)}, bf16[64,2048]{1,0:T(8,128)(2,1)}) custom-call(bf16[16,64,640]{2,1,0:T(8,128)(2,1)S(1)} %all_to_all.10.x), custom_call_target="tpu_custom_call" | custom-call | tf_op jit(solution)/shard_map/unpack/pallas_call | solution.py:110
  (17 shorter events, 0.2 us)
Async XLA Ops:
  3.2 7.7 %copy-start = (s32[16]{0:T(128)S(1)}, s32[16]{0:T(128)}, u32[]{:S(2)}) copy-start(s32[16]{0:T(128)} %doc_ref.3) | copy-start | bytes 196
  3.2 31.6 %all-to-all-start = ((bf16[16,64,896]{2,1,0:T(8,128)(2,1)}), bf16[16,64,896]{2,1,0:T(8,128)(2,1)S(1)}, u32[]{:S(2)}, u32[]{:S(2)}) async-start(bf16[16,64,896]{2,1,0:T(8,128)(2,1)} %pack.1), calls=%async_computation | async-start | bytes 3670016 | tf_op jit(solution)/shard_map/all_to_all | solution.py:326
  11.0 3.2 %collective-permute-start = (s32[16]{0:T(128)S(1)}, s32[16]{0:T(128)S(1)}, u32[]{:S(2)}, u32[]{:S(2)}) collective-permute-start(s32[16]{0:T(128)S(1)} %copy-done), channel_id=1, source_target_pairs={{0,16},{16,32},{32,48},{48,64},{64,80},{80,96},{96,112},{112,128},... | collective-permute-start | bytes 200 | tf_op jit(solution)/shard_map/ppermute | solution.py:324
  36.2 5.2 %collective-permute-start.1 = (f32[264,128]{1,0:T(8,128)S(1)}, f32[264,128]{1,0:T(8,128)S(1)}, u32[]{:S(2)}, u32[]{:S(2)}) collective-permute-start(f32[264,128]{1,0:T(8,128)S(1)} %get-tuple-element.6), channel_id=1, source_target_pairs={{0,16},{16,0},{32,48},{48,32},{64,80},{80,64},{96,112},{112,96},{1... | collective-permute-start | bytes 405512 | tf_op jit(solution)/shard_map/ppermute | solution.py:178
  41.5 7.6 %collective-permute-start.2 = (f32[264,128]{1,0:T(8,128)S(1)}, f32[264,128]{1,0:T(8,128)S(1)}, u32[]{:S(2)}, u32[]{:S(2)}) collective-permute-start(f32[264,128]{1,0:T(8,128)S(1)} %pad_maximum_fusion), channel_id=1, source_target_pairs={{0,32},{16,240},{32,64},{48,16},{64,96},{80,48},{96,128},{112,80},... | collective-permute-start | bytes 405512 | tf_op jit(solution)/shard_map/ppermute | solution.py:183
  47.2 5.1 %collective-permute-start.3 = (f32[264,128]{1,0:T(8,128)S(1)}, f32[264,128]{1,0:T(8,128)S(1)}, u32[]{:S(2)}, u32[]{:S(2)}) collective-permute-start(f32[264,128]{1,0:T(8,128)S(1)} %pad_maximum_fusion), channel_id=1, source_target_pairs={{0,64},{16,208},{32,96},{48,240},{64,128},{80,16},{96,160},{112,48... | collective-permute-start | bytes 405512 | tf_op jit(solution)/shard_map/ppermute | solution.py:183
  52.3 6.3 %collective-permute-start.4 = (f32[264,128]{1,0:T(8,128)S(1)}, f32[264,128]{1,0:T(8,128)S(1)}, u32[]{:S(2)}, u32[]{:S(2)}) collective-permute-start(f32[264,128]{1,0:T(8,128)S(1)} %pad_maximum_fusion.1), channel_id=1, source_target_pairs={{0,64},{16,208},{32,96},{48,240},{64,128},{80,16},{96,160},{112,48... | collective-permute-start | bytes 405512 | tf_op jit(solution)/shard_map/ppermute | solution.py:183
  58.7 4.3 %collective-permute-start.5 = (f32[264,128]{1,0:T(8,128)S(1)}, f32[264,128]{1,0:T(8,128)S(1)}, u32[]{:S(2)}, u32[]{:S(2)}) collective-permute-start(f32[264,128]{1,0:T(8,128)S(1)} %pad_maximum_fusion.3), channel_id=1, source_target_pairs={{0,16},{16,0},{32,48},{48,32},{64,80},{80,64},{96,112},{112,96},{1... | collective-permute-start | bytes 405512 | tf_op jit(solution)/shard_map/ppermute | solution.py:178

commit v4 on v3

--- a/solution.py
+++ b/solution.py
@@ -187,12 +187,15 @@
     return jnp.where((source >= 0) & (source < n), moved, 0.0)
 
 
-def window(kept, sent, index):
+def window(kept, sent, index, beside):
     other = swapped(sent)
     chip = joined(other, kept)
-    e = joined(upstream(chip, index, 1), upstream(chip, index, 2))
+    near, far = upstream(chip, index, 1), upstream(chip, index, 2)
+    done = beside(chip)
+    near, far, done = lax.optimization_barrier((near, far, done))
+    e = joined(near, far)
     e = joined(e, upstream(e, index, 2))
-    return e, swapped(joined(kept, e))
+    return e, swapped(joined(kept, e)), done
 
 
 PAIR = 2 * BLOCK
@@ -207,25 +210,32 @@
     return jnp.concatenate(split(x), axis=1)
 
 
-def grads_kernel(
-    live_ref, doc_ref, prev_ref, pos_ref, x, own, other, out, states, qw, kw, fw, qsw, ksw
-):
-    lives, keeps = flags(live_ref, doc_ref, prev_ref, pos_ref)
+def one(mask):
+    return jnp.where(mask, 1.0, 0.0).astype(F32)
+
+
+def pair_masks():
     i = lax.broadcasted_iota(jnp.int32, (PAIR, PAIR), 0)
     j = lax.broadcasted_iota(jnp.int32, (PAIR, PAIR), 1)
     first = i < BLOCK
-    same = first == (j < BLOCK)
-    one = lambda m: jnp.where(m, 1.0, 0.0).astype(F32)
+    return i, j, first, first == (j < BLOCK)
+
+
+def local_kernel(
+    live_ref, doc_ref, prev_ref, pos_ref, x,
+    query_o, rise_o, fall_o, value_o, qin_o, kout_o, kf_o, state_o, grad_o, small_o,
+    qw, kw, fw, qsw, ksw,
+):
+    lives, keeps = flags(live_ref, doc_ref, prev_ref, pos_ref)
+    i, j, first, same = pair_masks()
+    cross = jnp.logical_not(same)
     tri = one((j <= i) & same).astype(BF)
-    low_same, low_cross = one((j <= i) & same), one((j < i) & jnp.logical_not(same))
-    up_same, up_cross = one((j >= i) & same), one((j > i) & jnp.logical_not(same))
-    upper, strict = one(j >= i).astype(BF), one(j < i).astype(BF)
-    sums = jnp.concatenate([upper, upper, strict, strict], axis=1)
+    low_same, low_cross = one((j <= i) & same), one((j < i) & cross)
+    up_same, up_cross = one((j >= i) & same), one((j > i) & cross)
     first_v = lax.broadcasted_iota(jnp.int32, (PAIR, DV), 0) < BLOCK
 
-    even = lax.rem(pos_ref[0], 2) == 0
-    state = jnp.where(even, own[:DV], other[:DV])
     ends = []
+    prefix = jnp.ones((1, DK), F32)
     for p in range(NP):
         a, b = 2 * p, 2 * p + 1
         live = jnp.where(first, lives[a], lives[b])
@@ -234,26 +244,33 @@
         d = jnp.where(first, c - ca, c)
         qs, ks = jnp.exp(d), jnp.exp(-d)
         ea, eb = keeps[a] * jnp.exp(ca), jnp.exp(cb)
-        ends.append((ea, eb))
+        decay = ea * (keeps[b] * eb)
+        ends.append((ea, eb, decay))
         q = rows_of(x, p, QC, DK).astype(F32) * (qs * SCALE)
         k = rows_of(x, p, KC, DK).astype(F32) * (ks * live)
         kf = k * jnp.where(first, keeps[b] * eb, eb)
         qsw[p], ksw[p] = qs, ks
         qw[p], kw[p] = two(q), two(k)
-        kfs = two(kf)
-        fw[p] = kfs
-        states[p] = two(state)
+        fw[p] = kf
+        small_o[p, 0:1] = prefix
+        qin_o[p] = (qs * (live * SCALE)) * (jnp.where(first, ea, ea * keeps[b]) * prefix)
+        prefix = prefix * decay
+        if p == 0:
+            state_o[p] = jnp.zeros((DV, DK), F32)
+        else:
+            state_o[p] = state
         if p < NP - 1:
-            state = (ea * (keeps[b] * eb)) * state + halves(dot(rows_of(x, p, VC, DV), kfs, 0, 0))
-
-    grad = jnp.where(even, other[:DV], own[:DV])
+            update = halves(dot(rows_of(x, p, VC, DV), two(kf), 0, 0))
+            state = update if p == 0 else decay * state + update
+
+    suffix = jnp.ones((1, DK), F32)
     for p in reversed(range(NP)):
         a, b = 2 * p, 2 * p + 1
-        ea, eb = ends[p]
+        ea, eb, decay = ends[p]
         live = jnp.where(first, lives[a], lives[b])
         qin = jnp.where(first, ea, ea * keeps[b])
         kout = jnp.where(first, keeps[b] * eb, eb)
-        qq, kk, ff = qw[p], kw[p], fw[p]
+        qq, kk = qw[p], kw[p]
         qh, ql, kh = qq[:, :DK], qq[:, DK:], kk[:, :DK]
         qs, ks = qsw[p], ksw[p]
         v = rows_of(x, p, VC, DV)
@@ -265,56 +282,124 @@
         ds = dot(u, v, 1, 1) * (low_same + keeps[b] * low_cross)
         dh, dl = split(ds)
         th, tl = split(dst)
-        ss = states[p]
-        gg = two(grad)
-        gh, gl = gg[:, :DK], gg[:, DK:]
-        query = qs * (
-            halves(dot(dh, kk, 1, 0))
-            + dot(dl, kh, 1, 0)
-            + qin * halves(dot(u, ss, 1, 0))
+        query = halves(dot(dh, kk, 1, 0)) + dot(dl, kh, 1, 0)
+        if p > 0:
+            query = query + qin * halves(dot(u, two(state_o[p]), 1, 0))
+        query_o[p] = query * (qs * SCALE)
+        rise_o[p] = ks * live * (halves(dot(th, qq, 1, 0)) + dot(tl, qh, 1, 0))
+        value = dot(two(st), jnp.concatenate([u, u], axis=0), 1, 0)
+        fall_scale = (ks * live) * kout
+        kf = fw[p]
+        if p < NP - 1:
+            gg = two(grad)
+            gh, gl = gg[:, :DK], gg[:, DK:]
+            ff = two(kf)
+            value = (
+                value
+                + dot(ff, jnp.concatenate([gh, gh], axis=1), 1, 1)
+                + dot(ff[:, :DK], gl, 1, 1)
+            )
+            fall_o[p] = fall_scale * halves(dot(v, gg, 1, 0))
+            grad_o[p] = grad
+            small_o[p, 3:4] = jnp.sum(grad * state_o[p], axis=0, keepdims=True) * decay
+        else:
+            fall_o[p] = jnp.zeros((PAIR, DK), F32)
+            grad_o[p] = jnp.zeros((DV, DK), F32)
+            small_o[p, 3:4] = jnp.zeros((1, DK), F32)
+        value_o[p] = value
+        small_o[p, 1:2] = suffix
+        small_o[p, 2:3] = decay
+        kout_o[p] = fall_scale * suffix
+        kf_o[p] = two(kf * suffix)
+        suffix = suffix * decay
+        if p > 0:
+            qf = rows_of(x, p, QC, DK).astype(F32) * (qs * SCALE) * qin
+            update = halves(dot(u, two(qf), 0, 0))
+            grad = update if p == NP - 1 else decay * grad + update
+
+
+def local(live, doc, prev, pos, x):
+    f = lambda *s: jax.ShapeDtypeStruct((NP,) + s, F32)
+    t = f(PAIR, DK)
+    return pl.pallas_call(
+        local_kernel,
+        out_shape=(
+            t, t, t, f(PAIR, DV), t, t,
+            jax.ShapeDtypeStruct((NP, PAIR, 2 * DK), BF),
+            f(DV, DK), f(DV, DK), f(8, DK),
+        ),
+        in_specs=[sspec()] * 4 + [vspec()],
+        out_specs=(vspec(),) * 10,
+        scratch_shapes=[
+            VMEM((NP, PAIR, 2 * DK), BF),
+            VMEM((NP, PAIR, 2 * DK), BF),
+            VMEM((NP, PAIR, DK), F32),
+            VMEM((NP, PAIR, DK), F32),
+            VMEM((NP, PAIR, DK), F32),
+        ],
+        compiler_params=pltpu.CompilerParams(vmem_limit_bytes=32 * 1024 * 1024),
+        cost_estimate=pl.CostEstimate(flops=4 * 10**9, bytes_accessed=9 * 10**6, transcendentals=10**6),
+        name="local",
+    )(live, doc, prev, pos, x)
+
+
+def finish_kernel(
+    live_ref, pos_ref, x, own, other,
+    query_i, rise_i, fall_i, value_i, qin_i, kout_i, kf_i, state_i, grad_i, small_i,
+    out, qs, fs,
+):
+    i, j, first, _ = pair_masks()
+    upper, strict = one(j >= i).astype(BF), one(j < i).astype(BF)
+    sums = jnp.concatenate([upper, upper, strict, strict], axis=1)
+    even = lax.rem(pos_ref[0], 2) == 0
+    state = jnp.where(even, own[:DV], other[:DV])
+    grad = jnp.where(even, other[:DV], own[:DV])
+    rows = NB * BLOCK
+    u = x[:, :, UC : UC + DV].reshape(rows, DV)
+    v = x[:, :, VC : VC + DV].reshape(rows, DV)
+    gg = two(grad)
+    gh, gl = gg[:, :DK], gg[:, DK:]
+    qs[...] = halves(dot(u, two(state), 1, 0))
+    fs[...] = halves(dot(v, gg, 1, 0))
+    ghh = jnp.concatenate([gh, gh], axis=1)
+    both = jnp.sum(grad * state, axis=0, keepdims=True)
+    live = live_ref[0]
+    for p in range(NP):
+        a = 2 * p
+        alive = one((i + a * BLOCK) < live * BLOCK)
+        at = pl.ds(p * PAIR, PAIR)
+        query = query_i[p] + qin_i[p] * qs[at]
+        falling = fall_i[p] + kout_i[p] * fs[at]
+        rising = rise_i[p]
+        kf = kf_i[p]
+        value = value_i[p] + dot(kf, ghh, 1, 1) + dot(kf[:, :DK], gl, 1, 1)
+        q = rows_of(x, p, QC, DK).astype(F32)
+        k = rows_of(x, p, KC, DK).astype(F32)
+        pre, suf, decay, base = (small_i[p, r : r + 1] for r in range(4))
+        carry = base + decay * (
+            pre * jnp.sum(grad_i[p] * state, axis=0, keepdims=True)
+            + suf * jnp.sum(state_i[p] * grad, axis=0, keepdims=True)
+            + (pre * suf) * both
         )
-        rising = ks * (halves(dot(th, qq, 1, 0)) + dot(tl, qh, 1, 0))
-        falling = (ks * kout) * halves(dot(v, gg, 1, 0))
-        value = (
-            dot(two(st), jnp.concatenate([u, u], axis=0), 1, 0)
-            + dot(ff, jnp.concatenate([gh, gh], axis=1), 1, 1)
-            + dot(ff[:, :DK], gl, 1, 1)
-        )
-        query = query * SCALE
-        q = rows_of(x, p, QC, DK).astype(F32)
-        k = rows_of(x, p, KC, DK).astype(F32) * live
-        decay = ea * (keeps[b] * eb)
-        s32 = ss[:, :DK].astype(F32) + ss[:, DK:].astype(F32)
-        carry = jnp.sum(grad * s32, axis=0, keepdims=True) * decay
         terms = jnp.concatenate([*split(query * q - rising * k), *split(falling * k)], axis=0)
         gate = dot(sums, terms, 1, 0) + carry
         shape = lambda r: r.astype(BF).reshape(2, BLOCK, r.shape[1])
         out[a : a + 2, :, 0:DK] = shape(query)
-        out[a : a + 2, :, DK : 2 * DK] = shape((rising + falling) * live)
-        out[a : a + 2, :, 2 * DK : 3 * DK] = shape(gate * live)
+        out[a : a + 2, :, DK : 2 * DK] = shape(rising + falling)
+        out[a : a + 2, :, 2 * DK : 3 * DK] = shape(gate * alive)
         out[a : a + 2, :, 3 * DK :] = shape(value)
-        if p > 0:
-            qf = rows_of(x, p, QC, DK).astype(F32) * (qs * SCALE) * qin
-            grad = decay * grad + halves(dot(u, two(qf), 0, 0))
-
-
-def grads(live, doc, prev, pos, x, own, other):
+
+
+def finish(live, pos, x, own, other, parts):
     return pl.pallas_call(
-        grads_kernel,
+        finish_kernel,
         out_shape=jax.ShapeDtypeStruct((NB, BLOCK, OUT_W), BF),
-        in_specs=[sspec()] * 4 + [vspec()] * 3,
+        in_specs=[sspec()] * 2 + [vspec()] * 13,
         out_specs=vspec(),
-        scratch_shapes=[
-            VMEM((NP, DV, 2 * DK), BF),
-            VMEM((NP, PAIR, 2 * DK), BF),
-            VMEM((NP, PAIR, 2 * DK), BF),
-            VMEM((NP, PAIR, 2 * DK), BF),
-            VMEM((NP, PAIR, DK), F32),
-            VMEM((NP, PAIR, DK), F32),
-        ],
-        compiler_params=pltpu.CompilerParams(vmem_limit_bytes=40 * 1024 * 1024),
-        name="grads",
-    )(live, doc, prev, pos, x, own, other)
+        scratch_shapes=[VMEM((NB * BLOCK, DK), F32), VMEM((NB * BLOCK, DK), F32)],
+        compiler_params=pltpu.CompilerParams(vmem_limit_bytes=32 * 1024 * 1024),
+        name="finish",
+    )(live, pos, x, own, other, *parts)
 
 
 def per_device(queries, keys, values, out_grad, log_gates, live_blocks, block_doc):
@@ -325,8 +410,13 @@
     packed = pack(queries, keys, log_gates, values, out_grad)
     x = lax.all_to_all(packed, "head", split_axis=0, concat_axis=0, tiled=True)
     kept, sent = totals(live_blocks, block_doc, prev, pos, x)
-    own, other = window(kept, sent, index)
-    y = grads(live_blocks, block_doc, prev, pos, x, own, other)
+
+    def beside(chip):
+        y, _ = lax.optimization_barrier((x, chip))
+        return local(live_blocks, block_doc, prev, pos, y)
+
+    own, other, parts = window(kept, sent, index, beside)
+    y = finish(live_blocks, pos, x, own, other, parts)
     return unpack(lax.all_to_all(y, "head", split_axis=0, concat_axis=0, tiled=True))
 
 

time: 92.8 us -> 88.3 us (0.952)
  the two profiles are of different devices: /device:TPU:1 before, /device:TPU:32 now
where the time goes in v4:
time: 88.3 us; the launch traced here: 88.1 us
  waiting for transfers between devices  35.8 us (41%)
  blocking collectives  23.6 us (27%)
  starting transfers between devices  15.7 us (18%)
  Pallas kernels  11.3 us (13%)
  between operations  1.48 us (2%)
    all_to_all x1, waiting for transfers between devices, per_device(): x = lax.all_to_all(packed, 'head', split_axis=0, concat_axis=0, tiled=True)  24.1 us
    all_to_all x1, blocking collectives, per_device(): lax.all_to_all(y, 'head', split_axis=0, concat_axis=0, tiled=True)  23.6 us
    ppermute x3, starting transfers between devices, upstream(): lax.ppermute(x, 'ctx', [(i, (i + (2 * by if i % 2 == 0 else -2 * by)) % n...  8.36 us
    all_to_all x1, starting transfers between devices, per_device(): x = lax.all_to_all(packed, 'head', split_axis=0, concat_axis=0, tiled=True)  7.17 us
    ppermute x3, waiting for transfers between devices, upstream(): lax.ppermute(x, 'ctx', [(i, (i + (2 * by if i % 2 == 0 else -2 * by)) % n...  6.77 us
    pallas_call x1, Pallas kernels, local(): pl.pallas_call(local_kernel, out_shape=(t, t, t, f(PAIR, DV), t, t, jax.S...  4.86 us
    ppermute x2, waiting for transfers between devices, swapped(): return lax.ppermute(x, 'ctx', [(i, i ^ 1) for i in range(n)])  2.65 us
    pallas_call x1, Pallas kernels, pack(): pl.pallas_call(pack_kernel, grid=(PACK_STEPS,), out_shape=jax.ShapeDtypeS...  2.58 us
  transfers between devices with their start and end apart: 7, of which 5 were waited for; matrix products, arithmetic and copies ran while one was open for 0% of the time, Pallas kernels for 6%

profile of v4, /device:TPU:32, one launch (start us, length us, event | category | flops | bytes accessed | tf_op | source)
XLA Modules:
  0.0 88.1 jit_solution(1325762889553922162)
XLA Ops:
  0.6 2.6 %pack.1 = bf16[16,64,896]{2,1,0:T(8,128)(2,1)} custom-call(bf16[64,2048]{1,0:T(8,128)(2,1)} %q.1, bf16[64,2048]{1,0:T(8,128)(2,1)} %k.1, bf16[64,2048]{1,0:T(8,128)(2,1)} %g.1, bf16[64,4096]{1,0:T(8,128)(2,1)} %v.1, bf16[64,4096]{1,0:T(8,128)(2,1)} %u.1), custom_call_target="tpu_custom_call" | custom-call | tf_op jit(solution)/shard_map/pack/pallas_call | solution.py:87
  3.2 0.0 copy-start
  3.2 7.2 %all-to-all-start = ((bf16[16,64,896]{2,1,0:T(8,128)(2,1)}), bf16[16,64,896]{2,1,0:T(8,128)(2,1)S(1)}, u32[]{:S(2)}, u32[]{:S(2)}) async-start(bf16[16,64,896]{2,1,0:T(8,128)(2,1)} %pack.1), calls=%async_computation | async-start | bytes 3670016 | tf_op jit(solution)/shard_map/all_to_all | solution.py:411
  10.4 0.0 copy-done
  10.4 0.0 collective-permute-start
  11.1 2.3 %collective-permute-done.prev_ref = s32[16]{0:T(128)S(1)} collective-permute-done((s32[16]{0:T(128)S(1)}, s32[16]{0:T(128)S(1)}, u32[]{:S(2)}, u32[]{:S(2)}) %collective-permute-start) | collective-permute-done | bytes 96 | tf_op jit(solution)/shard_map/ppermute | solution.py:409
  13.4 24.1 %all-to-all-done.x = bf16[16,64,896]{2,1,0:T(8,128)(2,1)S(1)} async-done(((bf16[16,64,896]{2,1,0:T(8,128)(2,1)}), bf16[16,64,896]{2,1,0:T(8,128)(2,1)S(1)}, u32[]{:S(2)}, u32[]{:S(2)}) %all-to-all-start) | async-done | bytes 1835040 | tf_op jit(solution)/shard_map/all_to_all | solution.py:411
  37.4 1.4 %totals.1 = (f32[264,128]{1,0:T(8,128)S(1)}, f32[264,128]{1,0:T(8,128)S(1)}) custom-call(s32[1]{0:T(128)S(6)} %copy.11.live_ref, s32[16]{0:T(128)S(1)} %copy-done, s32[16]{0:T(128)S(1)} %collective-permute-done.prev_ref, s32[1]{0:T(128)} %bitcast.pos_ref, bf16[16,64,896]{2,1,0:T(8,128)(2,1)S(1)} %all-to-all-done.x), custom_call_target="tpu_custom_call" | custom-call | tf_op jit(solution)/shard_map/totals/pallas_call | solution.py:155
  38.9 0.1 collective-permute-start.1
  39.0 1.3 %collective-permute-done.1 = f32[264,128]{1,0:T(8,128)S(1)} collective-permute-done((f32[264,128]{1,0:T(8,128)S(1)}, f32[264,128]{1,0:T(8,128)S(1)}, u32[]{:S(2)}, u32[]{:S(2)}) %collective-permute-start.1) | collective-permute-done | bytes 135200 | tf_op jit(solution)/shard_map/ppermute | solution.py:178
  40.3 3.3 %collective-permute-start.3 = (f32[264,128]{1,0:T(8,128)S(1)}, f32[264,128]{1,0:T(8,128)S(1)}, u32[]{:S(2)}, u32[]{:S(2)}) collective-permute-start(f32[264,128]{1,0:T(8,128)S(1)} %pad_maximum_fusion), channel_id=1, source_target_pairs={{0,64},{16,208},{32,96},{48,240},{64,128},{80,16},{96,160},{112,48... | collective-permute-start | bytes 405512 | tf_op jit(solution)/shard_map/ppermute | solution.py:183
  43.7 3.1 %collective-permute-start.2 = (f32[264,128]{1,0:T(8,128)S(1)}, f32[264,128]{1,0:T(8,128)S(1)}, u32[]{:S(2)}, u32[]{:S(2)}) collective-permute-start(f32[264,128]{1,0:T(8,128)S(1)} %pad_maximum_fusion), channel_id=1, source_target_pairs={{0,32},{16,240},{32,64},{48,16},{64,96},{80,48},{96,128},{112,80},... | collective-permute-start | bytes 405512 | tf_op jit(solution)/shard_map/ppermute | solution.py:183
  46.8 4.9 %local.1 = (f32[8,128,128]{2,1,0:T(8,128)S(1)}, f32[8,128,128]{2,1,0:T(8,128)S(1)}, f32[8,128,128]{2,1,0:T(8,128)S(1)}, f32[8,128,256]{2,1,0:T(8,128)S(1)}, f32[...) custom-call(s32[1]{0:T(128)S(6)} %copy.11.live_ref, ...), custom_call_target="tpu_custom_call" | custom-call | flops 4000000000 | bytes 9000000 | tf_op jit(solution)/shard_map/local/pallas_call | solution.py:324
  51.7 0.0 collective-permute-done.3
  51.7 0.0 collective-permute-done.2
  51.8 1.9 %collective-permute-start.4 = (f32[264,128]{1,0:T(8,128)S(1)}, f32[264,128]{1,0:T(8,128)S(1)}, u32[]{:S(2)}, u32[]{:S(2)}) collective-permute-start(f32[264,128]{1,0:T(8,128)S(1)} %pad_maximum_fusion.1), channel_id=1, source_target_pairs={{0,64},{16,208},{32,96},{48,240},{64,128},{80,16},{96,160},{112,48... | collective-permute-start | bytes 405512 | tf_op jit(solution)/shard_map/ppermute | solution.py:183
  53.7 6.8 %collective-permute-done.4 = f32[264,128]{1,0:T(8,128)S(1)} collective-permute-done((f32[264,128]{1,0:T(8,128)S(1)}, f32[264,128]{1,0:T(8,128)S(1)}, u32[]{:S(2)}, u32[]{:S(2)}) %collective-permute-start.4) | collective-permute-done | bytes 135200 | tf_op jit(solution)/shard_map/ppermute | solution.py:183
  60.5 0.1 collective-permute-start.5
  60.7 1.3 %collective-permute-done.5.other = f32[264,128]{1,0:T(8,128)S(1)} collective-permute-done((f32[264,128]{1,0:T(8,128)S(1)}, f32[264,128]{1,0:T(8,128)S(1)}, u32[]{:S(2)}, u32[]{:S(2)}) %collective-permute-start.5) | collective-permute-done | bytes 135200 | tf_op jit(solution)/shard_map/ppermute | solution.py:178
  62.0 1.2 %finish.1 = bf16[16,64,640]{2,1,0:T(8,128)(2,1)S(1)} custom-call(s32[1]{0:T(128)S(6)} %copy.11.live_ref, s32[1]{0:T(128)} %bitcast.pos_ref, bf16[16,64,896]{2,1,0:T(8,128)(2,1)S(1)} %all-to-all-done.x, f32[264,128]{1,0:T(8,128)S(1)} %pad_maximum_fusion.2.own, f32[264,128]{1,0:T(8,128)S(1)} %collective-permute-done.5.other, ...), custom_call_target="tpu_custom_call" | custom-call | tf_op jit(solution)/shard_map/finish/pallas_call | solution.py:394
  63.2 23.6 %all_to_all.10.x = bf16[16,64,640]{2,1,0:T(8,128)(2,1)S(1)} all-to-all(bf16[16,64,640]{2,1,0:T(8,128)(2,1)S(1)} %finish.1), channel_id=1, replica_groups=mesh['ctx'=16,'head'=16] {'head'}, dimensions={0} | all-to-all | bytes 2621440 | tf_op jit(solution)/shard_map/all_to_all | solution.py:420
  86.8 1.3 %unpack.1 = (bf16[64,2048]{1,0:T(8,128)(2,1)}, bf16[64,2048]{1,0:T(8,128)(2,1)}, bf16[64,4096]{1,0:T(8,128)(2,1)}, bf16[64,2048]{1,0:T(8,128)(2,1)}) custom-call(bf16[16,64,640]{2,1,0:T(8,128)(2,1)S(1)} %all_to_all.10.x), custom_call_target="tpu_custom_call" | custom-call | tf_op jit(solution)/shard_map/unpack/pallas_call | solution.py:110
  (17 shorter events, 0.2 us)
Async XLA Ops:
  3.2 7.2 %copy-start = (s32[16]{0:T(128)S(1)}, s32[16]{0:T(128)}, u32[]{:S(2)}) copy-start(s32[16]{0:T(128)} %doc_ref.3) | copy-start | bytes 196
  3.2 34.2 %all-to-all-start = ((bf16[16,64,896]{2,1,0:T(8,128)(2,1)}), bf16[16,64,896]{2,1,0:T(8,128)(2,1)S(1)}, u32[]{:S(2)}, u32[]{:S(2)}) async-start(bf16[16,64,896]{2,1,0:T(8,128)(2,1)} %pack.1), calls=%async_computation | async-start | bytes 3670016 | tf_op jit(solution)/shard_map/all_to_all | solution.py:411
  10.4 3.0 %collective-permute-start = (s32[16]{0:T(128)S(1)}, s32[16]{0:T(128)S(1)}, u32[]{:S(2)}, u32[]{:S(2)}) collective-permute-start(s32[16]{0:T(128)S(1)} %copy-done), channel_id=1, source_target_pairs={{0,16},{16,32},{32,48},{48,64},{64,80},{80,96},{96,112},{112,128},... | collective-permute-start | bytes 200 | tf_op jit(solution)/shard_map/ppermute | solution.py:409
  38.9 1.4 %collective-permute-start.1 = (f32[264,128]{1,0:T(8,128)S(1)}, f32[264,128]{1,0:T(8,128)S(1)}, u32[]{:S(2)}, u32[]{:S(2)}) collective-permute-start(f32[264,128]{1,0:T(8,128)S(1)} %get-tuple-element.29), channel_id=1, source_target_pairs={{0,16},{16,0},{32,48},{48,32},{64,80},{80,64},{96,112},{112,96},{1... | collective-permute-start | bytes 405512 | tf_op jit(solution)/shard_map/ppermute | solution.py:178
  40.3 11.3 %collective-permute-start.3 = (f32[264,128]{1,0:T(8,128)S(1)}, f32[264,128]{1,0:T(8,128)S(1)}, u32[]{:S(2)}, u32[]{:S(2)}) collective-permute-start(f32[264,128]{1,0:T(8,128)S(1)} %pad_maximum_fusion), channel_id=1, source_target_pairs={{0,64},{16,208},{32,96},{48,240},{64,128},{80,16},{96,160},{112,48... | collective-permute-start | bytes 405512 | tf_op jit(solution)/shard_map/ppermute | solution.py:183
  43.7 8.0 %collective-permute-start.2 = (f32[264,128]{1,0:T(8,128)S(1)}, f32[264,128]{1,0:T(8,128)S(1)}, u32[]{:S(2)}, u32[]{:S(2)}) collective-permute-start(f32[264,128]{1,0:T(8,128)S(1)} %pad_maximum_fusion), channel_id=1, source_target_pairs={{0,32},{16,240},{32,64},{48,16},{64,96},{80,48},{96,128},{112,80},... | collective-permute-start | bytes 405512 | tf_op jit(solution)/shard_map/ppermute | solution.py:183
  51.8 8.6 %collective-permute-start.4 = (f32[264,128]{1,0:T(8,128)S(1)}, f32[264,128]{1,0:T(8,128)S(1)}, u32[]{:S(2)}, u32[]{:S(2)}) collective-permute-start(f32[264,128]{1,0:T(8,128)S(1)} %pad_maximum_fusion.1), channel_id=1, source_target_pairs={{0,64},{16,208},{32,96},{48,240},{64,128},{80,16},{96,160},{112,48... | collective-permute-start | bytes 405512 | tf_op jit(solution)/shard_map/ppermute | solution.py:183
  60.5 1.4 %collective-permute-start.5 = (f32[264,128]{1,0:T(8,128)S(1)}, f32[264,128]{1,0:T(8,128)S(1)}, u32[]{:S(2)}, u32[]{:S(2)}) collective-permute-start(f32[264,128]{1,0:T(8,128)S(1)} %pad_maximum_fusion.3), channel_id=1, source_target_pairs={{0,16},{16,0},{32,48},{48,32},{64,80},{80,64},{96,112},{112,96},{1... | collective-permute-start | bytes 405512 | tf_op jit(solution)/shard_map/ppermute | solution.py:178

commit v5 on v4

--- a/solution.py
+++ b/solution.py
@@ -20,15 +20,10 @@
 BF = jnp.bfloat16
 F32 = jnp.float32
 VMEM = pltpu.VMEM
-SMEM = pltpu.SMEM
 
 
 def vspec():
     return pl.BlockSpec(memory_space=VMEM)
-
-
-def sspec():
-    return pl.BlockSpec(memory_space=SMEM)
 
 
 def split(x):
@@ -45,25 +40,22 @@
     return r[:, :DK] + r[:, DK:]
 
 
-def triangle(lower, strict):
-    i = lax.broadcasted_iota(jnp.int32, (BLOCK, BLOCK), 0)
-    j = lax.broadcasted_iota(jnp.int32, (BLOCK, BLOCK), 1)
-    if lower:
-        return (j < i) if strict else (j <= i)
-    return j >= i
-
-
-def flags(live_ref, doc_ref, prev_ref, pos_ref):
-    live = live_ref[0]
-    first = pos_ref[0] == 0
-    lives, keeps = [], []
-    for b in range(NB):
-        lives.append(jnp.where(b < live, 1.0, 0.0).astype(F32))
-        same = (prev_ref[NB - 1] if b == 0 else doc_ref[b - 1]) == doc_ref[b]
-        if b == 0:
-            same = same & jnp.logical_not(first)
-        keeps.append(jnp.where(same, 1.0, 0.0).astype(F32))
-    return lives, keeps
+def flag_rows(live_blocks, block_doc, index):
+    n = lax.axis_size("ctx")
+    before = lax.ppermute(block_doc, "ctx", [(i, (i + 1) % n) for i in range(n)])
+    place = jnp.arange(NB)
+    live = place < live_blocks[0]
+    previous = jnp.concatenate([before[NB - 1 :], block_doc[: NB - 1]])
+    keep = (previous == block_doc) & ((place > 0) | (index > 0))
+    even = jnp.full((8,), index % 2 == 0)
+    rows = jnp.concatenate([live, keep, even]).astype(F32)
+    return jnp.broadcast_to(rows[:, None], (2 * NB + 8, DV))
+
+
+def flags(flag):
+    row = lambda r: flag[r : r + 1, :DK]
+    lives, keeps = [row(b) for b in range(NB)], [row(NB + b) for b in range(NB)]
+    return lives, keeps, row(2 * NB) > 0.0
 
 
 PACK_STEPS = 2
@@ -117,54 +109,80 @@
     )(x)
 
 
-def totals_kernel(live_ref, doc_ref, prev_ref, pos_ref, x, kept, sent, kw, qw, cs):
-    lives, keeps = flags(live_ref, doc_ref, prev_ref, pos_ref)
-    tri = jnp.where(triangle(True, False), 1.0, 0.0).astype(BF)
-    for b in range(NB):
-        cs[b] = dot(tri, x[b, :, GC : GC + DK], 1, 0) * lives[b]
-    suffix = jnp.ones((1, DK), F32)
-    for b in reversed(range(NB)):
-        c = cs[b]
-        last = c[BLOCK - 1 : BLOCK, :]
-        kf = x[b, :, KC : KC + DK].astype(F32) * (jnp.exp(last - c) * (suffix * lives[b]))
-        kw[b, :, :DK], kw[b, :, DK:] = split(kf)
-        suffix = suffix * (keeps[b] * jnp.exp(last))
-    prefix = jnp.ones((1, DK), F32)
-    for b in range(NB):
-        c = cs[b]
-        last = c[BLOCK - 1 : BLOCK, :]
-        qt = x[b, :, QC : QC + DK].astype(F32) * (
-            jnp.exp(c) * (prefix * (keeps[b] * lives[b] * SCALE))
-        )
-        qw[b, :, :DK], qw[b, :, DK:] = split(qt)
-        prefix = prefix * (keeps[b] * jnp.exp(last))
+PAIR = 2 * BLOCK
+NP = NB // 2
+
+
+def rows_of(x, p, col, width):
+    return x[2 * p : 2 * p + 2, :, col : col + width].reshape(PAIR, width)
+
+
+def two(x):
+    return jnp.concatenate(split(x), axis=1)
+
+
+def one(mask):
+    return jnp.where(mask, 1.0, 0.0).astype(F32)
+
+
+def pair_masks():
+    i = lax.broadcasted_iota(jnp.int32, (PAIR, PAIR), 0)
+    j = lax.broadcasted_iota(jnp.int32, (PAIR, PAIR), 1)
+    first = i < BLOCK
+    return i, j, first, first == (j < BLOCK)
+
+
+def totals_kernel(flag, x, kept, sent, kw, qw, cs):
+    lives, keeps, even = flags(flag)
+    i, j, first, same = pair_masks()
+    tri = one((j <= i) & same).astype(BF)
+    decay = jnp.ones((1, DK), F32)
+    for p in range(NP):
+        a, b = 2 * p, 2 * p + 1
+        c = dot(tri, rows_of(x, p, GC, DK), 1, 0) * jnp.where(first, lives[a], lives[b])
+        cs[p] = c
+        earlier = decay * keeps[a]
+        middle = earlier * (keeps[b] * jnp.exp(c[BLOCK - 1 : BLOCK]))
+        decay = middle * jnp.exp(c[PAIR - 1 : PAIR])
+        q = rows_of(x, p, QC, DK).astype(F32)
+        scale = jnp.where(first, earlier * (lives[a] * SCALE), middle * (lives[b] * SCALE))
+        qw[p] = two(q * (jnp.exp(c) * scale))
     rows = NB * BLOCK
+    u = x[:, :, UC : UC + DV].reshape(rows, DV)
+    bwd = halves(dot(u, qw[...].reshape(rows, 2 * DK), 0, 0))
+    later = jnp.ones((1, DK), F32)
+    for p in reversed(range(NP)):
+        a, b = 2 * p, 2 * p + 1
+        c = cs[p]
+        ca, cb = c[BLOCK - 1 : BLOCK], c[PAIR - 1 : PAIR]
+        middle = later * (keeps[b] * jnp.exp(cb))
+        k = rows_of(x, p, KC, DK).astype(F32)
+        fade = jnp.exp(jnp.where(first, ca, cb) - c)
+        kw[p] = two(k * (fade * jnp.where(first, middle * lives[a], later * lives[b])))
+        later = middle * (keeps[a] * jnp.exp(ca))
     v = x[:, :, VC : VC + DV].reshape(rows, DV)
-    u = x[:, :, UC : UC + DV].reshape(rows, DV)
     fwd = halves(dot(v, kw[...].reshape(rows, 2 * DK), 0, 0))
-    bwd = halves(dot(u, qw[...].reshape(rows, 2 * DK), 0, 0))
-    even = lax.rem(pos_ref[0], 2) == 0
     kept[:DV] = jnp.where(even, fwd, bwd)
     sent[:DV] = jnp.where(even, bwd, fwd)
-    kept[DV:] = jnp.broadcast_to(prefix, (MSG - DV, DK))
-    sent[DV:] = jnp.broadcast_to(prefix, (MSG - DV, DK))
-
-
-def totals(live, doc, prev, pos, x):
+    kept[DV:] = jnp.broadcast_to(decay, (MSG - DV, DK))
+    sent[DV:] = jnp.broadcast_to(decay, (MSG - DV, DK))
+
+
+def totals(flag, x):
     msg = jax.ShapeDtypeStruct((MSG, DK), F32)
     return pl.pallas_call(
         totals_kernel,
         out_shape=(msg, msg),
-        in_specs=[sspec()] * 4 + [vspec()],
+        in_specs=[vspec()] * 2,
         out_specs=(vspec(),) * 2,
         scratch_shapes=[
-            VMEM((NB, BLOCK, 2 * DK), BF),
-            VMEM((NB, BLOCK, 2 * DK), BF),
-            VMEM((NB, BLOCK, DK), F32),
+            VMEM((NP, PAIR, 2 * DK), BF),
+            VMEM((NP, PAIR, 2 * DK), BF),
+            VMEM((NP, PAIR, DK), F32),
         ],
-        compiler_params=pltpu.CompilerParams(vmem_limit_bytes=40 * 1024 * 1024),
+        compiler_params=pltpu.CompilerParams(vmem_limit_bytes=32 * 1024 * 1024),
         name="totals",
-    )(live, doc, prev, pos, x)
+    )(flag, x)
 
 
 def joined(near, far):
@@ -198,41 +216,19 @@
     return e, swapped(joined(kept, e)), done
 
 
-PAIR = 2 * BLOCK
-NP = NB // 2
-
-
-def rows_of(x, p, col, width):
-    return x[2 * p : 2 * p + 2, :, col : col + width].reshape(PAIR, width)
-
-
-def two(x):
-    return jnp.concatenate(split(x), axis=1)
-
-
-def one(mask):
-    return jnp.where(mask, 1.0, 0.0).astype(F32)
-
-
-def pair_masks():
-    i = lax.broadcasted_iota(jnp.int32, (PAIR, PAIR), 0)
-    j = lax.broadcasted_iota(jnp.int32, (PAIR, PAIR), 1)
-    first = i < BLOCK
-    return i, j, first, first == (j < BLOCK)
-
-
 def local_kernel(
-    live_ref, doc_ref, prev_ref, pos_ref, x,
+    flag, x,
     query_o, rise_o, fall_o, value_o, qin_o, kout_o, kf_o, state_o, grad_o, small_o,
     qw, kw, fw, qsw, ksw,
 ):
-    lives, keeps = flags(live_ref, doc_ref, prev_ref, pos_ref)
+    lives, keeps, _ = flags(flag)
     i, j, first, same = pair_masks()
     cross = jnp.logical_not(same)
     tri = one((j <= i) & same).astype(BF)
     low_same, low_cross = one((j <= i) & same), one((j < i) & cross)
     up_same, up_cross = one((j >= i) & same), one((j > i) & cross)
     first_v = lax.broadcasted_iota(jnp.int32, (PAIR, DV), 0) < BLOCK
+    wide = [flag[b : b + 1, :].astype(BF) for b in range(NB)]
 
     ends = []
     prefix = jnp.ones((1, DK), F32)
@@ -274,7 +270,7 @@
         qh, ql, kh = qq[:, :DK], qq[:, DK:], kk[:, :DK]
         qs, ks = qsw[p], ksw[p]
         v = rows_of(x, p, VC, DV)
-        u = rows_of(x, p, UC, DV) * jnp.where(first_v, lives[a], lives[b]).astype(BF)
+        u = rows_of(x, p, UC, DV) * jnp.where(first_v, wide[a], wide[b])
         st = dot(kk, jnp.concatenate([qh, qh], axis=1), 1, 1) + dot(kh, ql, 1, 1)
         up = up_same + keeps[b] * up_cross
         st = jnp.where(up > 0.0, st, 0.0)
@@ -318,7 +314,7 @@
             grad = update if p == NP - 1 else decay * grad + update
 
 
-def local(live, doc, prev, pos, x):
+def local(flag, x):
     f = lambda *s: jax.ShapeDtypeStruct((NP,) + s, F32)
     t = f(PAIR, DK)
     return pl.pallas_call(
@@ -328,7 +324,7 @@
             jax.ShapeDtypeStruct((NP, PAIR, 2 * DK), BF),
             f(DV, DK), f(DV, DK), f(8, DK),
         ),
-        in_specs=[sspec()] * 4 + [vspec()],
+        in_specs=[vspec()] * 2,
         out_specs=(vspec(),) * 10,
         scratch_shapes=[
             VMEM((NP, PAIR, 2 * DK), BF),
@@ -340,18 +336,18 @@
         compiler_params=pltpu.CompilerParams(vmem_limit_bytes=32 * 1024 * 1024),
         cost_estimate=pl.CostEstimate(flops=4 * 10**9, bytes_accessed=9 * 10**6, transcendentals=10**6),
         name="local",
-    )(live, doc, prev, pos, x)
+    )(flag, x)
 
 
 def finish_kernel(
-    live_ref, pos_ref, x, own, other,
+    flag, x, own, other,
     query_i, rise_i, fall_i, value_i, qin_i, kout_i, kf_i, state_i, grad_i, small_i,
     out, qs, fs,
 ):
     i, j, first, _ = pair_masks()
     upper, strict = one(j >= i).astype(BF), one(j < i).astype(BF)
     sums = jnp.concatenate([upper, upper, strict, strict], axis=1)
-    even = lax.rem(pos_ref[0], 2) == 0
+    lives, _, even = flags(flag)
     state = jnp.where(even, own[:DV], other[:DV])
     grad = jnp.where(even, other[:DV], own[:DV])
     rows = NB * BLOCK
@@ -363,10 +359,9 @@
     fs[...] = halves(dot(v, gg, 1, 0))
     ghh = jnp.concatenate([gh, gh], axis=1)
     both = jnp.sum(grad * state, axis=0, keepdims=True)
-    live = live_ref[0]
     for p in range(NP):
         a = 2 * p
-        alive = one((i + a * BLOCK) < live * BLOCK)
+        alive = jnp.where(first, lives[a], lives[a + 1])
         at = pl.ds(p * PAIR, PAIR)
         query = query_i[p] + qin_i[p] * qs[at]
         falling = fall_i[p] + kout_i[p] * fs[at]
@@ -390,33 +385,31 @@
         out[a : a + 2, :, 3 * DK :] = shape(value)
 
 
-def finish(live, pos, x, own, other, parts):
+def finish(flag, x, own, other, parts):
     return pl.pallas_call(
         finish_kernel,
         out_shape=jax.ShapeDtypeStruct((NB, BLOCK, OUT_W), BF),
-        in_specs=[sspec()] * 2 + [vspec()] * 13,
+        in_specs=[vspec()] * 14,
         out_specs=vspec(),
         scratch_shapes=[VMEM((NB * BLOCK, DK), F32), VMEM((NB * BLOCK, DK), F32)],
         compiler_params=pltpu.CompilerParams(vmem_limit_bytes=32 * 1024 * 1024),
         name="finish",
-    )(live, pos, x, own, other, *parts)
+    )(flag, x, own, other, *parts)
 
 
 def per_device(queries, keys, values, out_grad, log_gates, live_blocks, block_doc):
-    n = lax.axis_size("ctx")
     index = lax.axis_index("ctx")
-    pos = index.reshape(1)
-    prev = lax.ppermute(block_doc, "ctx", [(i, (i + 1) % n) for i in range(n)])
+    flag = flag_rows(live_blocks, block_doc, index)
     packed = pack(queries, keys, log_gates, values, out_grad)
     x = lax.all_to_all(packed, "head", split_axis=0, concat_axis=0, tiled=True)
-    kept, sent = totals(live_blocks, block_doc, prev, pos, x)
+    kept, sent = totals(flag, x)
 
     def beside(chip):
         y, _ = lax.optimization_barrier((x, chip))
-        return local(live_blocks, block_doc, prev, pos, y)
+        return local(flag, y)
 
     own, other, parts = window(kept, sent, index, beside)
-    y = finish(live_blocks, pos, x, own, other, parts)
+    y = finish(flag, x, own, other, parts)
     return unpack(lax.all_to_all(y, "head", split_axis=0, concat_axis=0, tiled=True))
 
 

time: 88.3 us -> 87.8 us (level)
  the two profiles are of different devices: /device:TPU:32 before, /device:TPU:1 now
where the time goes in v5:
time: 87.8 us; the launch traced here: 87.6 us
  starting transfers between devices  26.5 us (30%)
  waiting for transfers between devices  25.4 us (29%)
  blocking collectives  22.2 us (25%)
  Pallas kernels  10.3 us (12%)
  between operations  1.43 us (2%)
  other arithmetic  0.99 us (1%)
    all_to_all x1, blocking collectives, per_device(): lax.all_to_all(y, 'head', split_axis=0, concat_axis=0, tiled=True)  22.2 us
    all_to_all x1, waiting for transfers between devices, per_device(): x = lax.all_to_all(packed, 'head', split_axis=0, concat_axis=0, tiled=True)  19.2 us
    ppermute x3, starting transfers between devices, upstream(): lax.ppermute(x, 'ctx', [(i, (i + (2 * by if i % 2 == 0 else -2 * by)) % n...  9.24 us
    all_to_all x1, starting transfers between devices, per_device(): x = lax.all_to_all(packed, 'head', split_axis=0, concat_axis=0, tiled=True)  7.72 us
    ppermute x2, starting transfers between devices, swapped(): return lax.ppermute(x, 'ctx', [(i, i ^ 1) for i in range(n)])  7.09 us
    pallas_call x1, Pallas kernels, local(): pl.pallas_call(local_kernel, out_shape=(t, t, t, f(PAIR, DV), t, t, jax.S...  4.34 us
    ppermute x3, waiting for transfers between devices, upstream(): lax.ppermute(x, 'ctx', [(i, (i + (2 * by if i % 2 == 0 else -2 * by)) % n...  4.17 us
    pallas_call x1, Pallas kernels, pack(): pl.pallas_call(pack_kernel, grid=(PACK_STEPS,), out_shape=jax.ShapeDtypeS...  2.58 us
  transfers between devices with their start and end apart: 7, of which 5 were waited for; matrix products, arithmetic and copies ran while one was open for 2% of the time, Pallas kernels for 5%

profile of v5, /device:TPU:1, one launch (start us, length us, event | category | flops | bytes accessed | tf_op | source)
XLA Modules:
  0.0 87.6 jit_solution(7261641331558606194)
XLA Ops:
  0.6 2.6 %pack.1 = bf16[16,64,896]{2,1,0:T(8,128)(2,1)} custom-call(bf16[64,2048]{1,0:T(8,128)(2,1)} %q.1, bf16[64,2048]{1,0:T(8,128)(2,1)} %k.1, bf16[64,2048]{1,0:T(8,128)(2,1)} %g.1, bf16[64,4096]{1,0:T(8,128)(2,1)} %v.1, bf16[64,4096]{1,0:T(8,128)(2,1)} %u.1), custom_call_target="tpu_custom_call" | custom-call | tf_op jit(solution)/shard_map/pack/pallas_call | solution.py:79
  3.2 0.0 copy-start
  3.2 7.7 %all-to-all-start = ((bf16[16,64,896]{2,1,0:T(8,128)(2,1)}), bf16[16,64,896]{2,1,0:T(8,128)(2,1)S(1)}, u32[]{:S(2)}, u32[]{:S(2)}) async-start(bf16[16,64,896]{2,1,0:T(8,128)(2,1)} %pack.1), calls=%async_computation | async-start | bytes 3670016 | tf_op jit(solution)/shard_map/all_to_all | solution.py:404
  10.9 0.0 copy-done
  10.9 2.5 %collective-permute-start = (s32[16]{0:T(128)S(1)}, s32[16]{0:T(128)S(1)}, u32[]{:S(2)}, u32[]{:S(2)}) collective-permute-start(s32[16]{0:T(128)S(1)} %copy-done), channel_id=1, source_target_pairs={{0,16},{16,32},{32,48},{48,64},{64,80},{80,96},{96,112},{112,128},... | collective-permute-start | bytes 200 | tf_op jit(solution)/shard_map/ppermute | solution.py:45
  14.1 0.1 collective-permute-done
  14.2 0.6 slice.50
  14.7 0.7 or_and_fusion
  15.5 0.1 add_convert_fusion
  15.6 19.2 %all-to-all-done.x = bf16[16,64,896]{2,1,0:T(8,128)(2,1)S(1)} async-done(((bf16[16,64,896]{2,1,0:T(8,128)(2,1)}), bf16[16,64,896]{2,1,0:T(8,128)(2,1)S(1)}, u32[]{:S(2)}, u32[]{:S(2)}) %all-to-all-start) | async-done | bytes 1835040 | tf_op jit(solution)/shard_map/all_to_all | solution.py:404
  34.8 0.1 broadcast_in_dim.16.flag
  34.9 0.7 totals.1
  35.6 4.2 %collective-permute-start.1 = (f32[264,128]{1,0:T(8,128)S(1)}, f32[264,128]{1,0:T(8,128)S(1)}, u32[]{:S(2)}, u32[]{:S(2)}) collective-permute-start(f32[264,128]{1,0:T(8,128)S(1)} %get-tuple-element.29), channel_id=1, source_target_pairs={{0,16},{16,0},{32,48},{48,32},{64,80},{80,64},{96,112},{112,96},{1... | collective-permute-start | bytes 405512 | tf_op jit(solution)/shard_map/ppermute | solution.py:196
  39.8 1.0 %collective-permute-done.1 = f32[264,128]{1,0:T(8,128)S(1)} collective-permute-done((f32[264,128]{1,0:T(8,128)S(1)}, f32[264,128]{1,0:T(8,128)S(1)}, u32[]{:S(2)}, u32[]{:S(2)}) %collective-permute-start.1) | collective-permute-done | bytes 135200 | tf_op jit(solution)/shard_map/ppermute | solution.py:196
  40.9 6.1 %collective-permute-start.3 = (f32[264,128]{1,0:T(8,128)S(1)}, f32[264,128]{1,0:T(8,128)S(1)}, u32[]{:S(2)}, u32[]{:S(2)}) collective-permute-start(f32[264,128]{1,0:T(8,128)S(1)} %pad_maximum_fusion), channel_id=1, source_target_pairs={{0,64},{16,208},{32,96},{48,240},{64,128},{80,16},{96,160},{112,48... | collective-permute-start | bytes 405512 | tf_op jit(solution)/shard_map/ppermute | solution.py:201
  47.0 0.7 collective-permute-start.2
  47.7 4.3 %local.1 = (f32[8,128,128]{2,1,0:T(8,128)S(1)}, f32[8,128,128]{2,1,0:T(8,128)S(1)}, f32[8,128,128]{2,1,0:T(8,128)S(1)}, f32[8,128,256]{2,1,0:T(8,128)S(1)}, f32[...) custom-call(f32[40,256]{1,0:T(8,128)S(1)} %broadcast_in_dim.16.flag,, ...), custom_call_target="tpu_custom_call" | custom-call | flops 4000000000 | bytes 9000000 | tf_op jit(solution)/shard_map/local/pallas_call | solution.py:320
  52.1 0.0 collective-permute-done.3
  52.1 0.0 collective-permute-done.2
  52.2 2.4 %collective-permute-start.4 = (f32[264,128]{1,0:T(8,128)S(1)}, f32[264,128]{1,0:T(8,128)S(1)}, u32[]{:S(2)}, u32[]{:S(2)}) collective-permute-start(f32[264,128]{1,0:T(8,128)S(1)} %pad_maximum_fusion.1), channel_id=1, source_target_pairs={{0,64},{16,208},{32,96},{48,240},{64,128},{80,16},{96,160},{112,48... | collective-permute-start | bytes 405512 | tf_op jit(solution)/shard_map/ppermute | solution.py:201
  54.6 4.2 %collective-permute-done.4 = f32[264,128]{1,0:T(8,128)S(1)} collective-permute-done((f32[264,128]{1,0:T(8,128)S(1)}, f32[264,128]{1,0:T(8,128)S(1)}, u32[]{:S(2)}, u32[]{:S(2)}) %collective-permute-start.4) | collective-permute-done | bytes 135200 | tf_op jit(solution)/shard_map/ppermute | solution.py:201
  58.9 2.8 %collective-permute-start.5 = (f32[264,128]{1,0:T(8,128)S(1)}, f32[264,128]{1,0:T(8,128)S(1)}, u32[]{:S(2)}, u32[]{:S(2)}) collective-permute-start(f32[264,128]{1,0:T(8,128)S(1)} %pad_maximum_fusion.3), channel_id=1, source_target_pairs={{0,16},{16,0},{32,48},{48,32},{64,80},{80,64},{96,112},{112,96},{1... | collective-permute-start | bytes 405512 | tf_op jit(solution)/shard_map/ppermute | solution.py:196
  61.7 1.0 %collective-permute-done.5.other = f32[264,128]{1,0:T(8,128)S(1)} collective-permute-done((f32[264,128]{1,0:T(8,128)S(1)}, f32[264,128]{1,0:T(8,128)S(1)}, u32[]{:S(2)}, u32[]{:S(2)}) %collective-permute-start.5) | collective-permute-done | bytes 135200 | tf_op jit(solution)/shard_map/ppermute | solution.py:196
  62.7 1.4 %finish.1 = bf16[16,64,640]{2,1,0:T(8,128)(2,1)S(1)} custom-call(f32[40,256]{1,0:T(8,128)S(1)} %broadcast_in_dim.16.flag, bf16[16,64,896]{2,1,0:T(8,128)(2,1)S(1)} %all-to-all-done.x, f32[264,128]{1,0:T(8,128)S(1)} %pad_maximum_fusion.2.own, f32[264,128]{1,0:T(8,128)S(1)} %collective-permute-done.5.other, f32[8,128,128]{2,1,0:T(8,128)S(1)} %get-tuple-element.44.query_i, ...), custom_call_target="tpu_custom_call" | custom-call | tf_op jit(solution)/shard_map/finish/pallas_call | solution.py:389
  64.1 22.2 %all_to_all.10.x = bf16[16,64,640]{2,1,0:T(8,128)(2,1)S(1)} all-to-all(bf16[16,64,640]{2,1,0:T(8,128)(2,1)S(1)} %finish.1), channel_id=1, replica_groups=mesh['ctx'=16,'head'=16] {'head'}, dimensions={0} | all-to-all | bytes 2621440 | tf_op jit(solution)/shard_map/all_to_all | solution.py:413
  86.3 1.3 %unpack.1 = (bf16[64,2048]{1,0:T(8,128)(2,1)}, bf16[64,2048]{1,0:T(8,128)(2,1)}, bf16[64,4096]{1,0:T(8,128)(2,1)}, bf16[64,2048]{1,0:T(8,128)(2,1)}) custom-call(bf16[16,64,640]{2,1,0:T(8,128)(2,1)S(1)} %all_to_all.10.x), custom_call_target="tpu_custom_call" | custom-call | tf_op jit(solution)/shard_map/unpack/pallas_call | solution.py:102
  (19 shorter events, 0.2 us)
Async XLA Ops:
  3.2 7.7 %copy-start = (s32[16]{0:T(128)S(1)}, s32[16]{0:T(128)}, u32[]{:S(2)}) copy-start(s32[16]{0:T(128)} %param.13) | copy-start | bytes 196
  3.2 31.6 %all-to-all-start = ((bf16[16,64,896]{2,1,0:T(8,128)(2,1)}), bf16[16,64,896]{2,1,0:T(8,128)(2,1)S(1)}, u32[]{:S(2)}, u32[]{:S(2)}) async-start(bf16[16,64,896]{2,1,0:T(8,128)(2,1)} %pack.1), calls=%async_computation | async-start | bytes 3670016 | tf_op jit(solution)/shard_map/all_to_all | solution.py:404
  10.9 3.2 %collective-permute-start = (s32[16]{0:T(128)S(1)}, s32[16]{0:T(128)S(1)}, u32[]{:S(2)}, u32[]{:S(2)}) collective-permute-start(s32[16]{0:T(128)S(1)} %copy-done), channel_id=1, source_target_pairs={{0,16},{16,32},{32,48},{48,64},{64,80},{80,96},{96,112},{112,128},... | collective-permute-start | bytes 200 | tf_op jit(solution)/shard_map/ppermute | solution.py:45
  35.6 5.2 %collective-permute-start.1 = (f32[264,128]{1,0:T(8,128)S(1)}, f32[264,128]{1,0:T(8,128)S(1)}, u32[]{:S(2)}, u32[]{:S(2)}) collective-permute-start(f32[264,128]{1,0:T(8,128)S(1)} %get-tuple-element.29), channel_id=1, source_target_pairs={{0,16},{16,0},{32,48},{48,32},{64,80},{80,64},{96,112},{112,96},{1... | collective-permute-start | bytes 405512 | tf_op jit(solution)/shard_map/ppermute | solution.py:196
  40.9 11.2 %collective-permute-start.3 = (f32[264,128]{1,0:T(8,128)S(1)}, f32[264,128]{1,0:T(8,128)S(1)}, u32[]{:S(2)}, u32[]{:S(2)}) collective-permute-start(f32[264,128]{1,0:T(8,128)S(1)} %pad_maximum_fusion), channel_id=1, source_target_pairs={{0,64},{16,208},{32,96},{48,240},{64,128},{80,16},{96,160},{112,48... | collective-permute-start | bytes 405512 | tf_op jit(solution)/shard_map/ppermute | solution.py:201
  47.0 5.1 %collective-permute-start.2 = (f32[264,128]{1,0:T(8,128)S(1)}, f32[264,128]{1,0:T(8,128)S(1)}, u32[]{:S(2)}, u32[]{:S(2)}) collective-permute-start(f32[264,128]{1,0:T(8,128)S(1)} %pad_maximum_fusion), channel_id=1, source_target_pairs={{0,32},{16,240},{32,64},{48,16},{64,96},{80,48},{96,128},{112,80},... | collective-permute-start | bytes 405512 | tf_op jit(solution)/shard_map/ppermute | solution.py:201
  52.2 6.6 %collective-permute-start.4 = (f32[264,128]{1,0:T(8,128)S(1)}, f32[264,128]{1,0:T(8,128)S(1)}, u32[]{:S(2)}, u32[]{:S(2)}) collective-permute-start(f32[264,128]{1,0:T(8,128)S(1)} %pad_maximum_fusion.1), channel_id=1, source_target_pairs={{0,64},{16,208},{32,96},{48,240},{64,128},{80,16},{96,160},{112,48... | collective-permute-start | bytes 405512 | tf_op jit(solution)/shard_map/ppermute | solution.py:201
  58.9 3.8 %collective-permute-start.5 = (f32[264,128]{1,0:T(8,128)S(1)}, f32[264,128]{1,0:T(8,128)S(1)}, u32[]{:S(2)}, u32[]{:S(2)}) collective-permute-start(f32[264,128]{1,0:T(8,128)S(1)} %pad_maximum_fusion.3), channel_id=1, source_target_pairs={{0,16},{16,0},{32,48},{48,32},{64,80},{80,64},{96,112},{112,96},{1... | collective-permute-start | bytes 405512 | tf_op jit(solution)/shard_map/ppermute | solution.py:196

commit v6 on v5

--- a/solution.py
+++ b/solution.py
@@ -198,9 +198,9 @@
 
 def upstream(x, index, by):
     n = lax.axis_size("ctx")
-    moved = lax.ppermute(
-        x, "ctx", [(i, (i + (2 * by if i % 2 == 0 else -2 * by)) % n) for i in range(n)]
-    )
+    target = lambda i: i + (2 * by if i % 2 == 0 else -2 * by)
+    pairs = [(i, target(i) if 0 <= target(i) < n else i ^ 1) for i in range(n)]
+    moved = lax.ppermute(x, "ctx", pairs)
     source = jnp.where(index % 2 == 0, index - 2 * by, index + 2 * by)
     return jnp.where((source >= 0) & (source < n), moved, 0.0)
 

time: 87.8 us -> 85.8 us (0.977)
  the two profiles are of different devices: /device:TPU:1 before, /device:TPU:32 now
where the time goes in v6:
time: 85.8 us; the launch traced here: 84.5 us
  waiting for transfers between devices  31.1 us (36%)
  blocking collectives  23.6 us (28%)
  starting transfers between devices  16.2 us (19%)
  Pallas kernels  10.3 us (12%)
  between operations  1.49 us (2%)
  other arithmetic  0.99 us (1%)
    all_to_all x1, blocking collectives, per_device(): lax.all_to_all(y, 'head', split_axis=0, concat_axis=0, tiled=True)  23.6 us
    all_to_all x1, waiting for transfers between devices, per_device(): x = lax.all_to_all(packed, 'head', split_axis=0, concat_axis=0, tiled=True)  22.7 us
    ppermute x3, starting transfers between devices, upstream(): moved = lax.ppermute(x, 'ctx', pairs)  8.88 us
    all_to_all x1, starting transfers between devices, per_device(): x = lax.all_to_all(packed, 'head', split_axis=0, concat_axis=0, tiled=True)  7.17 us
    pallas_call x1, Pallas kernels, local(): pl.pallas_call(local_kernel, out_shape=(t, t, t, f(PAIR, DV), t, t, jax.S...  4.34 us
    ppermute x3, waiting for transfers between devices, upstream(): moved = lax.ppermute(x, 'ctx', pairs)  3.57 us
    ppermute x2, waiting for transfers between devices, swapped(): return lax.ppermute(x, 'ctx', [(i, i ^ 1) for i in range(n)])  2.65 us
    pallas_call x1, Pallas kernels, pack(): pl.pallas_call(pack_kernel, grid=(PACK_STEPS,), out_shape=jax.ShapeDtypeS...  2.58 us
  transfers between devices with their start and end apart: 7, of which 5 were waited for; matrix products, arithmetic and copies ran while one was open for 2% of the time, Pallas kernels for 5%

profile of v6, /device:TPU:32, one launch (start us, length us, event | category | flops | bytes accessed | tf_op | source)
XLA Modules:
  0.0 84.5 jit_solution(5842404980374908736)
XLA Ops:
  0.6 2.6 %pack.1 = bf16[16,64,896]{2,1,0:T(8,128)(2,1)} custom-call(bf16[64,2048]{1,0:T(8,128)(2,1)} %q.1, bf16[64,2048]{1,0:T(8,128)(2,1)} %k.1, bf16[64,2048]{1,0:T(8,128)(2,1)} %g.1, bf16[64,4096]{1,0:T(8,128)(2,1)} %v.1, bf16[64,4096]{1,0:T(8,128)(2,1)} %u.1), custom_call_target="tpu_custom_call" | custom-call | tf_op jit(solution)/shard_map/pack/pallas_call | solution.py:79
  3.2 0.0 copy-start
  3.2 7.2 %all-to-all-start = ((bf16[16,64,896]{2,1,0:T(8,128)(2,1)}), bf16[16,64,896]{2,1,0:T(8,128)(2,1)S(1)}, u32[]{:S(2)}, u32[]{:S(2)}) async-start(bf16[16,64,896]{2,1,0:T(8,128)(2,1)} %pack.1), calls=%async_computation | async-start | bytes 3670016 | tf_op jit(solution)/shard_map/all_to_all | solution.py:404
  10.4 0.0 copy-done
  10.4 0.0 collective-permute-start
  11.1 2.3 %collective-permute-done = s32[16]{0:T(128)S(1)} collective-permute-done((s32[16]{0:T(128)S(1)}, s32[16]{0:T(128)S(1)}, u32[]{:S(2)}, u32[]{:S(2)}) %collective-permute-start) | collective-permute-done | bytes 96 | tf_op jit(solution)/shard_map/ppermute | solution.py:45
  13.4 0.6 slice.50
  14.0 0.7 or_and_fusion
  14.7 0.1 add_convert_fusion
  14.8 22.7 %all-to-all-done.x = bf16[16,64,896]{2,1,0:T(8,128)(2,1)S(1)} async-done(((bf16[16,64,896]{2,1,0:T(8,128)(2,1)}), bf16[16,64,896]{2,1,0:T(8,128)(2,1)S(1)}, u32[]{:S(2)}, u32[]{:S(2)}) %all-to-all-start) | async-done | bytes 1835040 | tf_op jit(solution)/shard_map/all_to_all | solution.py:404
  37.4 0.1 broadcast_in_dim.16.flag
  37.5 0.7 totals.1
  38.3 0.1 collective-permute-start.1
  38.4 1.3 %collective-permute-done.1 = f32[264,128]{1,0:T(8,128)S(1)} collective-permute-done((f32[264,128]{1,0:T(8,128)S(1)}, f32[264,128]{1,0:T(8,128)S(1)}, u32[]{:S(2)}, u32[]{:S(2)}) %collective-permute-start.1) | collective-permute-done | bytes 135200 | tf_op jit(solution)/shard_map/ppermute | solution.py:196
  39.7 3.4 %collective-permute-start.3 = (f32[264,128]{1,0:T(8,128)S(1)}, f32[264,128]{1,0:T(8,128)S(1)}, u32[]{:S(2)}, u32[]{:S(2)}) collective-permute-start(f32[264,128]{1,0:T(8,128)S(1)} %pad_maximum_fusion), channel_id=1, source_target_pairs={{0,64},{16,0},{32,96},{48,32},{64,128},{80,16},{96,160},{112,48},{... | collective-permute-start | bytes 405512 | tf_op jit(solution)/shard_map/ppermute | solution.py:203
  43.1 3.1 %collective-permute-start.2 = (f32[264,128]{1,0:T(8,128)S(1)}, f32[264,128]{1,0:T(8,128)S(1)}, u32[]{:S(2)}, u32[]{:S(2)}) collective-permute-start(f32[264,128]{1,0:T(8,128)S(1)} %pad_maximum_fusion), channel_id=1, source_target_pairs={{0,32},{16,0},{32,64},{48,16},{64,96},{80,48},{96,128},{112,80},{1... | collective-permute-start | bytes 405512 | tf_op jit(solution)/shard_map/ppermute | solution.py:203
  46.2 4.3 %local.1 = (f32[8,128,128]{2,1,0:T(8,128)S(1)}, f32[8,128,128]{2,1,0:T(8,128)S(1)}, f32[8,128,128]{2,1,0:T(8,128)S(1)}, f32[8,128,256]{2,1,0:T(8,128)S(1)}, f32[...) custom-call(f32[40,256]{1,0:T(8,128)S(1)} %broadcast_in_dim.16.flag,, ...), custom_call_target="tpu_custom_call" | custom-call | flops 4000000000 | bytes 9000000 | tf_op jit(solution)/shard_map/local/pallas_call | solution.py:320
  50.6 0.0 collective-permute-done.3
  50.6 0.0 collective-permute-done.2
  50.7 2.4 %collective-permute-start.4 = (f32[264,128]{1,0:T(8,128)S(1)}, f32[264,128]{1,0:T(8,128)S(1)}, u32[]{:S(2)}, u32[]{:S(2)}) collective-permute-start(f32[264,128]{1,0:T(8,128)S(1)} %pad_maximum_fusion.1), channel_id=1, source_target_pairs={{0,64},{16,0},{32,96},{48,32},{64,128},{80,16},{96,160},{112,48},{... | collective-permute-start | bytes 405512 | tf_op jit(solution)/shard_map/ppermute | solution.py:203
  53.1 3.6 %collective-permute-done.4 = f32[264,128]{1,0:T(8,128)S(1)} collective-permute-done((f32[264,128]{1,0:T(8,128)S(1)}, f32[264,128]{1,0:T(8,128)S(1)}, u32[]{:S(2)}, u32[]{:S(2)}) %collective-permute-start.4) | collective-permute-done | bytes 135200 | tf_op jit(solution)/shard_map/ppermute | solution.py:203
  56.8 0.1 collective-permute-start.5
  56.9 1.3 %collective-permute-done.5.other = f32[264,128]{1,0:T(8,128)S(1)} collective-permute-done((f32[264,128]{1,0:T(8,128)S(1)}, f32[264,128]{1,0:T(8,128)S(1)}, u32[]{:S(2)}, u32[]{:S(2)}) %collective-permute-start.5) | collective-permute-done | bytes 135200 | tf_op jit(solution)/shard_map/ppermute | solution.py:196
  58.2 1.4 %finish.1 = bf16[16,64,640]{2,1,0:T(8,128)(2,1)S(1)} custom-call(f32[40,256]{1,0:T(8,128)S(1)} %broadcast_in_dim.16.flag, bf16[16,64,896]{2,1,0:T(8,128)(2,1)S(1)} %all-to-all-done.x, f32[264,128]{1,0:T(8,128)S(1)} %pad_maximum_fusion.2.own, f32[264,128]{1,0:T(8,128)S(1)} %collective-permute-done.5.other, f32[8,128,128]{2,1,0:T(8,128)S(1)} %get-tuple-element.44.query_i, ...), custom_call_target="tpu_custom_call" | custom-call | tf_op jit(solution)/shard_map/finish/pallas_call | solution.py:389
  59.6 23.6 %all_to_all.10.x = bf16[16,64,640]{2,1,0:T(8,128)(2,1)S(1)} all-to-all(bf16[16,64,640]{2,1,0:T(8,128)(2,1)S(1)} %finish.1), channel_id=1, replica_groups=mesh['ctx'=16,'head'=16] {'head'}, dimensions={0} | all-to-all | bytes 2621440 | tf_op jit(solution)/shard_map/all_to_all | solution.py:413
  83.2 1.3 %unpack.1 = (bf16[64,2048]{1,0:T(8,128)(2,1)}, bf16[64,2048]{1,0:T(8,128)(2,1)}, bf16[64,4096]{1,0:T(8,128)(2,1)}, bf16[64,2048]{1,0:T(8,128)(2,1)}) custom-call(bf16[16,64,640]{2,1,0:T(8,128)(2,1)S(1)} %all_to_all.10.x), custom_call_target="tpu_custom_call" | custom-call | tf_op jit(solution)/shard_map/unpack/pallas_call | solution.py:102
  (19 shorter events, 0.2 us)
Async XLA Ops:
  3.2 7.2 %copy-start = (s32[16]{0:T(128)S(1)}, s32[16]{0:T(128)}, u32[]{:S(2)}) copy-start(s32[16]{0:T(128)} %param.13) | copy-start | bytes 196
  3.2 34.2 %all-to-all-start = ((bf16[16,64,896]{2,1,0:T(8,128)(2,1)}), bf16[16,64,896]{2,1,0:T(8,128)(2,1)S(1)}, u32[]{:S(2)}, u32[]{:S(2)}) async-start(bf16[16,64,896]{2,1,0:T(8,128)(2,1)} %pack.1), calls=%async_computation | async-start | bytes 3670016 | tf_op jit(solution)/shard_map/all_to_all | solution.py:404
  10.4 3.0 %collective-permute-start = (s32[16]{0:T(128)S(1)}, s32[16]{0:T(128)S(1)}, u32[]{:S(2)}, u32[]{:S(2)}) collective-permute-start(s32[16]{0:T(128)S(1)} %copy-done), channel_id=1, source_target_pairs={{0,16},{16,32},{32,48},{48,64},{64,80},{80,96},{96,112},{112,128},... | collective-permute-start | bytes 200 | tf_op jit(solution)/shard_map/ppermute | solution.py:45
  38.3 1.4 %collective-permute-start.1 = (f32[264,128]{1,0:T(8,128)S(1)}, f32[264,128]{1,0:T(8,128)S(1)}, u32[]{:S(2)}, u32[]{:S(2)}) collective-permute-start(f32[264,128]{1,0:T(8,128)S(1)} %get-tuple-element.29), channel_id=1, source_target_pairs={{0,16},{16,0},{32,48},{48,32},{64,80},{80,64},{96,112},{112,96},{1... | collective-permute-start | bytes 405512 | tf_op jit(solution)/shard_map/ppermute | solution.py:196
  39.7 10.8 %collective-permute-start.3 = (f32[264,128]{1,0:T(8,128)S(1)}, f32[264,128]{1,0:T(8,128)S(1)}, u32[]{:S(2)}, u32[]{:S(2)}) collective-permute-start(f32[264,128]{1,0:T(8,128)S(1)} %pad_maximum_fusion), channel_id=1, source_target_pairs={{0,64},{16,0},{32,96},{48,32},{64,128},{80,16},{96,160},{112,48},{... | collective-permute-start | bytes 405512 | tf_op jit(solution)/shard_map/ppermute | solution.py:203
  43.1 7.5 %collective-permute-start.2 = (f32[264,128]{1,0:T(8,128)S(1)}, f32[264,128]{1,0:T(8,128)S(1)}, u32[]{:S(2)}, u32[]{:S(2)}) collective-permute-start(f32[264,128]{1,0:T(8,128)S(1)} %pad_maximum_fusion), channel_id=1, source_target_pairs={{0,32},{16,0},{32,64},{48,16},{64,96},{80,48},{96,128},{112,80},{1... | collective-permute-start | bytes 405512 | tf_op jit(solution)/shard_map/ppermute | solution.py:203
  50.7 6.0 %collective-permute-start.4 = (f32[264,128]{1,0:T(8,128)S(1)}, f32[264,128]{1,0:T(8,128)S(1)}, u32[]{:S(2)}, u32[]{:S(2)}) collective-permute-start(f32[264,128]{1,0:T(8,128)S(1)} %pad_maximum_fusion.1), channel_id=1, source_target_pairs={{0,64},{16,0},{32,96},{48,32},{64,128},{80,16},{96,160},{112,48},{... | collective-permute-start | bytes 405512 | tf_op jit(solution)/shard_map/ppermute | solution.py:203
  56.8 1.4 %collective-permute-start.5 = (f32[264,128]{1,0:T(8,128)S(1)}, f32[264,128]{1,0:T(8,128)S(1)}, u32[]{:S(2)}, u32[]{:S(2)}) collective-permute-start(f32[264,128]{1,0:T(8,128)S(1)} %pad_maximum_fusion.3), channel_id=1, source_target_pairs={{0,16},{16,0},{32,48},{48,32},{64,80},{80,64},{96,112},{112,96},{1... | collective-permute-start | bytes 405512 | tf_op jit(solution)/shard_map/ppermute | solution.py:196

commit v7 on v6

--- a/solution.py
+++ b/solution.py
@@ -40,50 +40,78 @@
     return r[:, :DK] + r[:, DK:]
 
 
-def flag_rows(live_blocks, block_doc, index):
-    n = lax.axis_size("ctx")
-    before = lax.ppermute(block_doc, "ctx", [(i, (i + 1) % n) for i in range(n)])
-    place = jnp.arange(NB)
-    live = place < live_blocks[0]
-    previous = jnp.concatenate([before[NB - 1 :], block_doc[: NB - 1]])
-    keep = (previous == block_doc) & ((place > 0) | (index > 0))
-    even = jnp.full((8,), index % 2 == 0)
-    rows = jnp.concatenate([live, keep, even]).astype(F32)
-    return jnp.broadcast_to(rows[:, None], (2 * NB + 8, DV))
+EVEN, INSIDE, HEAD_ID, TAIL_ID, FLAG_ROWS = 2 * NB, 2 * NB + 1, 2 * NB + 3, 2 * NB + 4, 2 * NB + 8
 
 
 def flags(flag):
     row = lambda r: flag[r : r + 1, :DK]
     lives, keeps = [row(b) for b in range(NB)], [row(NB + b) for b in range(NB)]
-    return lives, keeps, row(2 * NB) > 0.0
-
-
-PACK_STEPS = 2
-PER = HEADS // PACK_STEPS
-
-
-def pack_kernel(q, k, g, v, u, out):
-    for h in range(PER):
-        kc = slice(h * DK, (h + 1) * DK)
-        vc = slice(h * DV, (h + 1) * DV)
-        out[h, :, QC : QC + DK] = q[:, kc]
-        out[h, :, KC : KC + DK] = k[:, kc]
-        out[h, :, GC : GC + DK] = g[:, kc]
-        out[h, :, VC : VC + DV] = v[:, vc]
-        out[h, :, UC : UC + DV] = u[:, vc]
-
-
-def pack(q, k, g, v, u):
-    narrow = pl.BlockSpec((BLOCK, PER * DK), lambda i: (0, i))
-    wide = pl.BlockSpec((BLOCK, PER * DV), lambda i: (0, i))
+    return lives, keeps, row(EVEN) > 0.0
+
+
+SPLIT = 2
+
+
+def pack_kernel(
+    owners, live_h, doc_h, q, k, g, v, u, out, flag, qv, kv, gv, vv, uv, live, doc, sem, small_sem
+):
+    arrays = (
+        (v, vv, DV, VC), (u, uv, DV, UC), (q, qv, DK, QC), (k, kv, DK, KC), (g, gv, DK, GC),
+    )
+    rows = BLOCK // SPLIT
+    copies = {}
+    for r in range(SPLIT):
+        at = pl.ds(r * rows, rows)
+        for n, (src, dst, _, _) in enumerate(arrays):
+            copies[r, n] = pltpu.make_async_copy(src.at[at], dst.at[at], sem.at[r * 5 + n])
+            copies[r, n].start()
+
+    small = [
+        pltpu.make_async_copy(live_h, live, small_sem.at[0]),
+        pltpu.make_async_copy(doc_h, doc, small_sem.at[1]),
+    ]
+    for copy in small:
+        copy.start()
+    for copy in small:
+        copy.wait()
+    one_if = lambda c: jnp.where(c, 1.0, 0.0).astype(F32)
+    index = lax.axis_index("ctx")
+    even = lax.rem(index, 2) == 0
+    first, last = doc[0].astype(F32), doc[NB - 1].astype(F32)
+    numbers = [one_if(b < live[0]) for b in range(NB)] + [jnp.float32(1.0)]
+    numbers += [one_if(doc[b - 1] == doc[b]) for b in range(1, NB)]
+    numbers.append(one_if(even))
+    for by in (1, 2):
+        numbers.append(one_if(jnp.where(even, index >= 2 * by, index < owners - 2 * by)))
+    numbers += [jnp.where(even, last, first), jnp.where(even, first, last)]
+    for r in range(FLAG_ROWS):
+        flag[r : r + 1] = jnp.full((1, DV), numbers[r] if r < len(numbers) else 0.0, F32)
+
+    for r in range(SPLIT):
+        at = slice(r * rows, (r + 1) * rows)
+        for n, (_, src, width, col) in enumerate(arrays):
+            copies[r, n].wait()
+            for h in range(HEADS):
+                out[h, at, col : col + width] = src[at, h * width : (h + 1) * width]
+
+
+def pack(live, doc, q, k, g, v, u):
+    hbm = pl.BlockSpec(memory_space=pltpu.HBM)
     return pl.pallas_call(
-        pack_kernel,
-        grid=(PACK_STEPS,),
-        out_shape=jax.ShapeDtypeStruct((HEADS, BLOCK, IN_W), BF),
-        in_specs=[narrow] * 3 + [wide] * 2,
-        out_specs=pl.BlockSpec((PER, BLOCK, IN_W), lambda i: (i, 0, 0)),
+        functools.partial(pack_kernel, lax.axis_size("ctx")),
+        out_shape=(
+            jax.ShapeDtypeStruct((HEADS, BLOCK, IN_W), BF),
+            jax.ShapeDtypeStruct((FLAG_ROWS, DV), F32),
+        ),
+        in_specs=[hbm] * 7,
+        out_specs=(vspec(),) * 2,
+        scratch_shapes=[VMEM((BLOCK, HEADS * DK), BF)] * 3
+        + [VMEM((BLOCK, HEADS * DV), BF)] * 2
+        + [pltpu.SMEM((1,), jnp.int32), pltpu.SMEM((NB,), jnp.int32)]
+        + [pltpu.SemaphoreType.DMA((5 * SPLIT,)), pltpu.SemaphoreType.DMA((2,))],
+        compiler_params=pltpu.CompilerParams(vmem_limit_bytes=56 * 1024 * 1024),
         name="pack",
-    )(q, k, g, v, u)
+    )(live, doc, q, k, g, v, u)
 
 
 def unpack_kernel(x, dq, dk, dv, dg):
@@ -164,8 +192,10 @@
     fwd = halves(dot(v, kw[...].reshape(rows, 2 * DK), 0, 0))
     kept[:DV] = jnp.where(even, fwd, bwd)
     sent[:DV] = jnp.where(even, bwd, fwd)
-    kept[DV:] = jnp.broadcast_to(decay, (MSG - DV, DK))
-    sent[DV:] = jnp.broadcast_to(decay, (MSG - DV, DK))
+    head, tail = flag[HEAD_ID : HEAD_ID + 1, :DK], flag[TAIL_ID : TAIL_ID + 1, :DK]
+    rest = jnp.zeros((MSG - DV - 3, DK), F32)
+    kept[DV:] = jnp.concatenate([decay, head, tail, rest])
+    sent[DV:] = jnp.concatenate([decay, tail, head, rest])
 
 
 def totals(flag, x):
@@ -185,10 +215,14 @@
     )(flag, x)
 
 
+def passing(near, far):
+    return jnp.where(near[DV + 2 : DV + 3] == far[DV + 1 : DV + 2], near[DV : DV + 1], 0.0)
+
+
 def joined(near, far):
-    return jnp.concatenate(
-        [near[DV : DV + 1] * far[:DV] + near[:DV], near[DV:] * far[DV:]], axis=0
-    )
+    decay = passing(near, far)
+    ends = [decay * far[DV : DV + 1], near[DV + 1 : DV + 2], far[DV + 2 :]]
+    return jnp.concatenate([decay * far[:DV] + near[:DV], *ends], axis=0)
 
 
 def swapped(x):
@@ -196,24 +230,27 @@
     return lax.ppermute(x, "ctx", [(i, i ^ 1) for i in range(n)])
 
 
-def upstream(x, index, by):
+def upstream(x, flag, by):
     n = lax.axis_size("ctx")
     target = lambda i: i + (2 * by if i % 2 == 0 else -2 * by)
     pairs = [(i, target(i) if 0 <= target(i) < n else i ^ 1) for i in range(n)]
     moved = lax.ppermute(x, "ctx", pairs)
-    source = jnp.where(index % 2 == 0, index - 2 * by, index + 2 * by)
-    return jnp.where((source >= 0) & (source < n), moved, 0.0)
-
-
-def window(kept, sent, index, beside):
+    row = INSIDE + by - 1
+    return jnp.where(flag[row : row + 1, :DK] > 0.0, moved, 0.0)
+
+
+def window(kept, sent, flag, beside):
     other = swapped(sent)
     chip = joined(other, kept)
-    near, far = upstream(chip, index, 1), upstream(chip, index, 2)
+    near, far = upstream(chip, flag, 1), upstream(chip, flag, 2)
     done = beside(chip)
     near, far, done = lax.optimization_barrier((near, far, done))
     e = joined(near, far)
-    e = joined(e, upstream(e, index, 2))
-    return e, swapped(joined(kept, e)), done
+    e = joined(e, upstream(e, flag, 2))
+    own = jnp.where(kept[DV + 2 : DV + 3] == e[DV + 1 : DV + 2], e[:DV], 0.0)
+    onward = kept[DV : DV + 1] * own + kept[:DV]
+    onward = jnp.where(other[DV + 2 : DV + 3] == kept[DV + 1 : DV + 2], onward, 0.0)
+    return own, swapped(onward), done
 
 
 def local_kernel(
@@ -348,8 +385,8 @@
     upper, strict = one(j >= i).astype(BF), one(j < i).astype(BF)
     sums = jnp.concatenate([upper, upper, strict, strict], axis=1)
     lives, _, even = flags(flag)
-    state = jnp.where(even, own[:DV], other[:DV])
-    grad = jnp.where(even, other[:DV], own[:DV])
+    state = jnp.where(even, own[...], other[...])
+    grad = jnp.where(even, other[...], own[...])
     rows = NB * BLOCK
     u = x[:, :, UC : UC + DV].reshape(rows, DV)
     v = x[:, :, VC : VC + DV].reshape(rows, DV)
@@ -398,9 +435,7 @@
 
 
 def per_device(queries, keys, values, out_grad, log_gates, live_blocks, block_doc):
-    index = lax.axis_index("ctx")
-    flag = flag_rows(live_blocks, block_doc, index)
-    packed = pack(queries, keys, log_gates, values, out_grad)
+    packed, flag = pack(live_blocks, block_doc, queries, keys, log_gates, values, out_grad)
     x = lax.all_to_all(packed, "head", split_axis=0, concat_axis=0, tiled=True)
     kept, sent = totals(flag, x)
 
@@ -408,7 +443,7 @@
         y, _ = lax.optimization_barrier((x, chip))
         return local(flag, y)
 
-    own, other, parts = window(kept, sent, index, beside)
+    own, other, parts = window(kept, sent, flag, beside)
     y = finish(flag, x, own, other, parts)
     return unpack(lax.all_to_all(y, "head", split_axis=0, concat_axis=0, tiled=True))
 

time: 85.8 us -> 85 us (level)
  blocking collectives: 23.6 us -> 56.1 us
  waiting for transfers between devices: 31.1 us -> 6.24 us
  starting transfers between devices: 16.2 us -> 9.03 us
    all_to_all x0 -> x1, blocking collectives: none -> 32.4 us  [per_device(): x = lax.all_to_all(packed, 'head', split_axis=0, concat_axis=0, tiled=True)]
    all_to_all x1 -> x0, waiting for transfers between devices: 22.7 us -> none  [per_device(): x = lax.all_to_all(packed, 'head', split_axis=0, concat_axis=0, tiled=True)]
    all_to_all x1 -> x0, starting transfers between devices: 7.17 us -> none  [per_device(): x = lax.all_to_all(packed, 'head', split_axis=0, concat_axis=0, tiled=True)]
    ppermute x1 -> x0, waiting for transfers between devices: 2.26 us -> none  [flag_rows(): lax.ppermute(block_doc, 'ctx', [(i, (i + 1) % n) for i in range(n)])]
  transfers between devices with their start and end apart: 7 -> 5, of which waited for: 5 -> 3; matrix products, arithmetic and copies ran while one was open for 2% -> 0% of each run, Pallas kernels for 5% -> 5%
where the time goes in v7:
time: 85 us; the launch traced here: 83.6 us
  blocking collectives  56.1 us (66%)
  Pallas kernels  10.6 us (12%)
  starting transfers between devices  9.03 us (11%)
  waiting for transfers between devices  6.24 us (7%)
  between operations  1.42 us (2%)
    all_to_all x1, blocking collectives, per_device(): x = lax.all_to_all(packed, 'head', split_axis=0, concat_axis=0, tiled=True)  32.4 us
    all_to_all x1, blocking collectives, per_device(): lax.all_to_all(y, 'head', split_axis=0, concat_axis=0, tiled=True)  23.7 us
    ppermute x3, starting transfers between devices, upstream(): moved = lax.ppermute(x, 'ctx', pairs)  8.84 us
    pallas_call x1, Pallas kernels, local(): pl.pallas_call(local_kernel, out_shape=(t, t, t, f(PAIR, DV), t, t, jax.S...  4.37 us
    ppermute x3, waiting for transfers between devices, upstream(): moved = lax.ppermute(x, 'ctx', pairs)  3.59 us
    pallas_call x1, Pallas kernels, pack(): pl.pallas_call(functools.partial(pack_kernel, lax.axis_size('ctx')), out_...  2.81 us
    ppermute x2, waiting for transfers between devices, swapped(): return lax.ppermute(x, 'ctx', [(i, i ^ 1) for i in range(n)])  2.65 us
  transfers between devices with their start and end apart: 5, of which 3 were waited for; matrix products, arithmetic and copies ran while one was open for 0% of the time, Pallas kernels for 5%

profile of v7, /device:TPU:32, one launch (start us, length us, event | category | flops | bytes accessed | tf_op | source)
XLA Modules:
  0.0 83.6 jit_solution(16606006402449099012)
XLA Ops:
  1.3 2.8 %pack.1 = (bf16[16,64,896]{2,1,0:T(8,128)(2,1)}, f32[40,256]{1,0:T(8,128)}) custom-call(s32[1]{0:T(128)S(6)} %copy.11.live_h, s32[16]{0:T(128)} %doc_h.1, bf16[64,2048]{1,0:T(8,128)(2,1)} %q.1, bf16[64,2048]{1,0:T(8,128)(2,1)} %k.1, bf16[64,2048]{1,0:T(8,128)(2,1)} %g.1, bf16[64,4096]{1,0:T(8,128)(2,1)} %v.1, bf16[64,4096]{1,0:T(8,128)(2,1)} %u.1), custom_call_target="tpu_custom_call" | custom-call | tf_op jit(solution)/shard_map/pack/pallas_call | solution.py:100
  4.1 0.0 copy-start
  4.1 32.4 %all_to_all.10.x = bf16[16,64,896]{2,1,0:T(8,128)(2,1)S(1)} all-to-all(bf16[16,64,896]{2,1,0:T(8,128)(2,1)} %get-tuple-element.32), channel_id=1, replica_groups=mesh['ctx'=16,'head'=16] {'head'}, dimensions={0} | all-to-all | bytes 3670016 | tf_op jit(solution)/shard_map/all_to_all | solution.py:439
  36.5 0.0 copy-done
  36.5 0.8 totals.1
  37.3 0.1 collective-permute-start
  37.4 1.3 %collective-permute-done = f32[264,128]{1,0:T(8,128)S(1)} collective-permute-done((f32[264,128]{1,0:T(8,128)S(1)}, f32[264,128]{1,0:T(8,128)S(1)}, u32[]{:S(2)}, u32[]{:S(2)}) %collective-permute-start) | collective-permute-done | bytes 135200 | tf_op jit(solution)/shard_map/ppermute | solution.py:230
  38.8 3.3 %collective-permute-start.2 = (f32[264,128]{1,0:T(8,128)S(1)}, f32[264,128]{1,0:T(8,128)S(1)}, u32[]{:S(2)}, u32[]{:S(2)}) collective-permute-start(f32[264,128]{1,0:T(8,128)S(1)} %pad_maximum_fusion), channel_id=1, source_target_pairs={{0,64},{16,0},{32,96},{48,32},{64,128},{80,16},{96,160},{112,48},{... | collective-permute-start | bytes 405512 | tf_op jit(solution)/shard_map/ppermute | solution.py:237
  42.2 3.1 %collective-permute-start.1 = (f32[264,128]{1,0:T(8,128)S(1)}, f32[264,128]{1,0:T(8,128)S(1)}, u32[]{:S(2)}, u32[]{:S(2)}) collective-permute-start(f32[264,128]{1,0:T(8,128)S(1)} %pad_maximum_fusion), channel_id=1, source_target_pairs={{0,32},{16,0},{32,64},{48,16},{64,96},{80,48},{96,128},{112,80},{1... | collective-permute-start | bytes 405512 | tf_op jit(solution)/shard_map/ppermute | solution.py:237
  45.3 4.4 %local.1 = (f32[8,128,128]{2,1,0:T(8,128)S(1)}, f32[8,128,128]{2,1,0:T(8,128)S(1)}, f32[8,128,128]{2,1,0:T(8,128)S(1)}, f32[8,128,256]{2,1,0:T(8,128)S(1)}, f32[...) custom-call(f32[40,256]{1,0:T(8,128)S(1)} %copy-done, ...), custom_call_target="tpu_custom_call" | custom-call | flops 4000000000 | bytes 9000000 | tf_op jit(solution)/shard_map/local/pallas_call | solution.py:357
  49.7 0.0 collective-permute-done.2
  49.7 0.0 collective-permute-done.1
  49.8 2.4 %collective-permute-start.3 = (f32[264,128]{1,0:T(8,128)S(1)}, f32[264,128]{1,0:T(8,128)S(1)}, u32[]{:S(2)}, u32[]{:S(2)}) collective-permute-start(f32[264,128]{1,0:T(8,128)S(1)} %pad_maximum_fusion.1), channel_id=1, source_target_pairs={{0,64},{16,0},{32,96},{48,32},{64,128},{80,16},{96,160},{112,48},{... | collective-permute-start | bytes 405512 | tf_op jit(solution)/shard_map/ppermute | solution.py:237
  52.2 3.6 %collective-permute-done.3 = f32[264,128]{1,0:T(8,128)S(1)} collective-permute-done((f32[264,128]{1,0:T(8,128)S(1)}, f32[264,128]{1,0:T(8,128)S(1)}, u32[]{:S(2)}, u32[]{:S(2)}) %collective-permute-start.3) | collective-permute-done | bytes 135200 | tf_op jit(solution)/shard_map/ppermute | solution.py:237
  55.8 0.1 collective-permute-start.4
  55.9 1.3 %collective-permute-done.4.other = f32[256,128]{1,0:T(8,128)S(1)} collective-permute-done((f32[256,128]{1,0:T(8,128)S(1)}, f32[256,128]{1,0:T(8,128)S(1)}, u32[]{:S(2)}, u32[]{:S(2)}) %collective-permute-start.4) | collective-permute-done | bytes 131104 | tf_op jit(solution)/shard_map/ppermute | solution.py:230
  57.3 1.3 %finish.1 = bf16[16,64,640]{2,1,0:T(8,128)(2,1)S(1)} custom-call(f32[40,256]{1,0:T(8,128)S(1)} %copy-done, bf16[16,64,896]{2,1,0:T(8,128)(2,1)S(1)} %all_to_all.10.x, f32[256,128]{1,0:T(8,128)S(1)} %get-tuple-element.59.own, f32[256,128]{1,0:T(8,128)S(1)} %collective-permute-done.4.other, f32[8,128,128]{2,1,0:T(8,128)S(1)} %get-tuple-element.48.query_i, ...), custom_call_target="tpu_custom_call" | custom-call | tf_op jit(solution)/shard_map/finish/pallas_call | solution.py:426
  58.6 23.7 %all_to_all.11.x = bf16[16,64,640]{2,1,0:T(8,128)(2,1)S(1)} all-to-all(bf16[16,64,640]{2,1,0:T(8,128)(2,1)S(1)} %finish.1), channel_id=1, replica_groups=mesh['ctx'=16,'head'=16] {'head'}, dimensions={0} | all-to-all | bytes 2621440 | tf_op jit(solution)/shard_map/all_to_all | solution.py:448
  82.3 1.3 %unpack.1 = (bf16[64,2048]{1,0:T(8,128)(2,1)}, bf16[64,2048]{1,0:T(8,128)(2,1)}, bf16[64,4096]{1,0:T(8,128)(2,1)}, bf16[64,2048]{1,0:T(8,128)(2,1)}) custom-call(bf16[16,64,640]{2,1,0:T(8,128)(2,1)S(1)} %all_to_all.11.x), custom_call_target="tpu_custom_call" | custom-call | tf_op jit(solution)/shard_map/unpack/pallas_call | solution.py:130
  (15 shorter events, 0.2 us)
Async XLA Ops:
  4.1 32.4 %copy-start = (f32[40,256]{1,0:T(8,128)S(1)}, f32[40,256]{1,0:T(8,128)}, u32[]{:S(2)}) copy-start(f32[40,256]{1,0:T(8,128)} %get-tuple-element.31.flag) | copy-start | bytes 122884
  37.3 1.4 %collective-permute-start = (f32[264,128]{1,0:T(8,128)S(1)}, f32[264,128]{1,0:T(8,128)S(1)}, u32[]{:S(2)}, u32[]{:S(2)}) collective-permute-start(f32[264,128]{1,0:T(8,128)S(1)} %get-tuple-element.34), channel_id=1, source_target_pairs={{0,16},{16,0},{32,48},{48,32},{64,80},{80,64},{96,112},{112,96},{1... | collective-permute-start | bytes 405512 | tf_op jit(solution)/shard_map/ppermute | solution.py:230
  38.8 10.9 %collective-permute-start.2 = (f32[264,128]{1,0:T(8,128)S(1)}, f32[264,128]{1,0:T(8,128)S(1)}, u32[]{:S(2)}, u32[]{:S(2)}) collective-permute-start(f32[264,128]{1,0:T(8,128)S(1)} %pad_maximum_fusion), channel_id=1, source_target_pairs={{0,64},{16,0},{32,96},{48,32},{64,128},{80,16},{96,160},{112,48},{... | collective-permute-start | bytes 405512 | tf_op jit(solution)/shard_map/ppermute | solution.py:237
  42.2 7.5 %collective-permute-start.1 = (f32[264,128]{1,0:T(8,128)S(1)}, f32[264,128]{1,0:T(8,128)S(1)}, u32[]{:S(2)}, u32[]{:S(2)}) collective-permute-start(f32[264,128]{1,0:T(8,128)S(1)} %pad_maximum_fusion), channel_id=1, source_target_pairs={{0,32},{16,0},{32,64},{48,16},{64,96},{80,48},{96,128},{112,80},{1... | collective-permute-start | bytes 405512 | tf_op jit(solution)/shard_map/ppermute | solution.py:237
  49.8 6.0 %collective-permute-start.3 = (f32[264,128]{1,0:T(8,128)S(1)}, f32[264,128]{1,0:T(8,128)S(1)}, u32[]{:S(2)}, u32[]{:S(2)}) collective-permute-start(f32[264,128]{1,0:T(8,128)S(1)} %pad_maximum_fusion.1), channel_id=1, source_target_pairs={{0,64},{16,0},{32,96},{48,32},{64,128},{80,16},{96,160},{112,48},{... | collective-permute-start | bytes 405512 | tf_op jit(solution)/shard_map/ppermute | solution.py:237
  55.8 1.4 %collective-permute-start.4 = (f32[256,128]{1,0:T(8,128)S(1)}, f32[256,128]{1,0:T(8,128)S(1)}, u32[]{:S(2)}, u32[]{:S(2)}) collective-permute-start(f32[256,128]{1,0:T(8,128)S(1)} %get-tuple-element.58), channel_id=1, source_target_pairs={{0,16},{16,0},{32,48},{48,32},{64,80},{80,64},{96,112},{112,96},{1... | collective-permute-start | bytes 393224 | tf_op jit(solution)/shard_map/ppermute | solution.py:230

commit v8 on v7

--- a/solution.py
+++ b/solution.py
@@ -53,7 +53,8 @@
 
 
 def pack_kernel(
-    owners, live_h, doc_h, q, k, g, v, u, out, flag, qv, kv, gv, vv, uv, live, doc, sem, small_sem
+    owners, live_h, doc_h, q, k, g, v, u, out_h, flag_h,
+    qv, kv, gv, vv, uv, out, flag, live, doc, sem, small_sem, out_sem,
 ):
     arrays = (
         (v, vv, DV, VC), (u, uv, DV, UC), (q, qv, DK, QC), (k, kv, DK, KC), (g, gv, DK, GC),
@@ -86,6 +87,8 @@
     numbers += [jnp.where(even, last, first), jnp.where(even, first, last)]
     for r in range(FLAG_ROWS):
         flag[r : r + 1] = jnp.full((1, DV), numbers[r] if r < len(numbers) else 0.0, F32)
+    outs = [pltpu.make_async_copy(flag, flag_h, out_sem.at[SPLIT])]
+    outs[0].start()
 
     for r in range(SPLIT):
         at = slice(r * rows, (r + 1) * rows)
@@ -93,6 +96,11 @@
             copies[r, n].wait()
             for h in range(HEADS):
                 out[h, at, col : col + width] = src[at, h * width : (h + 1) * width]
+        at = pl.ds(r * rows, rows)
+        outs.append(pltpu.make_async_copy(out.at[:, at], out_h.at[:, at], out_sem.at[r]))
+        outs[-1].start()
+    for copy in outs:
+        copy.wait()
 
 
 def pack(live, doc, q, k, g, v, u):
@@ -104,24 +112,28 @@
             jax.ShapeDtypeStruct((FLAG_ROWS, DV), F32),
         ),
         in_specs=[hbm] * 7,
-        out_specs=(vspec(),) * 2,
+        out_specs=(hbm,) * 2,
         scratch_shapes=[VMEM((BLOCK, HEADS * DK), BF)] * 3
         + [VMEM((BLOCK, HEADS * DV), BF)] * 2
+        + [VMEM((HEADS, BLOCK, IN_W), BF), VMEM((FLAG_ROWS, DV), F32)]
         + [pltpu.SMEM((1,), jnp.int32), pltpu.SMEM((NB,), jnp.int32)]
-        + [pltpu.SemaphoreType.DMA((5 * SPLIT,)), pltpu.SemaphoreType.DMA((2,))],
+        + [pltpu.SemaphoreType.DMA((n,)) for n in (5 * SPLIT, 2, SPLIT + 1)],
         compiler_params=pltpu.CompilerParams(vmem_limit_bytes=56 * 1024 * 1024),
         name="pack",
     )(live, doc, q, k, g, v, u)
 
 
-def unpack_kernel(x, dq, dk, dv, dg):
-    for h in range(HEADS):
-        kc = slice(h * DK, (h + 1) * DK)
-        vc = slice(h * DV, (h + 1) * DV)
-        dq[:, kc] = x[h, :, 0:DK]
-        dk[:, kc] = x[h, :, DK : 2 * DK]
-        dg[:, kc] = x[h, :, 2 * DK : 3 * DK]
-        dv[:, vc] = x[h, :, 3 * DK :]
+def unpack_kernel(x, dq, dk, dv, dg, qv, kv, vv, gv, sem):
+    copies = []
+    for n, (dst, buf, width, col) in enumerate(
+        ((dv, vv, DV, 3 * DK), (dq, qv, DK, 0), (dk, kv, DK, DK), (dg, gv, DK, 2 * DK))
+    ):
+        for h in range(HEADS):
+            buf[:, h * width : (h + 1) * width] = x[h, :, col : col + width]
+        copies.append(pltpu.make_async_copy(buf, dst, sem.at[n]))
+        copies[-1].start()
+    for copy in copies:
+        copy.wait()
 
 
 def unpack(x):
@@ -131,7 +143,9 @@
         unpack_kernel,
         out_shape=(narrow, narrow, wide, narrow),
         in_specs=[vspec()],
-        out_specs=(vspec(),) * 4,
+        out_specs=(pl.BlockSpec(memory_space=pltpu.HBM),) * 4,
+        scratch_shapes=[VMEM(s.shape, BF) for s in (narrow, narrow, wide, narrow)]
+        + [pltpu.SemaphoreType.DMA((4,))],
         compiler_params=pltpu.CompilerParams(vmem_limit_bytes=16 * 1024 * 1024),
         name="unpack",
     )(x)

time: 85 us -> 84.5 us (level)
  no operation moved by 1% of the time
where the time goes in v8:
time: 84.5 us; the launch traced here: 83.2 us
  blocking collectives  56.1 us (66%)
  Pallas kernels  10.1 us (12%)
  starting transfers between devices  9.03 us (11%)
  waiting for transfers between devices  6.24 us (7%)
  between operations  1.42 us (2%)
    all_to_all x1, blocking collectives, per_device(): x = lax.all_to_all(packed, 'head', split_axis=0, concat_axis=0, tiled=True)  32.4 us
    all_to_all x1, blocking collectives, per_device(): lax.all_to_all(y, 'head', split_axis=0, concat_axis=0, tiled=True)  23.7 us
    ppermute x3, starting transfers between devices, upstream(): moved = lax.ppermute(x, 'ctx', pairs)  8.85 us
    pallas_call x1, Pallas kernels, local(): pl.pallas_call(local_kernel, out_shape=(t, t, t, f(PAIR, DV), t, t, jax.S...  4.37 us
    ppermute x3, waiting for transfers between devices, upstream(): moved = lax.ppermute(x, 'ctx', pairs)  3.59 us
    ppermute x2, waiting for transfers between devices, swapped(): return lax.ppermute(x, 'ctx', [(i, i ^ 1) for i in range(n)])  2.65 us
    pallas_call x1, Pallas kernels, pack(): pl.pallas_call(functools.partial(pack_kernel, lax.axis_size('ctx')), out_...  2.53 us
  transfers between devices with their start and end apart: 5, of which 3 were waited for; matrix products, arithmetic and copies ran while one was open for 0% of the time, Pallas kernels for 5%

profile of v8, /device:TPU:32, one launch (start us, length us, event | category | flops | bytes accessed | tf_op | source)
XLA Modules:
  0.0 83.2 jit_solution(2795858710532427311)
XLA Ops:
  1.3 2.5 %pack.1 = (bf16[16,64,896]{2,1,0:T(8,128)(2,1)}, f32[40,256]{1,0:T(8,128)}) custom-call(s32[1]{0:T(128)S(6)} %copy.11.live_h, s32[16]{0:T(128)} %doc_h.1, bf16[64,2048]{1,0:T(8,128)(2,1)} %q.1, bf16[64,2048]{1,0:T(8,128)(2,1)} %k.1, bf16[64,2048]{1,0:T(8,128)(2,1)} %g.1, bf16[64,4096]{1,0:T(8,128)(2,1)} %v.1, bf16[64,4096]{1,0:T(8,128)(2,1)} %u.1), custom_call_target="tpu_custom_call" | custom-call | tf_op jit(solution)/shard_map/pack/pallas_call | solution.py:108
  3.8 0.0 copy-start
  3.8 32.4 %all_to_all.10.x = bf16[16,64,896]{2,1,0:T(8,128)(2,1)S(1)} all-to-all(bf16[16,64,896]{2,1,0:T(8,128)(2,1)} %get-tuple-element.32), channel_id=1, replica_groups=mesh['ctx'=16,'head'=16] {'head'}, dimensions={0} | all-to-all | bytes 3670016 | tf_op jit(solution)/shard_map/all_to_all | solution.py:453
  36.2 0.0 copy-done
  36.2 0.8 totals.1
  37.0 0.1 collective-permute-start
  37.2 1.3 %collective-permute-done = f32[264,128]{1,0:T(8,128)S(1)} collective-permute-done((f32[264,128]{1,0:T(8,128)S(1)}, f32[264,128]{1,0:T(8,128)S(1)}, u32[]{:S(2)}, u32[]{:S(2)}) %collective-permute-start) | collective-permute-done | bytes 135200 | tf_op jit(solution)/shard_map/ppermute | solution.py:244
  38.5 3.3 %collective-permute-start.2 = (f32[264,128]{1,0:T(8,128)S(1)}, f32[264,128]{1,0:T(8,128)S(1)}, u32[]{:S(2)}, u32[]{:S(2)}) collective-permute-start(f32[264,128]{1,0:T(8,128)S(1)} %pad_maximum_fusion), channel_id=1, source_target_pairs={{0,64},{16,0},{32,96},{48,32},{64,128},{80,16},{96,160},{112,48},{... | collective-permute-start | bytes 405512 | tf_op jit(solution)/shard_map/ppermute | solution.py:251
  41.9 3.1 %collective-permute-start.1 = (f32[264,128]{1,0:T(8,128)S(1)}, f32[264,128]{1,0:T(8,128)S(1)}, u32[]{:S(2)}, u32[]{:S(2)}) collective-permute-start(f32[264,128]{1,0:T(8,128)S(1)} %pad_maximum_fusion), channel_id=1, source_target_pairs={{0,32},{16,0},{32,64},{48,16},{64,96},{80,48},{96,128},{112,80},{1... | collective-permute-start | bytes 405512 | tf_op jit(solution)/shard_map/ppermute | solution.py:251
  45.0 4.4 %local.1 = (f32[8,128,128]{2,1,0:T(8,128)S(1)}, f32[8,128,128]{2,1,0:T(8,128)S(1)}, f32[8,128,128]{2,1,0:T(8,128)S(1)}, f32[8,128,256]{2,1,0:T(8,128)S(1)}, f32[...) custom-call(f32[40,256]{1,0:T(8,128)S(1)} %copy-done, ...), custom_call_target="tpu_custom_call" | custom-call | flops 4000000000 | bytes 9000000 | tf_op jit(solution)/shard_map/local/pallas_call | solution.py:371
  49.4 0.0 collective-permute-done.2
  49.4 0.0 collective-permute-done.1
  49.5 2.4 %collective-permute-start.3 = (f32[264,128]{1,0:T(8,128)S(1)}, f32[264,128]{1,0:T(8,128)S(1)}, u32[]{:S(2)}, u32[]{:S(2)}) collective-permute-start(f32[264,128]{1,0:T(8,128)S(1)} %pad_maximum_fusion.1), channel_id=1, source_target_pairs={{0,64},{16,0},{32,96},{48,32},{64,128},{80,16},{96,160},{112,48},{... | collective-permute-start | bytes 405512 | tf_op jit(solution)/shard_map/ppermute | solution.py:251
  51.9 3.6 %collective-permute-done.3 = f32[264,128]{1,0:T(8,128)S(1)} collective-permute-done((f32[264,128]{1,0:T(8,128)S(1)}, f32[264,128]{1,0:T(8,128)S(1)}, u32[]{:S(2)}, u32[]{:S(2)}) %collective-permute-start.3) | collective-permute-done | bytes 135200 | tf_op jit(solution)/shard_map/ppermute | solution.py:251
  55.6 0.1 collective-permute-start.4
  55.7 1.3 %collective-permute-done.4.other = f32[256,128]{1,0:T(8,128)S(1)} collective-permute-done((f32[256,128]{1,0:T(8,128)S(1)}, f32[256,128]{1,0:T(8,128)S(1)}, u32[]{:S(2)}, u32[]{:S(2)}) %collective-permute-start.4) | collective-permute-done | bytes 131104 | tf_op jit(solution)/shard_map/ppermute | solution.py:244
  57.0 1.3 %finish.1 = bf16[16,64,640]{2,1,0:T(8,128)(2,1)S(1)} custom-call(f32[40,256]{1,0:T(8,128)S(1)} %copy-done, bf16[16,64,896]{2,1,0:T(8,128)(2,1)S(1)} %all_to_all.10.x, f32[256,128]{1,0:T(8,128)S(1)} %get-tuple-element.59.own, f32[256,128]{1,0:T(8,128)S(1)} %collective-permute-done.4.other, f32[8,128,128]{2,1,0:T(8,128)S(1)} %get-tuple-element.48.query_i, ...), custom_call_target="tpu_custom_call" | custom-call | tf_op jit(solution)/shard_map/finish/pallas_call | solution.py:440
  58.3 23.7 %all_to_all.11.x = bf16[16,64,640]{2,1,0:T(8,128)(2,1)S(1)} all-to-all(bf16[16,64,640]{2,1,0:T(8,128)(2,1)S(1)} %finish.1), channel_id=1, replica_groups=mesh['ctx'=16,'head'=16] {'head'}, dimensions={0} | all-to-all | bytes 2621440 | tf_op jit(solution)/shard_map/all_to_all | solution.py:462
  82.0 1.1 %unpack.1 = (bf16[64,2048]{1,0:T(8,128)(2,1)}, bf16[64,2048]{1,0:T(8,128)(2,1)}, bf16[64,4096]{1,0:T(8,128)(2,1)}, bf16[64,2048]{1,0:T(8,128)(2,1)}) custom-call(bf16[16,64,640]{2,1,0:T(8,128)(2,1)S(1)} %all_to_all.11.x), custom_call_target="tpu_custom_call" | custom-call | tf_op jit(solution)/shard_map/unpack/pallas_call | solution.py:142
  (15 shorter events, 0.2 us)
Async XLA Ops:
  3.8 32.4 %copy-start = (f32[40,256]{1,0:T(8,128)S(1)}, f32[40,256]{1,0:T(8,128)}, u32[]{:S(2)}) copy-start(f32[40,256]{1,0:T(8,128)} %get-tuple-element.31.flag) | copy-start | bytes 122884
  37.0 1.4 %collective-permute-start = (f32[264,128]{1,0:T(8,128)S(1)}, f32[264,128]{1,0:T(8,128)S(1)}, u32[]{:S(2)}, u32[]{:S(2)}) collective-permute-start(f32[264,128]{1,0:T(8,128)S(1)} %get-tuple-element.34), channel_id=1, source_target_pairs={{0,16},{16,0},{32,48},{48,32},{64,80},{80,64},{96,112},{112,96},{1... | collective-permute-start | bytes 405512 | tf_op jit(solution)/shard_map/ppermute | solution.py:244
  38.5 10.9 %collective-permute-start.2 = (f32[264,128]{1,0:T(8,128)S(1)}, f32[264,128]{1,0:T(8,128)S(1)}, u32[]{:S(2)}, u32[]{:S(2)}) collective-permute-start(f32[264,128]{1,0:T(8,128)S(1)} %pad_maximum_fusion), channel_id=1, source_target_pairs={{0,64},{16,0},{32,96},{48,32},{64,128},{80,16},{96,160},{112,48},{... | collective-permute-start | bytes 405512 | tf_op jit(solution)/shard_map/ppermute | solution.py:251
  41.9 7.5 %collective-permute-start.1 = (f32[264,128]{1,0:T(8,128)S(1)}, f32[264,128]{1,0:T(8,128)S(1)}, u32[]{:S(2)}, u32[]{:S(2)}) collective-permute-start(f32[264,128]{1,0:T(8,128)S(1)} %pad_maximum_fusion), channel_id=1, source_target_pairs={{0,32},{16,0},{32,64},{48,16},{64,96},{80,48},{96,128},{112,80},{1... | collective-permute-start | bytes 405512 | tf_op jit(solution)/shard_map/ppermute | solution.py:251
  49.5 6.0 %collective-permute-start.3 = (f32[264,128]{1,0:T(8,128)S(1)}, f32[264,128]{1,0:T(8,128)S(1)}, u32[]{:S(2)}, u32[]{:S(2)}) collective-permute-start(f32[264,128]{1,0:T(8,128)S(1)} %pad_maximum_fusion.1), channel_id=1, source_target_pairs={{0,64},{16,0},{32,96},{48,32},{64,128},{80,16},{96,160},{112,48},{... | collective-permute-start | bytes 405512 | tf_op jit(solution)/shard_map/ppermute | solution.py:251
  55.6 1.4 %collective-permute-start.4 = (f32[256,128]{1,0:T(8,128)S(1)}, f32[256,128]{1,0:T(8,128)S(1)}, u32[]{:S(2)}, u32[]{:S(2)}) collective-permute-start(f32[256,128]{1,0:T(8,128)S(1)} %get-tuple-element.58), channel_id=1, source_target_pairs={{0,16},{16,0},{32,48},{48,32},{64,80},{80,64},{96,112},{112,96},{1... | collective-permute-start | bytes 393224 | tf_op jit(solution)/shard_map/ppermute | solution.py:244

commit v9 on v8

--- a/solution.py
+++ b/solution.py
@@ -256,9 +256,10 @@
 def window(kept, sent, flag, beside):
     other = swapped(sent)
     chip = joined(other, kept)
-    near, far = upstream(chip, flag, 1), upstream(chip, flag, 2)
+    far = upstream(chip, flag, 2)
+    near = upstream(chip, flag, 1)
     done = beside(chip)
-    near, far, done = lax.optimization_barrier((near, far, done))
+    far, near, done = lax.optimization_barrier((far, near, done))
     e = joined(near, far)
     e = joined(e, upstream(e, flag, 2))
     own = jnp.where(kept[DV + 2 : DV + 3] == e[DV + 1 : DV + 2], e[:DV], 0.0)

time: 84.5 us -> 84.1 us (level)
  no operation moved by 1% of the time
where the time goes in v9:
time: 84.1 us; the launch traced here: 82.8 us
  blocking collectives  56.1 us (67%)
  Pallas kernels  10.1 us (12%)
  starting transfers between devices  8.26 us (10%)
  waiting for transfers between devices  6.62 us (8%)
  between operations  1.42 us (2%)
    all_to_all x1, blocking collectives, per_device(): x = lax.all_to_all(packed, 'head', split_axis=0, concat_axis=0, tiled=True)  32.4 us
    all_to_all x1, blocking collectives, per_device(): lax.all_to_all(y, 'head', split_axis=0, concat_axis=0, tiled=True)  23.7 us
    ppermute x3, starting transfers between devices, upstream(): moved = lax.ppermute(x, 'ctx', pairs)  8.08 us
    pallas_call x1, Pallas kernels, local(): pl.pallas_call(local_kernel, out_shape=(t, t, t, f(PAIR, DV), t, t, jax.S...  4.37 us
    ppermute x3, waiting for transfers between devices, upstream(): moved = lax.ppermute(x, 'ctx', pairs)  3.97 us
    ppermute x2, waiting for transfers between devices, swapped(): return lax.ppermute(x, 'ctx', [(i, i ^ 1) for i in range(n)])  2.65 us
    pallas_call x1, Pallas kernels, pack(): pl.pallas_call(functools.partial(pack_kernel, lax.axis_size('ctx')), out_...  2.53 us
  transfers between devices with their start and end apart: 5, of which 3 were waited for; matrix products, arithmetic and copies ran while one was open for 0% of the time, Pallas kernels for 5%

profile of v9, /device:TPU:32, one launch (start us, length us, event | category | flops | bytes accessed | tf_op | source)
XLA Modules:
  0.0 82.8 jit_solution(5686004554246225750)
XLA Ops:
  1.3 2.5 %pack.1 = (bf16[16,64,896]{2,1,0:T(8,128)(2,1)}, f32[40,256]{1,0:T(8,128)}) custom-call(s32[1]{0:T(128)S(6)} %copy.11.live_h, s32[16]{0:T(128)} %doc_h.1, bf16[64,2048]{1,0:T(8,128)(2,1)} %q.1, bf16[64,2048]{1,0:T(8,128)(2,1)} %k.1, bf16[64,2048]{1,0:T(8,128)(2,1)} %g.1, bf16[64,4096]{1,0:T(8,128)(2,1)} %v.1, bf16[64,4096]{1,0:T(8,128)(2,1)} %u.1), custom_call_target="tpu_custom_call" | custom-call | tf_op jit(solution)/shard_map/pack/pallas_call | solution.py:108
  3.8 0.0 copy-start
  3.8 32.4 %all_to_all.10.x = bf16[16,64,896]{2,1,0:T(8,128)(2,1)S(1)} all-to-all(bf16[16,64,896]{2,1,0:T(8,128)(2,1)} %get-tuple-element.32), channel_id=1, replica_groups=mesh['ctx'=16,'head'=16] {'head'}, dimensions={0} | all-to-all | bytes 3670016 | tf_op jit(solution)/shard_map/all_to_all | solution.py:454
  36.2 0.0 copy-done
  36.2 0.8 totals.1
  37.0 0.1 collective-permute-start
  37.2 1.3 %collective-permute-done = f32[264,128]{1,0:T(8,128)S(1)} collective-permute-done((f32[264,128]{1,0:T(8,128)S(1)}, f32[264,128]{1,0:T(8,128)S(1)}, u32[]{:S(2)}, u32[]{:S(2)}) %collective-permute-start) | collective-permute-done | bytes 135200 | tf_op jit(solution)/shard_map/ppermute | solution.py:244
  38.5 1.9 %collective-permute-start.2 = (f32[264,128]{1,0:T(8,128)S(1)}, f32[264,128]{1,0:T(8,128)S(1)}, u32[]{:S(2)}, u32[]{:S(2)}) collective-permute-start(f32[264,128]{1,0:T(8,128)S(1)} %pad_maximum_fusion), channel_id=1, source_target_pairs={{0,32},{16,0},{32,64},{48,16},{64,96},{80,48},{96,128},{112,80},{1... | collective-permute-start | bytes 405512 | tf_op jit(solution)/shard_map/ppermute | solution.py:251
  40.5 4.5 %collective-permute-start.1 = (f32[264,128]{1,0:T(8,128)S(1)}, f32[264,128]{1,0:T(8,128)S(1)}, u32[]{:S(2)}, u32[]{:S(2)}) collective-permute-start(f32[264,128]{1,0:T(8,128)S(1)} %pad_maximum_fusion), channel_id=1, source_target_pairs={{0,64},{16,0},{32,96},{48,32},{64,128},{80,16},{96,160},{112,48},{... | collective-permute-start | bytes 405512 | tf_op jit(solution)/shard_map/ppermute | solution.py:251
  44.9 4.4 %local.1 = (f32[8,128,128]{2,1,0:T(8,128)S(1)}, f32[8,128,128]{2,1,0:T(8,128)S(1)}, f32[8,128,128]{2,1,0:T(8,128)S(1)}, f32[8,128,256]{2,1,0:T(8,128)S(1)}, f32[...) custom-call(f32[40,256]{1,0:T(8,128)S(1)} %copy-done, ...), custom_call_target="tpu_custom_call" | custom-call | flops 4000000000 | bytes 9000000 | tf_op jit(solution)/shard_map/local/pallas_call | solution.py:372
  49.3 0.0 collective-permute-done.2
  49.3 0.0 collective-permute-done.1
  49.5 1.7 %collective-permute-start.3 = (f32[264,128]{1,0:T(8,128)S(1)}, f32[264,128]{1,0:T(8,128)S(1)}, u32[]{:S(2)}, u32[]{:S(2)}) collective-permute-start(f32[264,128]{1,0:T(8,128)S(1)} %pad_maximum_fusion.1), channel_id=1, source_target_pairs={{0,64},{16,0},{32,96},{48,32},{64,128},{80,16},{96,160},{112,48},{... | collective-permute-start | bytes 405512 | tf_op jit(solution)/shard_map/ppermute | solution.py:251
  51.1 4.0 %collective-permute-done.3 = f32[264,128]{1,0:T(8,128)S(1)} collective-permute-done((f32[264,128]{1,0:T(8,128)S(1)}, f32[264,128]{1,0:T(8,128)S(1)}, u32[]{:S(2)}, u32[]{:S(2)}) %collective-permute-start.3) | collective-permute-done | bytes 135200 | tf_op jit(solution)/shard_map/ppermute | solution.py:251
  55.2 0.1 collective-permute-start.4
  55.3 1.3 %collective-permute-done.4.other = f32[256,128]{1,0:T(8,128)S(1)} collective-permute-done((f32[256,128]{1,0:T(8,128)S(1)}, f32[256,128]{1,0:T(8,128)S(1)}, u32[]{:S(2)}, u32[]{:S(2)}) %collective-permute-start.4) | collective-permute-done | bytes 131104 | tf_op jit(solution)/shard_map/ppermute | solution.py:244
  56.6 1.3 %finish.1 = bf16[16,64,640]{2,1,0:T(8,128)(2,1)S(1)} custom-call(f32[40,256]{1,0:T(8,128)S(1)} %copy-done, bf16[16,64,896]{2,1,0:T(8,128)(2,1)S(1)} %all_to_all.10.x, f32[256,128]{1,0:T(8,128)S(1)} %get-tuple-element.59.own, f32[256,128]{1,0:T(8,128)S(1)} %collective-permute-done.4.other, f32[8,128,128]{2,1,0:T(8,128)S(1)} %get-tuple-element.48.query_i, ...), custom_call_target="tpu_custom_call" | custom-call | tf_op jit(solution)/shard_map/finish/pallas_call | solution.py:441
  58.0 23.7 %all_to_all.11.x = bf16[16,64,640]{2,1,0:T(8,128)(2,1)S(1)} all-to-all(bf16[16,64,640]{2,1,0:T(8,128)(2,1)S(1)} %finish.1), channel_id=1, replica_groups=mesh['ctx'=16,'head'=16] {'head'}, dimensions={0} | all-to-all | bytes 2621440 | tf_op jit(solution)/shard_map/all_to_all | solution.py:463
  81.7 1.1 %unpack.1 = (bf16[64,2048]{1,0:T(8,128)(2,1)}, bf16[64,2048]{1,0:T(8,128)(2,1)}, bf16[64,4096]{1,0:T(8,128)(2,1)}, bf16[64,2048]{1,0:T(8,128)(2,1)}) custom-call(bf16[16,64,640]{2,1,0:T(8,128)(2,1)S(1)} %all_to_all.11.x), custom_call_target="tpu_custom_call" | custom-call | tf_op jit(solution)/shard_map/unpack/pallas_call | solution.py:142
  (15 shorter events, 0.2 us)
Async XLA Ops:
  3.8 32.4 %copy-start = (f32[40,256]{1,0:T(8,128)S(1)}, f32[40,256]{1,0:T(8,128)}, u32[]{:S(2)}) copy-start(f32[40,256]{1,0:T(8,128)} %get-tuple-element.31.flag) | copy-start | bytes 122884
  37.0 1.4 %collective-permute-start = (f32[264,128]{1,0:T(8,128)S(1)}, f32[264,128]{1,0:T(8,128)S(1)}, u32[]{:S(2)}, u32[]{:S(2)}) collective-permute-start(f32[264,128]{1,0:T(8,128)S(1)} %get-tuple-element.34), channel_id=1, source_target_pairs={{0,16},{16,0},{32,48},{48,32},{64,80},{80,64},{96,112},{112,96},{1... | collective-permute-start | bytes 405512 | tf_op jit(solution)/shard_map/ppermute | solution.py:244
  38.5 10.8 %collective-permute-start.2 = (f32[264,128]{1,0:T(8,128)S(1)}, f32[264,128]{1,0:T(8,128)S(1)}, u32[]{:S(2)}, u32[]{:S(2)}) collective-permute-start(f32[264,128]{1,0:T(8,128)S(1)} %pad_maximum_fusion), channel_id=1, source_target_pairs={{0,32},{16,0},{32,64},{48,16},{64,96},{80,48},{96,128},{112,80},{1... | collective-permute-start | bytes 405512 | tf_op jit(solution)/shard_map/ppermute | solution.py:251
  40.5 8.9 %collective-permute-start.1 = (f32[264,128]{1,0:T(8,128)S(1)}, f32[264,128]{1,0:T(8,128)S(1)}, u32[]{:S(2)}, u32[]{:S(2)}) collective-permute-start(f32[264,128]{1,0:T(8,128)S(1)} %pad_maximum_fusion), channel_id=1, source_target_pairs={{0,64},{16,0},{32,96},{48,32},{64,128},{80,16},{96,160},{112,48},{... | collective-permute-start | bytes 405512 | tf_op jit(solution)/shard_map/ppermute | solution.py:251
  49.5 5.6 %collective-permute-start.3 = (f32[264,128]{1,0:T(8,128)S(1)}, f32[264,128]{1,0:T(8,128)S(1)}, u32[]{:S(2)}, u32[]{:S(2)}) collective-permute-start(f32[264,128]{1,0:T(8,128)S(1)} %pad_maximum_fusion.1), channel_id=1, source_target_pairs={{0,64},{16,0},{32,96},{48,32},{64,128},{80,16},{96,160},{112,48},{... | collective-permute-start | bytes 405512 | tf_op jit(solution)/shard_map/ppermute | solution.py:251
  55.2 1.4 %collective-permute-start.4 = (f32[256,128]{1,0:T(8,128)S(1)}, f32[256,128]{1,0:T(8,128)S(1)}, u32[]{:S(2)}, u32[]{:S(2)}) collective-permute-start(f32[256,128]{1,0:T(8,128)S(1)} %get-tuple-element.58), channel_id=1, source_target_pairs={{0,16},{16,0},{32,48},{48,32},{64,80},{80,64},{96,112},{112,96},{1... | collective-permute-start | bytes 393224 | tf_op jit(solution)/shard_map/ppermute | solution.py:244

commit v10 on v9

--- a/solution.py
+++ b/solution.py
@@ -174,58 +174,65 @@
     return i, j, first, first == (j < BLOCK)
 
 
-def totals_kernel(flag, x, kept, sent, kw, qw, cs):
-    lives, keeps, even = flags(flag)
+def totals_kernel(kept, flag, x, out, w):
+    lives, keeps, _ = flags(flag)
     i, j, first, same = pair_masks()
     tri = one((j <= i) & same).astype(BF)
-    decay = jnp.ones((1, DK), F32)
-    for p in range(NP):
-        a, b = 2 * p, 2 * p + 1
-        c = dot(tri, rows_of(x, p, GC, DK), 1, 0) * jnp.where(first, lives[a], lives[b])
-        cs[p] = c
-        earlier = decay * keeps[a]
-        middle = earlier * (keeps[b] * jnp.exp(c[BLOCK - 1 : BLOCK]))
-        decay = middle * jnp.exp(c[PAIR - 1 : PAIR])
-        q = rows_of(x, p, QC, DK).astype(F32)
-        scale = jnp.where(first, earlier * (lives[a] * SCALE), middle * (lives[b] * SCALE))
-        qw[p] = two(q * (jnp.exp(c) * scale))
     rows = NB * BLOCK
-    u = x[:, :, UC : UC + DV].reshape(rows, DV)
-    bwd = halves(dot(u, qw[...].reshape(rows, 2 * DK), 0, 0))
-    later = jnp.ones((1, DK), F32)
-    for p in reversed(range(NP)):
-        a, b = 2 * p, 2 * p + 1
-        c = cs[p]
-        ca, cb = c[BLOCK - 1 : BLOCK], c[PAIR - 1 : PAIR]
-        middle = later * (keeps[b] * jnp.exp(cb))
-        k = rows_of(x, p, KC, DK).astype(F32)
-        fade = jnp.exp(jnp.where(first, ca, cb) - c)
-        kw[p] = two(k * (fade * jnp.where(first, middle * lives[a], later * lives[b])))
-        later = middle * (keeps[a] * jnp.exp(ca))
-    v = x[:, :, VC : VC + DV].reshape(rows, DV)
-    fwd = halves(dot(v, kw[...].reshape(rows, 2 * DK), 0, 0))
-    kept[:DV] = jnp.where(even, fwd, bwd)
-    sent[:DV] = jnp.where(even, bwd, fwd)
-    head, tail = flag[HEAD_ID : HEAD_ID + 1, :DK], flag[TAIL_ID : TAIL_ID + 1, :DK]
-    rest = jnp.zeros((MSG - DV - 3, DK), F32)
-    kept[DV:] = jnp.concatenate([decay, head, tail, rest])
-    sent[DV:] = jnp.concatenate([decay, tail, head, rest])
-
-
-def totals(flag, x):
-    msg = jax.ShapeDtypeStruct((MSG, DK), F32)
+
+    def cumul(p):
+        c = dot(tri, rows_of(x, p, GC, DK), 1, 0)
+        return c * jnp.where(first, lives[2 * p], lives[2 * p + 1])
+
+    def ends(decay):
+        head, tail = flag[HEAD_ID : HEAD_ID + 1, :DK], flag[TAIL_ID : TAIL_ID + 1, :DK]
+        head, tail = (head, tail) if kept else (tail, head)
+        return jnp.concatenate([decay, head, tail, jnp.zeros((MSG - DV - 3, DK), F32)])
+
+    def forward():
+        later = jnp.ones((1, DK), F32)
+        for p in reversed(range(NP)):
+            a, b = 2 * p, 2 * p + 1
+            c = cumul(p)
+            ca, cb = c[BLOCK - 1 : BLOCK], c[PAIR - 1 : PAIR]
+            middle = later * (keeps[b] * jnp.exp(cb))
+            k = rows_of(x, p, KC, DK).astype(F32)
+            fade = jnp.exp(jnp.where(first, ca, cb) - c)
+            w[p] = two(k * (fade * jnp.where(first, middle * lives[a], later * lives[b])))
+            later = middle * (keeps[a] * jnp.exp(ca))
+        v = x[:, :, VC : VC + DV].reshape(rows, DV)
+        out[:DV] = halves(dot(v, w[...].reshape(rows, 2 * DK), 0, 0))
+        out[DV:] = ends(later)
+
+    def backward():
+        decay = jnp.ones((1, DK), F32)
+        for p in range(NP):
+            a, b = 2 * p, 2 * p + 1
+            c = cumul(p)
+            earlier = decay * keeps[a]
+            middle = earlier * (keeps[b] * jnp.exp(c[BLOCK - 1 : BLOCK]))
+            decay = middle * jnp.exp(c[PAIR - 1 : PAIR])
+            q = rows_of(x, p, QC, DK).astype(F32)
+            scale = jnp.where(first, earlier * (lives[a] * SCALE), middle * (lives[b] * SCALE))
+            w[p] = two(q * (jnp.exp(c) * scale))
+        u = x[:, :, UC : UC + DV].reshape(rows, DV)
+        out[:DV] = halves(dot(u, w[...].reshape(rows, 2 * DK), 0, 0))
+        out[DV:] = ends(decay)
+
+    even = lax.rem(lax.axis_index("ctx"), 2) == 0
+    pl.when(even)(forward if kept else backward)
+    pl.when(jnp.logical_not(even))(backward if kept else forward)
+
+
+def totals(kept, flag, x):
     return pl.pallas_call(
-        totals_kernel,
-        out_shape=(msg, msg),
+        functools.partial(totals_kernel, kept),
+        out_shape=jax.ShapeDtypeStruct((MSG, DK), F32),
         in_specs=[vspec()] * 2,
-        out_specs=(vspec(),) * 2,
-        scratch_shapes=[
-            VMEM((NP, PAIR, 2 * DK), BF),
-            VMEM((NP, PAIR, 2 * DK), BF),
-            VMEM((NP, PAIR, DK), F32),
-        ],
+        out_specs=vspec(),
+        scratch_shapes=[VMEM((NP, PAIR, 2 * DK), BF)],
         compiler_params=pltpu.CompilerParams(vmem_limit_bytes=32 * 1024 * 1024),
-        name="totals",
+        name="kept" if kept else "sent",
     )(flag, x)
 
 
@@ -253,8 +260,8 @@
     return jnp.where(flag[row : row + 1, :DK] > 0.0, moved, 0.0)
 
 
-def window(kept, sent, flag, beside):
-    other = swapped(sent)
+def window(sent, keep, flag, beside):
+    other, kept = lax.optimization_barrier((swapped(sent), keep(sent)))
     chip = joined(other, kept)
     far = upstream(chip, flag, 2)
     near = upstream(chip, flag, 1)
@@ -452,13 +459,17 @@
 def per_device(queries, keys, values, out_grad, log_gates, live_blocks, block_doc):
     packed, flag = pack(live_blocks, block_doc, queries, keys, log_gates, values, out_grad)
     x = lax.all_to_all(packed, "head", split_axis=0, concat_axis=0, tiled=True)
-    kept, sent = totals(flag, x)
+    sent = totals(False, flag, x)
+
+    def keep(sent):
+        y, _ = lax.optimization_barrier((x, sent))
+        return totals(True, flag, y)
 
     def beside(chip):
         y, _ = lax.optimization_barrier((x, chip))
         return local(flag, y)
 
-    own, other, parts = window(kept, sent, flag, beside)
+    own, other, parts = window(sent, keep, flag, beside)
     y = finish(flag, x, own, other, parts)
     return unpack(lax.all_to_all(y, "head", split_axis=0, concat_axis=0, tiled=True))
 

time: 84.1 us -> 84 us (level)
  transfers between devices with their start and end apart: 5 -> 5, of which waited for: 3 -> 3; matrix products, arithmetic and copies ran while one was open for 0% -> 0% of each run, Pallas kernels for 5% -> 6%
where the time goes in v10:
time: 84 us; the launch traced here: 82.7 us
  blocking collectives  56.1 us (67%)
  Pallas kernels  10.7 us (13%)
  starting transfers between devices  8.27 us (10%)
  waiting for transfers between devices  5.99 us (7%)
  between operations  1.43 us (2%)
    all_to_all x1, blocking collectives, per_device(): x = lax.all_to_all(packed, 'head', split_axis=0, concat_axis=0, tiled=True)  32.4 us
    all_to_all x1, blocking collectives, per_device(): lax.all_to_all(y, 'head', split_axis=0, concat_axis=0, tiled=True)  23.7 us
    ppermute x3, starting transfers between devices, upstream(): moved = lax.ppermute(x, 'ctx', pairs)  8.08 us
    pallas_call x1, Pallas kernels, local(): pl.pallas_call(local_kernel, out_shape=(t, t, t, f(PAIR, DV), t, t, jax.S...  4.37 us
    ppermute x3, waiting for transfers between devices, upstream(): moved = lax.ppermute(x, 'ctx', pairs)  3.97 us
    pallas_call x1, Pallas kernels, pack(): pl.pallas_call(functools.partial(pack_kernel, lax.axis_size('ctx')), out_...  2.57 us
    ppermute x2, waiting for transfers between devices, swapped(): return lax.ppermute(x, 'ctx', [(i, i ^ 1) for i in range(n)])  2.02 us
  transfers between devices with their start and end apart: 5, of which 3 were waited for; matrix products, arithmetic and copies ran while one was open for 0% of the time, Pallas kernels for 6%

profile of v10, /device:TPU:32, one launch (start us, length us, event | category | flops | bytes accessed | tf_op | source)
XLA Modules:
  0.0 82.7 jit_solution(14413714127910909430)
XLA Ops:
  1.3 2.6 %pack.1 = (bf16[16,64,896]{2,1,0:T(8,128)(2,1)}, f32[40,256]{1,0:T(8,128)}) custom-call(s32[1]{0:T(128)S(6)} %copy.11.live_h, s32[16]{0:T(128)} %doc_h.1, bf16[64,2048]{1,0:T(8,128)(2,1)} %q.1, bf16[64,2048]{1,0:T(8,128)(2,1)} %k.1, bf16[64,2048]{1,0:T(8,128)(2,1)} %g.1, bf16[64,4096]{1,0:T(8,128)(2,1)} %v.1, bf16[64,4096]{1,0:T(8,128)(2,1)} %u.1), custom_call_target="tpu_custom_call" | custom-call | tf_op jit(solution)/shard_map/pack/pallas_call | solution.py:108
  3.9 0.0 copy-start
  3.9 32.4 %all_to_all.10.x = bf16[16,64,896]{2,1,0:T(8,128)(2,1)S(1)} all-to-all(bf16[16,64,896]{2,1,0:T(8,128)(2,1)} %get-tuple-element.33), channel_id=1, replica_groups=mesh['ctx'=16,'head'=16] {'head'}, dimensions={0} | all-to-all | bytes 3670016 | tf_op jit(solution)/shard_map/all_to_all | solution.py:461
  36.3 0.0 copy-done
  36.3 0.6 sent.1
  36.9 0.1 collective-permute-start
  37.0 0.6 kept.1
  37.7 0.7 collective-permute-done
  38.4 1.9 %collective-permute-start.2 = (f32[264,128]{1,0:T(8,128)S(1)}, f32[264,128]{1,0:T(8,128)S(1)}, u32[]{:S(2)}, u32[]{:S(2)}) collective-permute-start(f32[264,128]{1,0:T(8,128)S(1)} %pad_maximum_fusion), channel_id=1, source_target_pairs={{0,32},{16,0},{32,64},{48,16},{64,96},{80,48},{96,128},{112,80},{1... | collective-permute-start | bytes 405512 | tf_op jit(solution)/shard_map/ppermute | solution.py:258
  40.4 4.5 %collective-permute-start.1 = (f32[264,128]{1,0:T(8,128)S(1)}, f32[264,128]{1,0:T(8,128)S(1)}, u32[]{:S(2)}, u32[]{:S(2)}) collective-permute-start(f32[264,128]{1,0:T(8,128)S(1)} %pad_maximum_fusion), channel_id=1, source_target_pairs={{0,64},{16,0},{32,96},{48,32},{64,128},{80,16},{96,160},{112,48},{... | collective-permute-start | bytes 405512 | tf_op jit(solution)/shard_map/ppermute | solution.py:258
  44.8 4.4 %local.1 = (f32[8,128,128]{2,1,0:T(8,128)S(1)}, f32[8,128,128]{2,1,0:T(8,128)S(1)}, f32[8,128,128]{2,1,0:T(8,128)S(1)}, f32[8,128,256]{2,1,0:T(8,128)S(1)}, f32[...) custom-call(f32[40,256]{1,0:T(8,128)S(1)} %copy-done, ...), custom_call_target="tpu_custom_call" | custom-call | flops 4000000000 | bytes 9000000 | tf_op jit(solution)/shard_map/local/pallas_call | solution.py:379
  49.2 0.0 collective-permute-done.2
  49.2 0.0 collective-permute-done.1
  49.4 1.7 %collective-permute-start.3 = (f32[264,128]{1,0:T(8,128)S(1)}, f32[264,128]{1,0:T(8,128)S(1)}, u32[]{:S(2)}, u32[]{:S(2)}) collective-permute-start(f32[264,128]{1,0:T(8,128)S(1)} %pad_maximum_fusion.1), channel_id=1, source_target_pairs={{0,64},{16,0},{32,96},{48,32},{64,128},{80,16},{96,160},{112,48},{... | collective-permute-start | bytes 405512 | tf_op jit(solution)/shard_map/ppermute | solution.py:258
  51.0 4.0 %collective-permute-done.3 = f32[264,128]{1,0:T(8,128)S(1)} collective-permute-done((f32[264,128]{1,0:T(8,128)S(1)}, f32[264,128]{1,0:T(8,128)S(1)}, u32[]{:S(2)}, u32[]{:S(2)}) %collective-permute-start.3) | collective-permute-done | bytes 135200 | tf_op jit(solution)/shard_map/ppermute | solution.py:258
  55.1 0.1 collective-permute-start.4
  55.2 1.3 %collective-permute-done.4.other = f32[256,128]{1,0:T(8,128)S(1)} collective-permute-done((f32[256,128]{1,0:T(8,128)S(1)}, f32[256,128]{1,0:T(8,128)S(1)}, u32[]{:S(2)}, u32[]{:S(2)}) %collective-permute-start.4) | collective-permute-done | bytes 131104 | tf_op jit(solution)/shard_map/ppermute | solution.py:251
  56.5 1.4 %finish.1 = bf16[16,64,640]{2,1,0:T(8,128)(2,1)S(1)} custom-call(f32[40,256]{1,0:T(8,128)S(1)} %copy-done, bf16[16,64,896]{2,1,0:T(8,128)(2,1)S(1)} %all_to_all.10.x, f32[256,128]{1,0:T(8,128)S(1)} %get-tuple-element.61.own, f32[256,128]{1,0:T(8,128)S(1)} %collective-permute-done.4.other, f32[8,128,128]{2,1,0:T(8,128)S(1)} %get-tuple-element.50.query_i, ...), custom_call_target="tpu_custom_call" | custom-call | tf_op jit(solution)/shard_map/finish/pallas_call | solution.py:448
  57.9 23.7 %all_to_all.11.x = bf16[16,64,640]{2,1,0:T(8,128)(2,1)S(1)} all-to-all(bf16[16,64,640]{2,1,0:T(8,128)(2,1)S(1)} %finish.1), channel_id=1, replica_groups=mesh['ctx'=16,'head'=16] {'head'}, dimensions={0} | all-to-all | bytes 2621440 | tf_op jit(solution)/shard_map/all_to_all | solution.py:474
  81.6 1.1 %unpack.1 = (bf16[64,2048]{1,0:T(8,128)(2,1)}, bf16[64,2048]{1,0:T(8,128)(2,1)}, bf16[64,4096]{1,0:T(8,128)(2,1)}, bf16[64,2048]{1,0:T(8,128)(2,1)}) custom-call(bf16[16,64,640]{2,1,0:T(8,128)(2,1)S(1)} %all_to_all.11.x), custom_call_target="tpu_custom_call" | custom-call | tf_op jit(solution)/shard_map/unpack/pallas_call | solution.py:142
  (15 shorter events, 0.2 us)
Async XLA Ops:
  3.9 32.4 %copy-start = (f32[40,256]{1,0:T(8,128)S(1)}, f32[40,256]{1,0:T(8,128)}, u32[]{:S(2)}) copy-start(f32[40,256]{1,0:T(8,128)} %get-tuple-element.32.flag) | copy-start | bytes 122884
  36.9 1.4 %collective-permute-start = (f32[264,128]{1,0:T(8,128)S(1)}, f32[264,128]{1,0:T(8,128)S(1)}, u32[]{:S(2)}, u32[]{:S(2)}) collective-permute-start(f32[264,128]{1,0:T(8,128)S(1)} %sent.1), channel_id=1, source_target_pairs={{0,16},{16,0},{32,48},{48,32},{64,80},{80,64},{96,112},{112,96},{1... | collective-permute-start | bytes 405512 | tf_op jit(solution)/shard_map/ppermute | solution.py:251
  38.4 10.8 %collective-permute-start.2 = (f32[264,128]{1,0:T(8,128)S(1)}, f32[264,128]{1,0:T(8,128)S(1)}, u32[]{:S(2)}, u32[]{:S(2)}) collective-permute-start(f32[264,128]{1,0:T(8,128)S(1)} %pad_maximum_fusion), channel_id=1, source_target_pairs={{0,32},{16,0},{32,64},{48,16},{64,96},{80,48},{96,128},{112,80},{1... | collective-permute-start | bytes 405512 | tf_op jit(solution)/shard_map/ppermute | solution.py:258
  40.4 8.9 %collective-permute-start.1 = (f32[264,128]{1,0:T(8,128)S(1)}, f32[264,128]{1,0:T(8,128)S(1)}, u32[]{:S(2)}, u32[]{:S(2)}) collective-permute-start(f32[264,128]{1,0:T(8,128)S(1)} %pad_maximum_fusion), channel_id=1, source_target_pairs={{0,64},{16,0},{32,96},{48,32},{64,128},{80,16},{96,160},{112,48},{... | collective-permute-start | bytes 405512 | tf_op jit(solution)/shard_map/ppermute | solution.py:258
  49.4 5.6 %collective-permute-start.3 = (f32[264,128]{1,0:T(8,128)S(1)}, f32[264,128]{1,0:T(8,128)S(1)}, u32[]{:S(2)}, u32[]{:S(2)}) collective-permute-start(f32[264,128]{1,0:T(8,128)S(1)} %pad_maximum_fusion.1), channel_id=1, source_target_pairs={{0,64},{16,0},{32,96},{48,32},{64,128},{80,16},{96,160},{112,48},{... | collective-permute-start | bytes 405512 | tf_op jit(solution)/shard_map/ppermute | solution.py:258
  55.1 1.4 %collective-permute-start.4 = (f32[256,128]{1,0:T(8,128)S(1)}, f32[256,128]{1,0:T(8,128)S(1)}, u32[]{:S(2)}, u32[]{:S(2)}) collective-permute-start(f32[256,128]{1,0:T(8,128)S(1)} %get-tuple-element.60), channel_id=1, source_target_pairs={{0,16},{16,0},{32,48},{48,32},{64,80},{80,64},{96,112},{112,96},{1... | collective-permute-start | bytes 393224 | tf_op jit(solution)/shard_map/ppermute | solution.py:251

commit v11 on v8

--- a/solution.py
+++ b/solution.py
@@ -256,11 +256,10 @@
 def window(kept, sent, flag, beside):
     other = swapped(sent)
     chip = joined(other, kept)
-    near, far = upstream(chip, flag, 1), upstream(chip, flag, 2)
-    done = beside(chip)
-    near, far, done = lax.optimization_barrier((near, far, done))
-    e = joined(near, far)
-    e = joined(e, upstream(e, flag, 2))
+    e = joined(upstream(chip, flag, 1), upstream(chip, flag, 2))
+    farther = upstream(e, flag, 2)
+    farther, done = lax.optimization_barrier((farther, beside(e)))
+    e = joined(e, farther)
     own = jnp.where(kept[DV + 2 : DV + 3] == e[DV + 1 : DV + 2], e[:DV], 0.0)
     onward = kept[DV : DV + 1] * own + kept[:DV]
     onward = jnp.where(other[DV + 2 : DV + 3] == kept[DV + 1 : DV + 2], onward, 0.0)

time: 84.5 us -> 85.2 us (level)
  starting transfers between devices: 9.03 us -> 10.9 us
  waiting for transfers between devices: 6.24 us -> 5.2 us
    ppermute x3, starting transfers between devices: 8.85 us -> 10.7 us  [upstream(): moved = lax.ppermute(x, 'ctx', pairs)]
    ppermute x3, waiting for transfers between devices: 3.59 us -> 2.54 us  [upstream(): moved = lax.ppermute(x, 'ctx', pairs)]
  transfers between devices with their start and end apart: 5 -> 5, of which waited for: 3 -> 4; matrix products, arithmetic and copies ran while one was open for 0% -> 0% of each run, Pallas kernels for 5% -> 5%
where the time goes in v11:
time: 85.2 us; the launch traced here: 84 us
  blocking collectives  56.1 us (66%)
  starting transfers between devices  10.9 us (13%)
  Pallas kernels  10.1 us (12%)
  waiting for transfers between devices  5.2 us (6%)
  between operations  1.42 us (2%)
    all_to_all x1, blocking collectives, per_device(): x = lax.all_to_all(packed, 'head', split_axis=0, concat_axis=0, tiled=True)  32.4 us
    all_to_all x1, blocking collectives, per_device(): lax.all_to_all(y, 'head', split_axis=0, concat_axis=0, tiled=True)  23.7 us
    ppermute x3, starting transfers between devices, upstream(): moved = lax.ppermute(x, 'ctx', pairs)  10.7 us
    pallas_call x1, Pallas kernels, local(): pl.pallas_call(local_kernel, out_shape=(t, t, t, f(PAIR, DV), t, t, jax.S...  4.37 us
    ppermute x2, waiting for transfers between devices, swapped(): return lax.ppermute(x, 'ctx', [(i, i ^ 1) for i in range(n)])  2.66 us
    ppermute x3, waiting for transfers between devices, upstream(): moved = lax.ppermute(x, 'ctx', pairs)  2.54 us
    pallas_call x1, Pallas kernels, pack(): pl.pallas_call(functools.partial(pack_kernel, lax.axis_size('ctx')), out_...  2.53 us
  transfers between devices with their start and end apart: 5, of which 4 were waited for; matrix products, arithmetic and copies ran while one was open for 0% of the time, Pallas kernels for 5%

profile of v11, /device:TPU:32, one launch (start us, length us, event | category | flops | bytes accessed | tf_op | source)
XLA Modules:
  0.0 84.0 jit_solution(12746983049743504807)
XLA Ops:
  1.3 2.5 %pack.1 = (bf16[16,64,896]{2,1,0:T(8,128)(2,1)}, f32[40,256]{1,0:T(8,128)}) custom-call(s32[1]{0:T(128)S(6)} %copy.11.live_h, s32[16]{0:T(128)} %doc_h.1, bf16[64,2048]{1,0:T(8,128)(2,1)} %q.1, bf16[64,2048]{1,0:T(8,128)(2,1)} %k.1, bf16[64,2048]{1,0:T(8,128)(2,1)} %g.1, bf16[64,4096]{1,0:T(8,128)(2,1)} %v.1, bf16[64,4096]{1,0:T(8,128)(2,1)} %u.1), custom_call_target="tpu_custom_call" | custom-call | tf_op jit(solution)/shard_map/pack/pallas_call | solution.py:108
  3.8 0.0 copy-start
  3.8 32.4 %all_to_all.10.x = bf16[16,64,896]{2,1,0:T(8,128)(2,1)S(1)} all-to-all(bf16[16,64,896]{2,1,0:T(8,128)(2,1)} %get-tuple-element.31), channel_id=1, replica_groups=mesh['ctx'=16,'head'=16] {'head'}, dimensions={0} | all-to-all | bytes 3670016 | tf_op jit(solution)/shard_map/all_to_all | solution.py:452
  36.2 0.0 copy-done
  36.2 0.8 totals.1
  37.0 0.1 collective-permute-start
  37.1 1.3 %collective-permute-done = f32[264,128]{1,0:T(8,128)S(1)} collective-permute-done((f32[264,128]{1,0:T(8,128)S(1)}, f32[264,128]{1,0:T(8,128)S(1)}, u32[]{:S(2)}, u32[]{:S(2)}) %collective-permute-start) | collective-permute-done | bytes 135200 | tf_op jit(solution)/shard_map/ppermute | solution.py:244
  38.5 3.3 %collective-permute-start.2 = (f32[264,128]{1,0:T(8,128)S(1)}, f32[264,128]{1,0:T(8,128)S(1)}, u32[]{:S(2)}, u32[]{:S(2)}) collective-permute-start(f32[264,128]{1,0:T(8,128)S(1)} %pad_maximum_fusion), channel_id=1, source_target_pairs={{0,64},{16,0},{32,96},{48,32},{64,128},{80,16},{96,160},{112,48},{... | collective-permute-start | bytes 405512 | tf_op jit(solution)/shard_map/ppermute | solution.py:251
  41.9 3.1 %collective-permute-start.1 = (f32[264,128]{1,0:T(8,128)S(1)}, f32[264,128]{1,0:T(8,128)S(1)}, u32[]{:S(2)}, u32[]{:S(2)}) collective-permute-start(f32[264,128]{1,0:T(8,128)S(1)} %pad_maximum_fusion), channel_id=1, source_target_pairs={{0,32},{16,0},{32,64},{48,16},{64,96},{80,48},{96,128},{112,80},{1... | collective-permute-start | bytes 405512 | tf_op jit(solution)/shard_map/ppermute | solution.py:251
  45.0 0.4 collective-permute-done.2
  45.4 2.1 %collective-permute-done.1 = f32[264,128]{1,0:T(8,128)S(1)} collective-permute-done((f32[264,128]{1,0:T(8,128)S(1)}, f32[264,128]{1,0:T(8,128)S(1)}, u32[]{:S(2)}, u32[]{:S(2)}) %collective-permute-start.1) | collective-permute-done | bytes 135200 | tf_op jit(solution)/shard_map/ppermute | solution.py:251
  47.6 4.2 %collective-permute-start.3 = (f32[264,128]{1,0:T(8,128)S(1)}, f32[264,128]{1,0:T(8,128)S(1)}, u32[]{:S(2)}, u32[]{:S(2)}) collective-permute-start(f32[264,128]{1,0:T(8,128)S(1)} %pad_maximum_fusion.1), channel_id=1, source_target_pairs={{0,64},{16,0},{32,96},{48,32},{64,128},{80,16},{96,160},{112,48},{... | collective-permute-start | bytes 405512 | tf_op jit(solution)/shard_map/ppermute | solution.py:251
  51.9 4.4 %local.1 = (f32[8,128,128]{2,1,0:T(8,128)S(1)}, f32[8,128,128]{2,1,0:T(8,128)S(1)}, f32[8,128,128]{2,1,0:T(8,128)S(1)}, f32[8,128,256]{2,1,0:T(8,128)S(1)}, f32[...) custom-call(f32[40,256]{1,0:T(8,128)S(1)} %copy-done, ...), custom_call_target="tpu_custom_call" | custom-call | flops 4000000000 | bytes 9000000 | tf_op jit(solution)/shard_map/local/pallas_call | solution.py:370
  56.3 0.0 collective-permute-done.3
  56.3 0.1 collective-permute-start.4
  56.4 1.3 %collective-permute-done.4.other = f32[256,128]{1,0:T(8,128)S(1)} collective-permute-done((f32[256,128]{1,0:T(8,128)S(1)}, f32[256,128]{1,0:T(8,128)S(1)}, u32[]{:S(2)}, u32[]{:S(2)}) %collective-permute-start.4) | collective-permute-done | bytes 131104 | tf_op jit(solution)/shard_map/ppermute | solution.py:244
  57.8 1.3 %finish.1 = bf16[16,64,640]{2,1,0:T(8,128)(2,1)S(1)} custom-call(f32[40,256]{1,0:T(8,128)S(1)} %copy-done, bf16[16,64,896]{2,1,0:T(8,128)(2,1)S(1)} %all_to_all.10.x, f32[256,128]{1,0:T(8,128)S(1)} %get-tuple-element.57.own, f32[256,128]{1,0:T(8,128)S(1)} %collective-permute-done.4.other, f32[8,128,128]{2,1,0:T(8,128)S(1)} %get-tuple-element.46.query_i, ...), custom_call_target="tpu_custom_call" | custom-call | tf_op jit(solution)/shard_map/finish/pallas_call | solution.py:439
  59.1 23.7 %all_to_all.11.x = bf16[16,64,640]{2,1,0:T(8,128)(2,1)S(1)} all-to-all(bf16[16,64,640]{2,1,0:T(8,128)(2,1)S(1)} %finish.1), channel_id=1, replica_groups=mesh['ctx'=16,'head'=16] {'head'}, dimensions={0} | all-to-all | bytes 2621440 | tf_op jit(solution)/shard_map/all_to_all | solution.py:461
  82.8 1.1 %unpack.1 = (bf16[64,2048]{1,0:T(8,128)(2,1)}, bf16[64,2048]{1,0:T(8,128)(2,1)}, bf16[64,4096]{1,0:T(8,128)(2,1)}, bf16[64,2048]{1,0:T(8,128)(2,1)}) custom-call(bf16[16,64,640]{2,1,0:T(8,128)(2,1)S(1)} %all_to_all.11.x), custom_call_target="tpu_custom_call" | custom-call | tf_op jit(solution)/shard_map/unpack/pallas_call | solution.py:142
  (15 shorter events, 0.2 us)
Async XLA Ops:
  3.8 32.4 %copy-start = (f32[40,256]{1,0:T(8,128)S(1)}, f32[40,256]{1,0:T(8,128)}, u32[]{:S(2)}) copy-start(f32[40,256]{1,0:T(8,128)} %get-tuple-element.30.flag) | copy-start | bytes 122884
  37.0 1.4 %collective-permute-start = (f32[264,128]{1,0:T(8,128)S(1)}, f32[264,128]{1,0:T(8,128)S(1)}, u32[]{:S(2)}, u32[]{:S(2)}) collective-permute-start(f32[264,128]{1,0:T(8,128)S(1)} %get-tuple-element.33), channel_id=1, source_target_pairs={{0,16},{16,0},{32,48},{48,32},{64,80},{80,64},{96,112},{112,96},{1... | collective-permute-start | bytes 405512 | tf_op jit(solution)/shard_map/ppermute | solution.py:244
  38.5 6.9 %collective-permute-start.2 = (f32[264,128]{1,0:T(8,128)S(1)}, f32[264,128]{1,0:T(8,128)S(1)}, u32[]{:S(2)}, u32[]{:S(2)}) collective-permute-start(f32[264,128]{1,0:T(8,128)S(1)} %pad_maximum_fusion), channel_id=1, source_target_pairs={{0,64},{16,0},{32,96},{48,32},{64,128},{80,16},{96,160},{112,48},{... | collective-permute-start | bytes 405512 | tf_op jit(solution)/shard_map/ppermute | solution.py:251
  41.9 5.7 %collective-permute-start.1 = (f32[264,128]{1,0:T(8,128)S(1)}, f32[264,128]{1,0:T(8,128)S(1)}, u32[]{:S(2)}, u32[]{:S(2)}) collective-permute-start(f32[264,128]{1,0:T(8,128)S(1)} %pad_maximum_fusion), channel_id=1, source_target_pairs={{0,32},{16,0},{32,64},{48,16},{64,96},{80,48},{96,128},{112,80},{1... | collective-permute-start | bytes 405512 | tf_op jit(solution)/shard_map/ppermute | solution.py:251
  47.6 8.6 %collective-permute-start.3 = (f32[264,128]{1,0:T(8,128)S(1)}, f32[264,128]{1,0:T(8,128)S(1)}, u32[]{:S(2)}, u32[]{:S(2)}) collective-permute-start(f32[264,128]{1,0:T(8,128)S(1)} %pad_maximum_fusion.1), channel_id=1, source_target_pairs={{0,64},{16,0},{32,96},{48,32},{64,128},{80,16},{96,160},{112,48},{... | collective-permute-start | bytes 405512 | tf_op jit(solution)/shard_map/ppermute | solution.py:251
  56.3 1.4 %collective-permute-start.4 = (f32[256,128]{1,0:T(8,128)S(1)}, f32[256,128]{1,0:T(8,128)S(1)}, u32[]{:S(2)}, u32[]{:S(2)}) collective-permute-start(f32[256,128]{1,0:T(8,128)S(1)} %get-tuple-element.56), channel_id=1, source_target_pairs={{0,16},{16,0},{32,48},{48,32},{64,80},{80,64},{96,112},{112,96},{1... | collective-permute-start | bytes 393224 | tf_op jit(solution)/shard_map/ppermute | solution.py:244
